TPU v7x, 32 devices: a whole 2x2x4 slice. The times are simulated.
32 devices in a mesh: groups: 2 (over y), seq: 4 (over z), head: 2 (over x), rep: 2 (over core).
Axes of the slice: x: 2, y: 2, z: 4, core: 2. Of those that a mesh axis runs over, the one named last changes fastest.
Arguments:
- queries: bfloat16 [4, 512, 4096], P(('groups', 'head'), ('seq', 'rep')), parts along dimension 0, may hold values from -96 to 96
- keys: bfloat16 [4, 512, 4096], P(('groups', 'head'), ('seq', 'rep')), parts along dimension 0, may hold values from -4 to 4
- values: bfloat16 [4, 512, 4096], P(('groups', 'head'), ('seq', 'rep')), parts along dimension 0, may hold values from -6 to 6
- grad_out: bfloat16 [4, 512, 4096], P(('groups', 'head'), ('seq', 'rep')), parts along dimension 0, may hold values from -192 to 192
- gauge_key: bfloat16 [1024, 4096], P(('groups', 'head'), ('seq', 'rep')), parts along dimension 0, may hold values from -6 to 6
- gauge_value: bfloat16 [1024, 4096], P(('groups', 'head'), ('seq', 'rep')), parts along dimension 0, may hold values from -6 to 6
- block_keys: int32 [4, 4, 3], P(('groups', 'head')), parts along dimension 0, may hold values from 0 to 3, as said below
- block_count: int32 [4, 4], P(('groups', 'head')), parts along dimension 0, may hold values from 2 to 3, as said below
- gauge_block: int32 [4, 4], P(('groups', 'head')), parts along dimension 0, may hold values from 0 to 3
Outputs:
- grad_queries: bfloat16 [4, 512, 4096], P(('groups', 'head'), ('seq', 'rep')), parts along dimension 0
- grad_keys: bfloat16 [4, 512, 4096], P(('groups', 'head'), ('seq', 'rep')), parts along dimension 0
- grad_values: bfloat16 [4, 512, 4096], P(('groups', 'head'), ('seq', 'rep')), parts along dimension 0
- grad_gauge_key: float32 [1024, 4096], P(('groups', 'head'), ('seq', 'rep')), parts along dimension 0
- grad_gauge_value: float32 [1024, 4096], P(('groups', 'head'), ('seq', 'rep')), parts along dimension 0
There are 2 independent parts, one for each index of `groups`. A program takes and returns all parts, laid end to end along the dimension named above; each array names one. Nothing has to cross between parts.
Inputs may be any that keep to these rules, and one draw needn't show every extreme that they name: `block_keys`: entry 0 of row [w, i] is i; the entries of a row are distinct. `block_count`: in every window some query block uses 3 key blocks.
All inputs are finite; a program needn't handle non-finite values.
Results may differ from a plain program's by a relative error of at most 0.005.
Values may be sent and summed in bfloat16 or wider, within the bound.
No kernel may reach another device: no remote copies, remote signals or barrier semaphores. Data moves between devices by JAX's collectives and lax.ppermute only.
A program may use at most 64 MiB of HBM per device.

v0:
```python
import functools
import math

import jax
import jax.numpy as jnp
from jax import lax
from jax.experimental import pallas as pl
from jax.experimental.pallas import tpu as pltpu
from jax.sharding import PartitionSpec as P

HD = 128
BLOCK = 128
K_MAX = 3
TOKENS = ("seq", "rep")
ANY = pl.BlockSpec(memory_space=pl.ANY)
SMEM = pl.BlockSpec(memory_space=pltpu.SMEM)
VMEM_LIMIT = 48 * 1024 * 1024


def run_copies(copies):
    for copy in copies:
        copy.start()
    for copy in copies:
        copy.wait()


def pack_kernel(off, width, columns, order, place, *refs):
    arrays, gauges = refs[0:4], refs[4:6]
    sends, gauge_send = refs[6 : 6 + len(order)], refs[6 + len(order)]
    sems, gauge_sems = refs[-2:]
    me = place[0]
    copies = []
    for at, k in enumerate(order):
        start = pl.multiple_of((me ^ k) * columns + off, HD)
        for a in range(4):
            copies.append(
                pltpu.make_async_copy(
                    arrays[a].at[:, pl.ds(start, width)], sends[at].at[a], sems.at[at, a]
                )
            )
    for a in range(2):
        copies.append(
            pltpu.make_async_copy(
                gauges[a].at[:, pl.ds(off, width)], gauge_send.at[a], gauge_sems.at[a]
            )
        )
    run_copies(copies)


def grads_kernel(off, width, columns, order, gauge_order, place, lists, counts, chosen, *refs):
    n_tok, n_gauge = len(order), len(gauge_order)
    refs = list(refs)

    def take(count):
        out = refs[:count]
        del refs[:count]
        return out

    arrays, gauges = take(4), take(2)
    recvs, gauge_recvs = take(n_tok), take(n_gauge)
    outs, gauge_outs = take(n_tok + 1), take(n_gauge + 1)
    tok, gau, acc, gacc, res, in_sems, own_sems, gin_sems, gown_sems, out_sems, gout_sems = refs
    me, gauge_me = place[0], place[1]
    rows = arrays[0].shape[0]
    gauge_rows = gauges[0].shape[0]
    length = tok.shape[1]
    scaling = 1.0 / math.sqrt(HD)

    copies = []
    start = pl.multiple_of(me * columns + off, HD)
    for a in range(4):
        copies.append(
            pltpu.make_async_copy(
                arrays[a].at[:, pl.ds(start, width)],
                tok.at[a, pl.ds(pl.multiple_of(me * rows, rows), rows), :],
                own_sems.at[a],
            )
        )
    for at, k in enumerate(order):
        copies.append(
            pltpu.make_async_copy(
                recvs[at],
                tok.at[:, pl.ds(pl.multiple_of((me ^ k) * rows, rows), rows), :],
                in_sems.at[at],
            )
        )
    for a in range(2):
        copies.append(
            pltpu.make_async_copy(
                gauges[a].at[:, pl.ds(off, width)],
                gau.at[a, pl.ds(pl.multiple_of(gauge_me * gauge_rows, gauge_rows), gauge_rows), :],
                gown_sems.at[a],
            )
        )
    for at, k in enumerate(gauge_order):
        copies.append(
            pltpu.make_async_copy(
                gauge_recvs[at],
                gau.at[
                    :, pl.ds(pl.multiple_of((gauge_me ^ k) * gauge_rows, gauge_rows), gauge_rows), :
                ],
                gin_sems.at[at],
            )
        )
    for copy in copies:
        copy.start()
    acc[...] = jnp.zeros_like(acc)
    gacc[...] = jnp.zeros_like(gacc)
    for copy in copies:
        copy.wait()

    def block(n, carry):
        here = pl.ds(pl.multiple_of(n * BLOCK, BLOCK), BLOCK)
        slots = [
            pl.ds(pl.multiple_of(lists[n, j] * BLOCK, BLOCK), BLOCK) for j in range(K_MAX)
        ]
        gslot = pl.ds(pl.multiple_of(chosen[n] * BLOCK, BLOCK), BLOCK)
        row = lax.broadcasted_iota(jnp.int32, ((K_MAX + 1) * BLOCK, BLOCK), 0)
        allowed = (row < counts[n] * BLOCK) | (row >= K_MAX * BLOCK)
        for h in range(width // HD):
            lanes = slice(h * HD, (h + 1) * HD)
            q = tok[0, here, lanes]
            g = tok[3, here, lanes]
            k = jnp.concatenate([tok[1, s, lanes] for s in slots] + [gau[0, gslot, lanes]], axis=0)
            v = jnp.concatenate([tok[2, s, lanes] for s in slots] + [gau[1, gslot, lanes]], axis=0)
            last = (((1,), (1,)), ((), ()))
            scores = lax.dot_general(k, q, last, preferred_element_type=jnp.float32) * scaling
            scores = jnp.where(allowed, scores, -jnp.inf)
            weights = jnp.exp(scores - jnp.max(scores, axis=0, keepdims=True))
            inverse = 1.0 / jnp.sum(weights, axis=0, keepdims=True)
            probs = weights * inverse
            grad_probs = lax.dot_general(v, g, last, preferred_element_type=jnp.float32)
            delta = jnp.sum(probs * grad_probs, axis=0, keepdims=True)
            grad_scores = (probs * (grad_probs - delta) * scaling).astype(jnp.bfloat16)
            probs_low = probs.astype(jnp.bfloat16)
            res[0, here, lanes] = lax.dot_general(
                grad_scores, k, (((0,), (0,)), ((), ())), preferred_element_type=jnp.float32
            ).astype(jnp.bfloat16)
            dk = jnp.dot(grad_scores, q, preferred_element_type=jnp.float32)
            dv = jnp.dot(probs_low, g, preferred_element_type=jnp.float32)
            for j in range(K_MAX):
                part = slice(j * BLOCK, (j + 1) * BLOCK)
                acc[0, slots[j], lanes] += dk[part]
                acc[1, slots[j], lanes] += dv[part]
            gacc[0, gslot, lanes] += dk[K_MAX * BLOCK :]
            gacc[1, gslot, lanes] += dv[K_MAX * BLOCK :]
        return carry

    lax.fori_loop(0, length // BLOCK, block, 0)

    copies = []
    for at, k in enumerate((0,) + tuple(gauge_order)):
        copies.append(
            pltpu.make_async_copy(
                gacc.at[
                    :, pl.ds(pl.multiple_of((gauge_me ^ k) * gauge_rows, gauge_rows), gauge_rows), :
                ],
                gauge_outs[at],
                gout_sems.at[at],
            )
        )
    for copy in copies:
        copy.start()
    res[1] = acc[0].astype(jnp.bfloat16)
    res[2] = acc[1].astype(jnp.bfloat16)
    token_copies = []
    for at, k in enumerate((0,) + tuple(order)):
        token_copies.append(
            pltpu.make_async_copy(
                res.at[:, pl.ds(pl.multiple_of((me ^ k) * rows, rows), rows), :],
                outs[at],
                out_sems.at[at],
            )
        )
    run_copies(token_copies)
    for copy in copies:
        copy.wait()


def unpack_kernel(off, width, columns, order, held, place, *refs):
    parts = refs[held : held + len(order)]
    outs = refs[held + len(order) : held + len(order) + 3]
    sems = refs[-1]
    me = place[0]
    copies = []
    for at, k in enumerate(order):
        start = pl.multiple_of((me ^ k) * columns + off, HD)
        for a in range(3):
            copies.append(
                pltpu.make_async_copy(
                    parts[at].at[a], outs[a].at[:, pl.ds(start, width)], sems.at[at, a]
                )
            )
    run_copies(copies)


def chunks_of(heads):
    if heads == 1:
        return [(0, HD)]
    half = heads // 2
    return [(0, half * HD), (half * HD, (heads - half) * HD)]


def local(
    sizes,
    queries,
    keys,
    values,
    grad_out,
    gauge_key,
    gauge_value,
    block_keys,
    block_count,
    gauge_block,
):
    total, head_total = sizes
    rows, model = queries.shape[1], queries.shape[2]
    gauge_rows = gauge_key.shape[0]
    length, gauge_total = rows * total, gauge_rows * head_total
    columns = model // total
    bf16, f32 = jnp.bfloat16, jnp.float32
    arrays = [x[0] for x in (queries, keys, values, grad_out)]
    me = lax.axis_index(TOKENS).astype(jnp.int32)
    gauge_me = lax.axis_index("head").astype(jnp.int32)
    place = jnp.stack([me, gauge_me])
    order = tuple(range(total - 1, 0, -1))
    gauge_order = tuple(range(1, head_total))
    lists = (block_keys[0], block_count[0], gauge_block[0])
    params = pltpu.CompilerParams(vmem_limit_bytes=VMEM_LIMIT)

    def swap(x, axis, size, k):
        return lax.ppermute(x, axis, [(i, i ^ k) for i in range(size)])

    chunks = chunks_of(columns // HD)
    received = []
    for off, width in chunks:
        sends = pl.pallas_call(
            functools.partial(pack_kernel, off, width, columns, order),
            out_shape=[jax.ShapeDtypeStruct((4, rows, width), bf16)] * len(order)
            + [jax.ShapeDtypeStruct((2, gauge_rows, width), bf16)],
            in_specs=[SMEM] + [ANY] * 6,
            out_specs=[ANY] * (len(order) + 1),
            scratch_shapes=[
                pltpu.SemaphoreType.DMA((len(order), 4)),
                pltpu.SemaphoreType.DMA((2,)),
            ],
            name="pack",
        )(place, *arrays, gauge_key, gauge_value)
        gauge_send = sends[-1]
        recvs = [swap(s, TOKENS, total, k) for s, k in zip(sends, order)]
        gauge_recvs = [swap(gauge_send, "head", head_total, k) for k in gauge_order]
        received.append((recvs, gauge_recvs))

    outs = None
    gauge_parts = []
    returned = []
    for (off, width), (recvs, gauge_recvs) in zip(chunks, received):
        pieces = pl.pallas_call(
            functools.partial(grads_kernel, off, width, columns, order, gauge_order),
            out_shape=[jax.ShapeDtypeStruct((3, rows, width), bf16)] * total
            + [jax.ShapeDtypeStruct((2, gauge_rows, width), f32)] * head_total,
            in_specs=[SMEM] * 4 + [ANY] * (6 + len(order) + len(gauge_order)),
            out_specs=[ANY] * (total + head_total),
            scratch_shapes=[
                pltpu.VMEM((4, length, width), bf16),
                pltpu.VMEM((2, gauge_total, width), bf16),
                pltpu.VMEM((2, length, width), f32),
                pltpu.VMEM((2, gauge_total, width), f32),
                pltpu.VMEM((3, length, width), bf16),
                pltpu.SemaphoreType.DMA((max(len(order), 1),)),
                pltpu.SemaphoreType.DMA((4,)),
                pltpu.SemaphoreType.DMA((max(len(gauge_order), 1),)),
                pltpu.SemaphoreType.DMA((2,)),
                pltpu.SemaphoreType.DMA((total,)),
                pltpu.SemaphoreType.DMA((head_total,)),
            ],
            compiler_params=params,
            name="grads",
        )(place, *lists, *arrays, gauge_key, gauge_value, *recvs, *gauge_recvs)
        back = [pieces[0]] + [swap(p, TOKENS, total, k) for p, k in zip(pieces[1:total], order)]
        gauge_back = [
            swap(p, "head", head_total, k) for p, k in zip(pieces[total + 1 :], gauge_order)
        ]
        gauge_parts.append(functools.reduce(jnp.add, gauge_back, pieces[total]))
        returned.append(back)

    for (off, width), back in zip(chunks, returned):
        held = 0 if outs is None else 3
        slots = (0,) + order
        outs = pl.pallas_call(
            functools.partial(unpack_kernel, off, width, columns, slots, held),
            out_shape=[jax.ShapeDtypeStruct((rows, model), bf16)] * 3,
            in_specs=[SMEM] + [ANY] * (held + total),
            out_specs=[ANY] * 3,
            scratch_shapes=[pltpu.SemaphoreType.DMA((total, 3))],
            input_output_aliases={1 + a: a for a in range(held)},
            name="unpack",
        )(place, *(outs if held else []), *back)

    gauge_grads = jnp.concatenate(gauge_parts, axis=2)
    return (outs[0][None], outs[1][None], outs[2][None], gauge_grads[0], gauge_grads[1])


def solution(mesh):
    tokens = P(("groups", "head"), TOKENS, None)
    gauges = P(("groups", "head"), TOKENS)
    lists = P(("groups", "head"), None, None)
    counts = P(("groups", "head"), None)
    sizes = (mesh.shape["seq"] * mesh.shape["rep"], mesh.shape["head"])
    return jax.shard_map(
        functools.partial(local, sizes),
        mesh=mesh,
        in_specs=(tokens,) * 4 + (gauges,) * 2 + (lists, counts, counts),
        out_specs=(tokens,) * 3 + (gauges,) * 2,
        check_vma=False,
    )
```

profile of v0, /device:TPU:0, one launch (start us, length us, event | category | flops | bytes accessed | tf_op | source)
XLA Modules:
  0.0 250.7 jit_solution(9879987463821514911)
XLA Ops:
  0.6 0.7 pad_add_fusion.place
  1.3 37.8 %pack.3 = (bf16[4,64,256]{2,1,0:T(8,128)(2,1)}, bf16[4,64,256]{2,1,0:T(8,128)(2,1)}, bf16[4,64,256]{2,1,0:T(8,128)(2,1)}, bf16[4,64,256]{2,1,0:T(8,128)(2,1)}, b...) custom-call(s32[2]{0:T(128)} %pad_add_fusion.place, ...), custom_call_target="tpu_custom_call" | custom-call | tf_op jit(solution)/shard_map/pack/pallas_call | solution.py:237
  39.1 4.6 %collective-permute-start.15 = (bf16[4,64,256]{2,1,0:T(8,128)(2,1)}, bf16[4,64,256]{2,1,0:T(8,128)(2,1)S(1)}, u32[]{:S(2)}, u32[]{:S(2)}) collective-permute-start(bf16[4,64,256]{2,1,0:T(8,128)(2,1)} %get-tuple-element.66), channel_id=1, source_target_pairs={{0,13},{1,12},{4,9},{5,8},{8,5},{9,4},{12,1},{13,0},{2,15},{3,14},... | collective-permute-start | bytes 393224 | tf_op jit(solution)/shard_map/ppermute | solution.py:232
  44.7 2.2 collective-permute-start.18
  46.8 1.0 collective-permute-start.19
  47.9 11.4 %collective-permute-start.20 = (bf16[4,64,256]{2,1,0:T(8,128)(2,1)}, bf16[4,64,256]{2,1,0:T(8,128)(2,1)S(1)}, u32[]{:S(2)}, u32[]{:S(2)}) collective-permute-start(bf16[4,64,256]{2,1,0:T(8,128)(2,1)} %get-tuple-element.71), channel_id=1, source_target_pairs={{0,4},{1,5},{4,0},{5,1},{8,12},{9,13},{12,8},{13,9},{2,6},{3,7},{6... | collective-permute-start | bytes 393224 | tf_op jit(solution)/shard_map/ppermute | solution.py:232
  59.9 1.5 collective-permute-start.22
  61.4 3.0 %collective-permute-done.17.refs_8_ = bf16[4,64,256]{2,1,0:T(8,128)(2,1)S(1)} collective-permute-done((bf16[4,64,256]{2,1,0:T(8,128)(2,1)}, bf16[4,64,256]{2,1,0:T(8,128)(2,1)S(1)}, u32[]{:S(2)}, u32[]{:S(2)}) %collective-permute-start.17) | collective-permute-done | bytes 131104 | tf_op jit(solution)/shard_map/ppermute | solution.py:232
  65.2 37.9 %pack.2 = (bf16[4,64,256]{2,1,0:T(8,128)(2,1)}, bf16[4,64,256]{2,1,0:T(8,128)(2,1)}, bf16[4,64,256]{2,1,0:T(8,128)(2,1)}, bf16[4,64,256]{2,1,0:T(8,128)(2,1)}, b...) custom-call(s32[2]{0:T(128)} %pad_add_fusion.place, ...), custom_call_target="tpu_custom_call" | custom-call | tf_op jit(solution)/shard_map/pack/pallas_call | solution.py:237
  103.8 2.6 %collective-permute-start = (bf16[4,64,256]{2,1,0:T(8,128)(2,1)}, bf16[4,64,256]{2,1,0:T(8,128)(2,1)S(1)}, u32[]{:S(2)}, u32[]{:S(2)}) collective-permute-start(bf16[4,64,256]{2,1,0:T(8,128)(2,1)} %get-tuple-element.47), channel_id=1, source_target_pairs={{0,13},{1,12},{4,9},{5,8},{8,5},{9,4},{12,1},{13,0},{2,15},{3,14},... | collective-permute-start | bytes 393224 | tf_op jit(solution)/shard_map/ppermute | solution.py:232
  107.1 1.2 collective-permute-start.1
  109.6 1.5 collective-permute-start.7
  111.2 0.7 copy-done.16
  111.8 6.8 %collective-permute-start.3 = (bf16[4,64,256]{2,1,0:T(8,128)(2,1)}, bf16[4,64,256]{2,1,0:T(8,128)(2,1)}, u32[]{:S(2)}, u32[]{:S(2)}) collective-permute-start(bf16[4,64,256]{2,1,0:T(8,128)(2,1)} %get-tuple-element.50), channel_id=1, source_target_pairs={{0,8},{1,9},{4,12},{5,13},{8,0},{9,1},{12,4},{13,5},{2,10},{3,11},... | collective-permute-start | bytes 393224 | tf_op jit(solution)/shard_map/ppermute | solution.py:232
  118.6 0.7 copy-done.20
  119.3 1.6 collective-permute-start.4
  120.9 4.7 %collective-permute-done.2.refs_8_ = bf16[4,64,256]{2,1,0:T(8,128)(2,1)S(1)} collective-permute-done((bf16[4,64,256]{2,1,0:T(8,128)(2,1)}, bf16[4,64,256]{2,1,0:T(8,128)(2,1)S(1)}, u32[]{:S(2)}, u32[]{:S(2)}) %collective-permute-start.2) | collective-permute-done | bytes 131104 | tf_op jit(solution)/shard_map/ppermute | solution.py:232
  125.6 0.7 copy-done.22
  126.2 0.7 collective-permute-start.5
  128.1 0.9 copy-done.9
  129.0 0.9 copy-done.11
  129.9 0.9 copy-done.13
  130.8 0.9 copy-done.15
  131.7 0.9 copy-done.19
  132.6 0.9 copy-done.25
  133.5 7.5 %grads.3 = (bf16[3,64,256]{2,1,0:T(8,128)(2,1)S(1)}, bf16[3,64,256]{2,1,0:T(8,128)(2,1)S(1)}, bf16[3,64,256]{2,1,0:T(8,128)(2,1)S(1)}, bf16[3,64,256]{2,1,0:T(8,...) custom-call(s32[2]{0:T(128)S(1)} %copy-done.28, ...), custom_call_target="tpu_custom_call" | custom-call | tf_op jit(solution)/shard_map/grads/pallas_call | solution.py:258
  141.7 1.3 collective-permute-start.31
  143.0 8.1 %grads.2 = (bf16[3,64,256]{2,1,0:T(8,128)(2,1)S(1)}, bf16[3,64,256]{2,1,0:T(8,128)(2,1)S(1)}, bf16[3,64,256]{2,1,0:T(8,128)(2,1)S(1)}, bf16[3,64,256]{2,1,0:T(8,...) custom-call(s32[2]{0:T(128)S(1)} %copy-done.28, ...), custom_call_target="tpu_custom_call" | custom-call | tf_op jit(solution)/shard_map/grads/pallas_call | solution.py:258
  151.2 0.8 copy-done.6
  152.6 0.7 collective-permute-start.30
  153.3 1.3 collective-permute-start.23
  154.6 1.7 collective-permute-start.24
  156.3 1.0 collective-permute-start.25
  157.3 2.8 %collective-permute-done.23.refs_4_ = bf16[3,64,256]{2,1,0:T(8,128)(2,1)S(1)} collective-permute-done((bf16[3,64,256]{2,1,0:T(8,128)(2,1)S(1)}, bf16[3,64,256]{2,1,0:T(8,128)(2,1)S(1)}, u32[]{:S(2)}, u32[]{:S(2)}) %collective-permute-start.23) | collective-permute-done | bytes 98336 | tf_op jit(solution)/shard_map/ppermute | solution.py:232
  160.1 7.2 %collective-permute-start.26 = (bf16[3,64,256]{2,1,0:T(8,128)(2,1)S(1)}, bf16[3,64,256]{2,1,0:T(8,128)(2,1)S(1)}, u32[]{:S(2)}, u32[]{:S(2)}) collective-permute-start(bf16[3,64,256]{2,1,0:T(8,128)(2,1)S(1)} %get-tuple-element.78), channel_id=1, source_target_pairs={{0,8},{1,9},{4,12},{5,13},{8,0},{9,1},{12,4},{13,5},{2,10},{3,11},... | collective-permute-start | bytes 294920 | tf_op jit(solution)/shard_map/ppermute | solution.py:232
  167.2 0.8 collective-permute-start.8
  168.0 6.3 %collective-permute-done.25.refs_6_ = bf16[3,64,256]{2,1,0:T(8,128)(2,1)S(1)} collective-permute-done((bf16[3,64,256]{2,1,0:T(8,128)(2,1)S(1)}, bf16[3,64,256]{2,1,0:T(8,128)(2,1)S(1)}, u32[]{:S(2)}, u32[]{:S(2)}) %collective-permute-start.25) | collective-permute-done | bytes 98336 | tf_op jit(solution)/shard_map/ppermute | solution.py:232
  174.3 2.2 collective-permute-start.9
  176.6 8.5 %collective-permute-start.11 = (bf16[3,64,256]{2,1,0:T(8,128)(2,1)S(1)}, bf16[3,64,256]{2,1,0:T(8,128)(2,1)S(1)}, u32[]{:S(2)}, u32[]{:S(2)}) collective-permute-start(bf16[3,64,256]{2,1,0:T(8,128)(2,1)S(1)} %get-tuple-element.59), channel_id=1, source_target_pairs={{0,8},{1,9},{4,12},{5,13},{8,0},{9,1},{12,4},{13,5},{2,10},{3,11},... | collective-permute-start | bytes 294920 | tf_op jit(solution)/shard_map/ppermute | solution.py:232
  185.1 1.9 collective-permute-start.12
  187.0 2.2 collective-permute-done.10.refs_3_
  189.2 1.8 collective-permute-done.11.refs_4_
  191.1 2.0 collective-permute-done.12.refs_5_
  193.1 2.2 collective-permute-done.13.refs_6_
  195.9 25.8 %unpack.2 = (bf16[64,4096]{1,0:T(8,128)(2,1)}, bf16[64,4096]{1,0:T(8,128)(2,1)}, bf16[64,4096]{1,0:T(8,128)(2,1)}) custom-call(s32[2]{0:T(128)} %pad_add_fusion.place, bf16[3,64,256]{2,1,0:T(8,128)(2,1)} %copy-done.27, bf16[3,64,256]{2,1,0:T(8,128)(2,1)} %copy-done.38, bf16[3,64,256]{2,1,0:T(8,128)(2,1)} %copy-done.39, bf16[3,64,256]{2,1,0:T(8,128)(2,1)} %copy-done.40, ...), custom_call_target="tpu_custom_call" | custom-call | tf_op jit(solution)/shard_map/unpack/pallas_call | solution.py:290
  222.5 25.8 %unpack.3 = (bf16[64,4096]{1,0:T(8,128)(2,1)}, bf16[64,4096]{1,0:T(8,128)(2,1)}, bf16[64,4096]{1,0:T(8,128)(2,1)}) custom-call(s32[2]{0:T(128)} %pad_add_fusion.place, bf16[64,4096]{1,0:T(8,128)(2,1)} %get-tuple-element.63.refs_0_, bf16[64,4096]{1,0:T(8,128)(2,1)} %get-tuple-element.64.refs_1_, ...), custom_call_target="tpu_custom_call", output_to_operand_aliasing={{0}: (1, {}), {1}: (2, {}), {2}: (3, {})} | custom-call | tf_op jit(solution)/shard_map/unpack/pallas_call | solution.py:290
  248.3 1.2 add.11
  249.6 1.1 fusion.2
  (119 shorter events, 9.1 us)
Async XLA Ops:
  39.1 8.8 %collective-permute-start.15 = (bf16[4,64,256]{2,1,0:T(8,128)(2,1)}, bf16[4,64,256]{2,1,0:T(8,128)(2,1)S(1)}, u32[]{:S(2)}, u32[]{:S(2)}) collective-permute-start(bf16[4,64,256]{2,1,0:T(8,128)(2,1)} %get-tuple-element.66), channel_id=1, source_target_pairs={{0,13},{1,12},{4,9},{5,8},{8,5},{9,4},{12,1},{13,0},{2,15},{3,14},... | collective-permute-start | bytes 393224 | tf_op jit(solution)/shard_map/ppermute | solution.py:232
  43.6 15.7 %collective-permute-start.16 = (bf16[4,64,256]{2,1,0:T(8,128)(2,1)}, bf16[4,64,256]{2,1,0:T(8,128)(2,1)S(1)}, u32[]{:S(2)}, u32[]{:S(2)}) collective-permute-start(bf16[4,64,256]{2,1,0:T(8,128)(2,1)} %get-tuple-element.67), channel_id=1, source_target_pairs={{0,12},{1,13},{4,8},{5,9},{8,4},{9,5},{12,0},{13,1},{2,14},{3,15},... | collective-permute-start | bytes 393224 | tf_op jit(solution)/shard_map/ppermute | solution.py:232
  44.3 20.2 %collective-permute-start.17 = (bf16[4,64,256]{2,1,0:T(8,128)(2,1)}, bf16[4,64,256]{2,1,0:T(8,128)(2,1)S(1)}, u32[]{:S(2)}, u32[]{:S(2)}) collective-permute-start(bf16[4,64,256]{2,1,0:T(8,128)(2,1)} %get-tuple-element.68), channel_id=1, source_target_pairs={{0,9},{1,8},{4,13},{5,12},{8,1},{9,0},{12,5},{13,4},{2,11},{3,10},... | collective-permute-start | bytes 393224 | tf_op jit(solution)/shard_map/ppermute | solution.py:232
  44.7 58.5 %collective-permute-start.18 = (bf16[4,64,256]{2,1,0:T(8,128)(2,1)}, bf16[4,64,256]{2,1,0:T(8,128)(2,1)S(1)}, u32[]{:S(2)}, u32[]{:S(2)}) collective-permute-start(bf16[4,64,256]{2,1,0:T(8,128)(2,1)} %get-tuple-element.69), channel_id=1, source_target_pairs={{0,8},{1,9},{4,12},{5,13},{8,0},{9,1},{12,4},{13,5},{2,10},{3,11},... | collective-permute-start | bytes 393224 | tf_op jit(solution)/shard_map/ppermute | solution.py:232
  46.8 59.6 %collective-permute-start.19 = (bf16[4,64,256]{2,1,0:T(8,128)(2,1)}, bf16[4,64,256]{2,1,0:T(8,128)(2,1)S(1)}, u32[]{:S(2)}, u32[]{:S(2)}) collective-permute-start(bf16[4,64,256]{2,1,0:T(8,128)(2,1)} %get-tuple-element.70), channel_id=1, source_target_pairs={{0,5},{1,4},{4,1},{5,0},{8,13},{9,12},{12,9},{13,8},{2,7},{3,6},{6... | collective-permute-start | bytes 393224 | tf_op jit(solution)/shard_map/ppermute | solution.py:232
  47.9 60.5 %collective-permute-start.20 = (bf16[4,64,256]{2,1,0:T(8,128)(2,1)}, bf16[4,64,256]{2,1,0:T(8,128)(2,1)S(1)}, u32[]{:S(2)}, u32[]{:S(2)}) collective-permute-start(bf16[4,64,256]{2,1,0:T(8,128)(2,1)} %get-tuple-element.71), channel_id=1, source_target_pairs={{0,4},{1,5},{4,0},{5,1},{8,12},{9,13},{12,8},{13,9},{2,6},{3,7},{6... | collective-permute-start | bytes 393224 | tf_op jit(solution)/shard_map/ppermute | solution.py:232
  59.9 67.0 %collective-permute-start.22 = (bf16[2,256,256]{2,1,0:T(8,128)(2,1)}, bf16[2,256,256]{2,1,0:T(8,128)(2,1)S(1)}, u32[]{:S(2)}, u32[]{:S(2)}) collective-permute-start(bf16[2,256,256]{2,1,0:T(8,128)(2,1)} %get-tuple-element.73), channel_id=1, source_target_pairs={{0,2},{2,0},{1,3},{3,1},{4,6},{6,4},{5,7},{7,5},{8,10},{10,8},{9,1... | collective-permute-start | bytes 786440 | tf_op jit(solution)/shard_map/ppermute | solution.py:232
  65.1 62.3 %copy-start = (bf16[1,64,4096]{2,1,0:T(8,128)(2,1)S(1)}, bf16[1,64,4096]{2,1,0:T(8,128)(2,1)}, u32[]{:S(2)}) copy-start(bf16[1,64,4096]{2,1,0:T(8,128)(2,1)} %param.9) | copy-start | bytes 1572868
  65.1 62.3 %copy-start.1 = (bf16[1,64,4096]{2,1,0:T(8,128)(2,1)S(1)}, bf16[1,64,4096]{2,1,0:T(8,128)(2,1)}, u32[]{:S(2)}) copy-start(bf16[1,64,4096]{2,1,0:T(8,128)(2,1)} %param.10) | copy-start | bytes 1572868
  65.1 62.4 %copy-start.2 = (bf16[1,64,4096]{2,1,0:T(8,128)(2,1)S(1)}, bf16[1,64,4096]{2,1,0:T(8,128)(2,1)}, u32[]{:S(2)}) copy-start(bf16[1,64,4096]{2,1,0:T(8,128)(2,1)} %param.11) | copy-start | bytes 1572868
  65.1 62.4 %copy-start.3 = (bf16[1,64,4096]{2,1,0:T(8,128)(2,1)S(1)}, bf16[1,64,4096]{2,1,0:T(8,128)(2,1)}, u32[]{:S(2)}) copy-start(bf16[1,64,4096]{2,1,0:T(8,128)(2,1)} %param.12) | copy-start | bytes 1572868
  65.1 62.4 %copy-start.4 = (bf16[256,512]{1,0:T(8,128)(2,1)S(1)}, bf16[256,512]{1,0:T(8,128)(2,1)}, u32[]{:S(2)}) copy-start(bf16[256,512]{1,0:T(8,128)(2,1)} %refs_4_.7) | copy-start | bytes 786436
  65.1 62.4 %copy-start.5 = (bf16[256,512]{1,0:T(8,128)(2,1)S(1)}, bf16[256,512]{1,0:T(8,128)(2,1)}, u32[]{:S(2)}) copy-start(bf16[256,512]{1,0:T(8,128)(2,1)} %refs_5_.7) | copy-start | bytes 786436
  65.1 43.9 %collective-permute-start.21 = (bf16[4,64,256]{2,1,0:T(8,128)(2,1)}, bf16[4,64,256]{2,1,0:T(8,128)(2,1)S(1)}, u32[]{:S(2)}, u32[]{:S(2)}) collective-permute-start(bf16[4,64,256]{2,1,0:T(8,128)(2,1)} %get-tuple-element.72), channel_id=1, source_target_pairs={{0,1},{1,0},{4,5},{5,4},{8,9},{9,8},{12,13},{13,12},{2,3},{3,2},{6... | collective-permute-start | bytes 393224 | tf_op jit(solution)/shard_map/ppermute | solution.py:232
  103.8 7.3 %collective-permute-start = (bf16[4,64,256]{2,1,0:T(8,128)(2,1)}, bf16[4,64,256]{2,1,0:T(8,128)(2,1)S(1)}, u32[]{:S(2)}, u32[]{:S(2)}) collective-permute-start(bf16[4,64,256]{2,1,0:T(8,128)(2,1)} %get-tuple-element.47), channel_id=1, source_target_pairs={{0,13},{1,12},{4,9},{5,8},{8,5},{9,4},{12,1},{13,0},{2,15},{3,14},... | collective-permute-start | bytes 393224 | tf_op jit(solution)/shard_map/ppermute | solution.py:232
  107.1 11.5 %collective-permute-start.1 = (bf16[4,64,256]{2,1,0:T(8,128)(2,1)}, bf16[4,64,256]{2,1,0:T(8,128)(2,1)S(1)}, u32[]{:S(2)}, u32[]{:S(2)}) collective-permute-start(bf16[4,64,256]{2,1,0:T(8,128)(2,1)} %get-tuple-element.48), channel_id=1, source_target_pairs={{0,12},{1,13},{4,8},{5,9},{8,4},{9,5},{12,0},{13,1},{2,14},{3,15},... | collective-permute-start | bytes 393224 | tf_op jit(solution)/shard_map/ppermute | solution.py:232
  109.0 16.6 %collective-permute-start.2 = (bf16[4,64,256]{2,1,0:T(8,128)(2,1)}, bf16[4,64,256]{2,1,0:T(8,128)(2,1)S(1)}, u32[]{:S(2)}, u32[]{:S(2)}) collective-permute-start(bf16[4,64,256]{2,1,0:T(8,128)(2,1)} %get-tuple-element.49), channel_id=1, source_target_pairs={{0,9},{1,8},{4,13},{5,12},{8,1},{9,0},{12,5},{13,4},{2,11},{3,10},... | collective-permute-start | bytes 393224 | tf_op jit(solution)/shard_map/ppermute | solution.py:232
  109.6 33.3 %collective-permute-start.7 = (bf16[2,256,256]{2,1,0:T(8,128)(2,1)}, bf16[2,256,256]{2,1,0:T(8,128)(2,1)}, u32[]{:S(2)}, u32[]{:S(2)}) collective-permute-start(bf16[2,256,256]{2,1,0:T(8,128)(2,1)} %get-tuple-element.54), channel_id=1, source_target_pairs={{0,2},{2,0},{1,3},{3,1},{4,6},{6,4},{5,7},{7,5},{8,10},{10,8},{9,1... | collective-permute-start | bytes 786440 | tf_op jit(solution)/shard_map/ppermute | solution.py:232
  111.8 29.8 %collective-permute-start.3 = (bf16[4,64,256]{2,1,0:T(8,128)(2,1)}, bf16[4,64,256]{2,1,0:T(8,128)(2,1)}, u32[]{:S(2)}, u32[]{:S(2)}) collective-permute-start(bf16[4,64,256]{2,1,0:T(8,128)(2,1)} %get-tuple-element.50), channel_id=1, source_target_pairs={{0,8},{1,9},{4,12},{5,13},{8,0},{9,1},{12,4},{13,5},{2,10},{3,11},... | collective-permute-start | bytes 393224 | tf_op jit(solution)/shard_map/ppermute | solution.py:232
  119.3 8.0 %copy-start.45 = (s32[1,4,3]{1,0,2:T(1,128)S(1)}, s32[1,4,3]{1,0,2:T(1,128)}, u32[]{:S(2)}) copy-start(s32[1,4,3]{1,0,2:T(1,128)} %param.15) | copy-start | bytes 148
  119.3 23.7 %collective-permute-start.4 = (bf16[4,64,256]{2,1,0:T(8,128)(2,1)}, bf16[4,64,256]{2,1,0:T(8,128)(2,1)}, u32[]{:S(2)}, u32[]{:S(2)}) collective-permute-start(bf16[4,64,256]{2,1,0:T(8,128)(2,1)} %get-tuple-element.51), channel_id=1, source_target_pairs={{0,5},{1,4},{4,1},{5,0},{8,13},{9,12},{12,9},{13,8},{2,7},{3,6},{6... | collective-permute-start | bytes 393224 | tf_op jit(solution)/shard_map/ppermute | solution.py:232
  126.2 16.7 %collective-permute-start.5 = (bf16[4,64,256]{2,1,0:T(8,128)(2,1)}, bf16[4,64,256]{2,1,0:T(8,128)(2,1)}, u32[]{:S(2)}, u32[]{:S(2)}) collective-permute-start(bf16[4,64,256]{2,1,0:T(8,128)(2,1)} %get-tuple-element.52), channel_id=1, source_target_pairs={{0,4},{1,5},{4,0},{5,1},{8,12},{9,13},{12,8},{13,9},{2,6},{3,7},{6... | collective-permute-start | bytes 393224 | tf_op jit(solution)/shard_map/ppermute | solution.py:232
  126.9 16.1 %collective-permute-start.6 = (bf16[4,64,256]{2,1,0:T(8,128)(2,1)}, bf16[4,64,256]{2,1,0:T(8,128)(2,1)}, u32[]{:S(2)}, u32[]{:S(2)}) collective-permute-start(bf16[4,64,256]{2,1,0:T(8,128)(2,1)} %get-tuple-element.53), channel_id=1, source_target_pairs={{0,1},{1,0},{4,5},{5,4},{8,9},{9,8},{12,13},{13,12},{2,3},{3,2},{6... | collective-permute-start | bytes 393224 | tf_op jit(solution)/shard_map/ppermute | solution.py:232
  133.5 9.5 %copy-start.17 = (bf16[4,64,256]{2,1,0:T(8,128)(2,1)S(1)}, bf16[4,64,256]{2,1,0:T(8,128)(2,1)}, u32[]{:S(2)}) copy-start(bf16[4,64,256]{2,1,0:T(8,128)(2,1)} %copy-done.16) | copy-start | bytes 393220
  133.5 9.5 %copy-start.21 = (bf16[4,64,256]{2,1,0:T(8,128)(2,1)S(1)}, bf16[4,64,256]{2,1,0:T(8,128)(2,1)}, u32[]{:S(2)}) copy-start(bf16[4,64,256]{2,1,0:T(8,128)(2,1)} %copy-done.20) | copy-start | bytes 393220
  133.5 9.5 %copy-start.23 = (bf16[4,64,256]{2,1,0:T(8,128)(2,1)S(1)}, bf16[4,64,256]{2,1,0:T(8,128)(2,1)}, u32[]{:S(2)}) copy-start(bf16[4,64,256]{2,1,0:T(8,128)(2,1)} %copy-done.22) | copy-start | bytes 393220
  141.7 106.7 %collective-permute-start.31 = (f32[2,256,256]{2,1,0:T(8,128)}, f32[2,256,256]{2,1,0:T(8,128)}, u32[]{:S(2)}, u32[]{:S(2)}) collective-permute-start(f32[2,256,256]{2,1,0:T(8,128)} %get-tuple-element.88), channel_id=1, source_target_pairs={{0,2},{2,0},{1,3},{3,1},{4,6},{6,4},{5,7},{7,5},{8,10},{10,8},{9,1... | collective-permute-start | bytes 1572872 | tf_op jit(solution)/shard_map/ppermute | solution.py:232
  152.6 96.9 %collective-permute-start.30 = (f32[2,256,256]{2,1,0:T(8,128)}, f32[2,256,256]{2,1,0:T(8,128)S(1)}, u32[]{:S(2)}, u32[]{:S(2)}) collective-permute-start(f32[2,256,256]{2,1,0:T(8,128)} %get-tuple-element.86), channel_id=1, source_target_pairs={{0,2},{2,0},{1,3},{3,1},{4,6},{6,4},{5,7},{7,5},{8,10},{10,8},{9,1... | collective-permute-start | bytes 1572872 | tf_op jit(solution)/shard_map/ppermute | solution.py:232
  153.3 6.7 %collective-permute-start.23 = (bf16[3,64,256]{2,1,0:T(8,128)(2,1)S(1)}, bf16[3,64,256]{2,1,0:T(8,128)(2,1)S(1)}, u32[]{:S(2)}, u32[]{:S(2)}) collective-permute-start(bf16[3,64,256]{2,1,0:T(8,128)(2,1)S(1)} %get-tuple-element.75), channel_id=1, source_target_pairs={{0,13},{1,12},{4,9},{5,8},{8,5},{9,4},{12,1},{13,0},{2,15},{3,14},... | collective-permute-start | bytes 294920 | tf_op jit(solution)/shard_map/ppermute | solution.py:232
  154.6 12.6 %collective-permute-start.24 = (bf16[3,64,256]{2,1,0:T(8,128)(2,1)S(1)}, bf16[3,64,256]{2,1,0:T(8,128)(2,1)S(1)}, u32[]{:S(2)}, u32[]{:S(2)}) collective-permute-start(bf16[3,64,256]{2,1,0:T(8,128)(2,1)S(1)} %get-tuple-element.76), channel_id=1, source_target_pairs={{0,12},{1,13},{4,8},{5,9},{8,4},{9,5},{12,0},{13,1},{2,14},{3,15},... | collective-permute-start | bytes 294920 | tf_op jit(solution)/shard_map/ppermute | solution.py:232
  156.3 18.0 %collective-permute-start.25 = (bf16[3,64,256]{2,1,0:T(8,128)(2,1)S(1)}, bf16[3,64,256]{2,1,0:T(8,128)(2,1)S(1)}, u32[]{:S(2)}, u32[]{:S(2)}) collective-permute-start(bf16[3,64,256]{2,1,0:T(8,128)(2,1)S(1)} %get-tuple-element.77), channel_id=1, source_target_pairs={{0,9},{1,8},{4,13},{5,12},{8,1},{9,0},{12,5},{13,4},{2,11},{3,10},... | collective-permute-start | bytes 294920 | tf_op jit(solution)/shard_map/ppermute | solution.py:232
  160.1 61.7 %copy-start.31 = (bf16[3,64,256]{2,1,0:T(8,128)(2,1)}, bf16[3,64,256]{2,1,0:T(8,128)(2,1)S(1)}, u32[]{:S(2)}) copy-start(bf16[3,64,256]{2,1,0:T(8,128)(2,1)S(1)} %collective-permute-done.23.refs_4_) | copy-start | bytes 294916
  160.1 16.5 %collective-permute-start.26 = (bf16[3,64,256]{2,1,0:T(8,128)(2,1)S(1)}, bf16[3,64,256]{2,1,0:T(8,128)(2,1)S(1)}, u32[]{:S(2)}, u32[]{:S(2)}) collective-permute-start(bf16[3,64,256]{2,1,0:T(8,128)(2,1)S(1)} %get-tuple-element.78), channel_id=1, source_target_pairs={{0,8},{1,9},{4,12},{5,13},{8,0},{9,1},{12,4},{13,5},{2,10},{3,11},... | collective-permute-start | bytes 294920 | tf_op jit(solution)/shard_map/ppermute | solution.py:232
  167.2 54.5 %copy-start.32 = (bf16[3,64,256]{2,1,0:T(8,128)(2,1)}, bf16[3,64,256]{2,1,0:T(8,128)(2,1)S(1)}, u32[]{:S(2)}) copy-start(bf16[3,64,256]{2,1,0:T(8,128)(2,1)S(1)} %collective-permute-done.24.refs_5_) | copy-start | bytes 294916
  167.2 9.3 %collective-permute-start.8 = (bf16[3,64,256]{2,1,0:T(8,128)(2,1)S(1)}, bf16[3,64,256]{2,1,0:T(8,128)(2,1)S(1)}, u32[]{:S(2)}, u32[]{:S(2)}) collective-permute-start(bf16[3,64,256]{2,1,0:T(8,128)(2,1)S(1)} %get-tuple-element.56), channel_id=1, source_target_pairs={{0,13},{1,12},{4,9},{5,8},{8,5},{9,4},{12,1},{13,0},{2,15},{3,14},... | collective-permute-start | bytes 294920 | tf_op jit(solution)/shard_map/ppermute | solution.py:232
  174.3 47.4 %copy-start.33 = (bf16[3,64,256]{2,1,0:T(8,128)(2,1)}, bf16[3,64,256]{2,1,0:T(8,128)(2,1)S(1)}, u32[]{:S(2)}) copy-start(bf16[3,64,256]{2,1,0:T(8,128)(2,1)S(1)} %collective-permute-done.25.refs_6_) | copy-start | bytes 294916
  174.3 10.8 %collective-permute-start.9 = (bf16[3,64,256]{2,1,0:T(8,128)(2,1)S(1)}, bf16[3,64,256]{2,1,0:T(8,128)(2,1)S(1)}, u32[]{:S(2)}, u32[]{:S(2)}) collective-permute-start(bf16[3,64,256]{2,1,0:T(8,128)(2,1)S(1)} %get-tuple-element.57), channel_id=1, source_target_pairs={{0,12},{1,13},{4,8},{5,9},{8,4},{9,5},{12,0},{13,1},{2,14},{3,15},... | collective-permute-start | bytes 294920 | tf_op jit(solution)/shard_map/ppermute | solution.py:232
  176.5 45.2 %copy-start.34 = (bf16[3,64,256]{2,1,0:T(8,128)(2,1)}, bf16[3,64,256]{2,1,0:T(8,128)(2,1)S(1)}, u32[]{:S(2)}) copy-start(bf16[3,64,256]{2,1,0:T(8,128)(2,1)S(1)} %collective-permute-done.26.refs_7_) | copy-start | bytes 294916
  176.5 12.6 %collective-permute-start.10 = (bf16[3,64,256]{2,1,0:T(8,128)(2,1)S(1)}, bf16[3,64,256]{2,1,0:T(8,128)(2,1)S(1)}, u32[]{:S(2)}, u32[]{:S(2)}) collective-permute-start(bf16[3,64,256]{2,1,0:T(8,128)(2,1)S(1)} %get-tuple-element.58), channel_id=1, source_target_pairs={{0,9},{1,8},{4,13},{5,12},{8,1},{9,0},{12,5},{13,4},{2,11},{3,10},... | collective-permute-start | bytes 294920 | tf_op jit(solution)/shard_map/ppermute | solution.py:232
  176.6 18.8 %copy-start.38 = (bf16[3,64,256]{2,1,0:T(8,128)(2,1)}, bf16[3,64,256]{2,1,0:T(8,128)(2,1)S(1)}, u32[]{:S(2)}) copy-start(bf16[3,64,256]{2,1,0:T(8,128)(2,1)S(1)} %collective-permute-done.8.refs_1_) | copy-start | bytes 294916
  176.6 14.4 %collective-permute-start.11 = (bf16[3,64,256]{2,1,0:T(8,128)(2,1)S(1)}, bf16[3,64,256]{2,1,0:T(8,128)(2,1)S(1)}, u32[]{:S(2)}, u32[]{:S(2)}) collective-permute-start(bf16[3,64,256]{2,1,0:T(8,128)(2,1)S(1)} %get-tuple-element.59), channel_id=1, source_target_pairs={{0,8},{1,9},{4,12},{5,13},{8,0},{9,1},{12,4},{13,5},{2,10},{3,11},... | collective-permute-start | bytes 294920 | tf_op jit(solution)/shard_map/ppermute | solution.py:232
  185.1 10.3 %copy-start.39 = (bf16[3,64,256]{2,1,0:T(8,128)(2,1)}, bf16[3,64,256]{2,1,0:T(8,128)(2,1)S(1)}, u32[]{:S(2)}) copy-start(bf16[3,64,256]{2,1,0:T(8,128)(2,1)S(1)} %collective-permute-done.9.refs_2_) | copy-start | bytes 294916
  185.1 8.0 %collective-permute-start.12 = (bf16[3,64,256]{2,1,0:T(8,128)(2,1)S(1)}, bf16[3,64,256]{2,1,0:T(8,128)(2,1)S(1)}, u32[]{:S(2)}, u32[]{:S(2)}) collective-permute-start(bf16[3,64,256]{2,1,0:T(8,128)(2,1)S(1)} %get-tuple-element.60), channel_id=1, source_target_pairs={{0,5},{1,4},{4,1},{5,0},{8,13},{9,12},{12,9},{13,8},{2,7},{3,6},{6... | collective-permute-start | bytes 294920 | tf_op jit(solution)/shard_map/ppermute | solution.py:232
  189.2 6.1 %collective-permute-start.13 = (bf16[3,64,256]{2,1,0:T(8,128)(2,1)S(1)}, bf16[3,64,256]{2,1,0:T(8,128)(2,1)S(1)}, u32[]{:S(2)}, u32[]{:S(2)}) collective-permute-start(bf16[3,64,256]{2,1,0:T(8,128)(2,1)S(1)} %get-tuple-element.61), channel_id=1, source_target_pairs={{0,4},{1,5},{4,0},{5,1},{8,12},{9,13},{12,8},{13,9},{2,6},{3,7},{6... | collective-permute-start | bytes 294920 | tf_op jit(solution)/shard_map/ppermute | solution.py:232
  191.0 4.3 %collective-permute-start.14 = (bf16[3,64,256]{2,1,0:T(8,128)(2,1)S(1)}, bf16[3,64,256]{2,1,0:T(8,128)(2,1)S(1)}, u32[]{:S(2)}, u32[]{:S(2)}) collective-permute-start(bf16[3,64,256]{2,1,0:T(8,128)(2,1)S(1)} %get-tuple-element.62), channel_id=1, source_target_pairs={{0,1},{1,0},{4,5},{5,4},{8,9},{9,8},{12,13},{13,12},{2,3},{3,2},{6... | collective-permute-start | bytes 294920 | tf_op jit(solution)/shard_map/ppermute | solution.py:232
  193.1 28.7 %collective-permute-start.27 = (bf16[3,64,256]{2,1,0:T(8,128)(2,1)}, bf16[3,64,256]{2,1,0:T(8,128)(2,1)S(1)}, u32[]{:S(2)}, u32[]{:S(2)}) collective-permute-start(bf16[3,64,256]{2,1,0:T(8,128)(2,1)} %get-tuple-element.79), channel_id=1, source_target_pairs={{0,5},{1,4},{4,1},{5,0},{8,13},{9,12},{12,9},{13,8},{2,7},{3,6},{6... | collective-permute-start | bytes 294920 | tf_op jit(solution)/shard_map/ppermute | solution.py:232
  195.3 26.5 %collective-permute-start.28 = (bf16[3,64,256]{2,1,0:T(8,128)(2,1)}, bf16[3,64,256]{2,1,0:T(8,128)(2,1)S(1)}, u32[]{:S(2)}, u32[]{:S(2)}) collective-permute-start(bf16[3,64,256]{2,1,0:T(8,128)(2,1)} %get-tuple-element.80), channel_id=1, source_target_pairs={{0,4},{1,5},{4,0},{5,1},{8,12},{9,13},{12,8},{13,9},{2,6},{3,7},{6... | collective-permute-start | bytes 294920 | tf_op jit(solution)/shard_map/ppermute | solution.py:232
  195.3 26.5 %collective-permute-start.29 = (bf16[3,64,256]{2,1,0:T(8,128)(2,1)}, bf16[3,64,256]{2,1,0:T(8,128)(2,1)S(1)}, u32[]{:S(2)}, u32[]{:S(2)}) collective-permute-start(bf16[3,64,256]{2,1,0:T(8,128)(2,1)} %get-tuple-element.81), channel_id=1, source_target_pairs={{0,1},{1,0},{4,5},{5,4},{8,9},{9,8},{12,13},{13,12},{2,3},{3,2},{6... | collective-permute-start | bytes 294920 | tf_op jit(solution)/shard_map/ppermute | solution.py:232
  (30 other events, 32.8 us)
where the time goes:
time: 251 us
  Pallas kernels  143 us (57%)
  starting transfers between devices  63.4 us (25%)
  waiting for transfers between devices  25.1 us (10%)
  local copies, waits for them, and re-layouts  15.2 us (6%)
  other arithmetic  3.01 us (1%)
    pallas_call x2, Pallas kernels, local(): pl.pallas_call(functools.partial(pack_kernel, off, width, columns, order)...  75.7 us
    ppermute x32, starting transfers between devices, swap(): return lax.ppermute(x, axis, [(i, i ^ k) for i in range(size)])  63.4 us
    pallas_call x2, Pallas kernels, local(): pl.pallas_call(functools.partial(unpack_kernel, off, width, columns, slot...  51.6 us
    ppermute x32, waiting for transfers between devices, swap(): return lax.ppermute(x, axis, [(i, i ^ k) for i in range(size)])  25.1 us
    pallas_call x2, Pallas kernels, local(): pl.pallas_call(functools.partial(grads_kernel, off, width, columns, order...  15.6 us
    unnamed x93, local copies, waits for them, and re-layouts  15.2 us
  transfers between devices with their start and end apart: 32, of which 9 were waited for; matrix products, arithmetic and copies ran while one was open for 1% of the time, Pallas kernels for 42%

commit v1 on v0

--- a/solution.py
+++ b/solution.py
@@ -11,10 +11,11 @@
 HD = 128
 BLOCK = 128
 K_MAX = 3
+EARLY = 5
 TOKENS = ("seq", "rep")
 ANY = pl.BlockSpec(memory_space=pl.ANY)
 SMEM = pl.BlockSpec(memory_space=pltpu.SMEM)
-VMEM_LIMIT = 48 * 1024 * 1024
+VMEM_LIMIT = 16 * 1024 * 1024
 
 
 def run_copies(copies):
@@ -24,9 +25,9 @@
         copy.wait()
 
 
-def pack_kernel(off, width, columns, order, place, *refs):
+def pack_kernel(off, width, columns, order, waits, with_gauges, place, *refs):
     arrays, gauges = refs[0:4], refs[4:6]
-    sends, gauge_send = refs[6 : 6 + len(order)], refs[6 + len(order)]
+    sends = refs[6 + waits : 6 + waits + len(order)]
     sems, gauge_sems = refs[-2:]
     me = place[0]
     copies = []
@@ -38,16 +39,15 @@
                     arrays[a].at[:, pl.ds(start, width)], sends[at].at[a], sems.at[at, a]
                 )
             )
-    for a in range(2):
-        copies.append(
-            pltpu.make_async_copy(
-                gauges[a].at[:, pl.ds(off, width)], gauge_send.at[a], gauge_sems.at[a]
-            )
-        )
+    if with_gauges:
+        for a in range(2):
+            copies.append(pltpu.make_async_copy(gauges[a], refs[-3].at[a], gauge_sems.at[a]))
     run_copies(copies)
 
 
-def grads_kernel(off, width, columns, order, gauge_order, place, lists, counts, chosen, *refs):
+def grads_kernel(
+    off, width, columns, order, gauge_order, waits, place, lists, counts, chosen, *refs
+):
     n_tok, n_gauge = len(order), len(gauge_order)
     refs = list(refs)
 
@@ -58,6 +58,7 @@
 
     arrays, gauges = take(4), take(2)
     recvs, gauge_recvs = take(n_tok), take(n_gauge)
+    take(waits)
     outs, gauge_outs = take(n_tok + 1), take(n_gauge + 1)
     tok, gau, acc, gacc, res, in_sems, own_sems, gin_sems, gown_sems, out_sems, gout_sems = refs
     me, gauge_me = place[0], place[1]
@@ -95,7 +96,7 @@
     for at, k in enumerate(gauge_order):
         copies.append(
             pltpu.make_async_copy(
-                gauge_recvs[at],
+                gauge_recvs[at].at[:, :, pl.ds(off, width)],
                 gau.at[
                     :, pl.ds(pl.multiple_of((gauge_me ^ k) * gauge_rows, gauge_rows), gauge_rows), :
                 ],
@@ -220,10 +221,15 @@
     columns = model // total
     bf16, f32 = jnp.bfloat16, jnp.float32
     arrays = [x[0] for x in (queries, keys, values, grad_out)]
+    arrays = [pltpu.with_memory_space_constraint(x, pltpu.HBM) for x in arrays]
+    gauge_key, gauge_value = [
+        pltpu.with_memory_space_constraint(x, pltpu.HBM) for x in (gauge_key, gauge_value)
+    ]
     me = lax.axis_index(TOKENS).astype(jnp.int32)
     gauge_me = lax.axis_index("head").astype(jnp.int32)
     place = jnp.stack([me, gauge_me])
-    order = tuple(range(total - 1, 0, -1))
+    half = total // 2
+    order = tuple(k for i in range(half) for k in (total - 1 - i, half - 1 - i) if k)
     gauge_order = tuple(range(1, head_total))
     lists = (block_keys[0], block_count[0], gauge_block[0])
     params = pltpu.CompilerParams(vmem_limit_bytes=VMEM_LIMIT)
@@ -232,34 +238,36 @@
         return lax.ppermute(x, axis, [(i, i ^ k) for i in range(size)])
 
     chunks = chunks_of(columns // HD)
-    received = []
-    for off, width in chunks:
-        sends = pl.pallas_call(
-            functools.partial(pack_kernel, off, width, columns, order),
-            out_shape=[jax.ShapeDtypeStruct((4, rows, width), bf16)] * len(order)
-            + [jax.ShapeDtypeStruct((2, gauge_rows, width), bf16)],
-            in_specs=[SMEM] + [ANY] * 6,
-            out_specs=[ANY] * (len(order) + 1),
+
+    def pack(chunk, part, after, with_gauges):
+        off, width = chunk
+        shapes = [jax.ShapeDtypeStruct((4, rows, width), bf16)] * len(part)
+        if with_gauges:
+            shapes.append(jax.ShapeDtypeStruct((2, gauge_rows, columns), bf16))
+        return pl.pallas_call(
+            functools.partial(
+                pack_kernel, off, width, columns, part, len(after), with_gauges
+            ),
+            out_shape=shapes,
+            in_specs=[SMEM] + [ANY] * (6 + len(after)),
+            out_specs=[ANY] * len(shapes),
             scratch_shapes=[
-                pltpu.SemaphoreType.DMA((len(order), 4)),
+                pltpu.SemaphoreType.DMA((len(part), 4)),
                 pltpu.SemaphoreType.DMA((2,)),
             ],
+            compiler_params=params,
             name="pack",
-        )(place, *arrays, gauge_key, gauge_value)
-        gauge_send = sends[-1]
-        recvs = [swap(s, TOKENS, total, k) for s, k in zip(sends, order)]
-        gauge_recvs = [swap(gauge_send, "head", head_total, k) for k in gauge_order]
-        received.append((recvs, gauge_recvs))
-
-    outs = None
-    gauge_parts = []
-    returned = []
-    for (off, width), (recvs, gauge_recvs) in zip(chunks, received):
-        pieces = pl.pallas_call(
-            functools.partial(grads_kernel, off, width, columns, order, gauge_order),
+        )(place, *arrays, gauge_key, gauge_value, *after)
+
+    def grads(chunk, recvs, after):
+        off, width = chunk
+        return pl.pallas_call(
+            functools.partial(
+                grads_kernel, off, width, columns, order, gauge_order, len(after)
+            ),
             out_shape=[jax.ShapeDtypeStruct((3, rows, width), bf16)] * total
             + [jax.ShapeDtypeStruct((2, gauge_rows, width), f32)] * head_total,
-            in_specs=[SMEM] * 4 + [ANY] * (6 + len(order) + len(gauge_order)),
+            in_specs=[SMEM] * 4 + [ANY] * (6 + len(order) + len(gauge_order) + len(after)),
             out_specs=[ANY] * (total + head_total),
             scratch_shapes=[
                 pltpu.VMEM((4, length, width), bf16),
@@ -275,14 +283,41 @@
                 pltpu.SemaphoreType.DMA((head_total,)),
             ],
             compiler_params=params,
+            cost_estimate=pl.CostEstimate(
+                flops=10 * (K_MAX + 1) * BLOCK * length * width * 16,
+                bytes_accessed=14 * length * width,
+                transcendentals=0,
+            ),
             name="grads",
-        )(place, *lists, *arrays, gauge_key, gauge_value, *recvs, *gauge_recvs)
-        back = [pieces[0]] + [swap(p, TOKENS, total, k) for p, k in zip(pieces[1:total], order)]
+        )(place, *lists, *arrays, gauge_key, gauge_value, *recvs, *gauge_recvs, *after)
+
+    def give_back(pieces):
         gauge_back = [
             swap(p, "head", head_total, k) for p, k in zip(pieces[total + 1 :], gauge_order)
         ]
-        gauge_parts.append(functools.reduce(jnp.add, gauge_back, pieces[total]))
-        returned.append(back)
+        back = [pieces[0]] + [swap(p, TOKENS, total, k) for p, k in zip(pieces[1:total], order)]
+        return back, functools.reduce(jnp.add, gauge_back, pieces[total])
+
+    def send(packed, part):
+        return [swap(s, TOKENS, total, k) for s, k in zip(packed, part)]
+
+    *packed, gauge_send = pack(chunks[0], order, [], True)
+    gauge_recvs = [swap(gauge_send, "head", head_total, k) for k in gauge_order]
+    recvs = send(packed, order)
+    returned, gauge_parts = [], []
+    for at, chunk in enumerate(chunks):
+        after = [returned[-1][0][1]] if returned else []
+        ahead = []
+        if at + 1 < len(chunks):
+            ahead = send(pack(chunks[at + 1], order[:EARLY], recvs[:1], False), order[:EARLY])
+        pieces = grads(chunk, recvs, after)
+        if at + 1 < len(chunks):
+            late = pack(chunks[at + 1], order[EARLY:], pieces[:1], False)
+            recvs = ahead + send(late, order[EARLY:])
+        returned.append(give_back(pieces))
+    gauge_parts = [part for _, part in returned]
+    returned = [back for back, _ in returned]
+    outs = None
 
     for (off, width), back in zip(chunks, returned):
         held = 0 if outs is None else 3
@@ -294,6 +329,7 @@
             out_specs=[ANY] * 3,
             scratch_shapes=[pltpu.SemaphoreType.DMA((total, 3))],
             input_output_aliases={1 + a: a for a in range(held)},
+            compiler_params=params,
             name="unpack",
         )(place, *(outs if held else []), *back)
 

time: 251 us -> 110 us (0.44)
  Pallas kernels: 143 us -> 24.3 us
  starting transfers between devices: 63.4 us -> 37.6 us
  waiting for transfers between devices: 25.1 us -> 44.3 us
  local copies, waits for them, and re-layouts: 15.2 us -> 0.77 us
    pallas_call x4 -> x5, Pallas kernels: 91.3 us -> 21.1 us  [the longest x2 15.6 us: grads(): pl.pallas_call(functools.partial(grads_kernel, off, width, columns, order...]
    pallas_call x2, Pallas kernels: 51.6 us -> 3.23 us  [local(): pl.pallas_call(functools.partial(unpack_kernel, off, width, columns, slot...]
    ppermute x32 -> x31, starting transfers between devices: 63.4 us -> 37.6 us  [swap(): return lax.ppermute(x, axis, [(i, i ^ k) for i in range(size)])]
    ppermute x32 -> x31, waiting for transfers between devices: 25.1 us -> 44.3 us  [swap(): return lax.ppermute(x, axis, [(i, i ^ k) for i in range(size)])]
    unnamed x93 -> x7, local copies, waits for them, and re-layouts: 15.2 us -> 0.77 us
  transfers between devices with their start and end apart: 32 -> 31, of which waited for: 9 -> 14; matrix products, arithmetic and copies ran while one was open for 1% -> 0% of each run, Pallas kernels for 42% -> 20%
where the time goes in v1:
time: 110 us; the launch traced here: 109 us
  waiting for transfers between devices  44.3 us (40%)
  starting transfers between devices  37.6 us (34%)
  Pallas kernels  24.3 us (22%)
  other arithmetic  1.37 us (1%)
    ppermute x31, waiting for transfers between devices, swap(): return lax.ppermute(x, axis, [(i, i ^ k) for i in range(size)])  44.3 us
    ppermute x31, starting transfers between devices, swap(): return lax.ppermute(x, axis, [(i, i ^ k) for i in range(size)])  37.6 us
    pallas_call x2, Pallas kernels, grads(): pl.pallas_call(functools.partial(grads_kernel, off, width, columns, order...  15.6 us
    pallas_call x3, Pallas kernels, pack(): pl.pallas_call(functools.partial(pack_kernel, off, width, columns, part,...  5.55 us
    pallas_call x2, Pallas kernels, local(): pl.pallas_call(functools.partial(unpack_kernel, off, width, columns, slot...  3.23 us
  transfers between devices with their start and end apart: 31, of which 14 were waited for; matrix products, arithmetic and copies ran while one was open for 0% of the time, Pallas kernels for 20%

profile of v1, /device:TPU:0, one launch (start us, length us, event | category | flops | bytes accessed | tf_op | source)
XLA Modules:
  0.0 109.1 jit_solution(16608293111375588143)
XLA Ops:
  0.7 2.3 %pack.3 = (bf16[4,64,256]{2,1,0:T(8,128)(2,1)S(1)}, bf16[4,64,256]{2,1,0:T(8,128)(2,1)S(1)}, bf16[4,64,256]{2,1,0:T(8,128)(2,1)S(1)}, bf16[4,64,256]{2,1,0:T(8,1...) custom-call(s32[2]{0:T(128)S(1)} %pad_add_fusion.place, ...), custom_call_target="tpu_custom_call" | custom-call | tf_op jit(solution)/shard_map/pack/pallas_call | solution.py:247
  3.0 3.0 %collective-permute-start.7 = (bf16[2,256,512]{2,1,0:T(8,128)(2,1)S(1)}, bf16[2,256,512]{2,1,0:T(8,128)(2,1)S(1)}, u32[]{:S(2)}, u32[]{:S(2)}) collective-permute-start(bf16[2,256,512]{2,1,0:T(8,128)(2,1)S(1)} %get-tuple-element.53), channel_id=1, source_target_pairs={{0,2},{2,0},{1,3},{3,1},{4,6},{6,4},{5,7},{7,5},{8,10},{10,8},{9,1... | collective-permute-start | bytes 1572872 | tf_op jit(solution)/shard_map/ppermute | solution.py:238
  6.0 2.8 %collective-permute-start = (bf16[4,64,256]{2,1,0:T(8,128)(2,1)S(1)}, bf16[4,64,256]{2,1,0:T(8,128)(2,1)S(1)}, u32[]{:S(2)}, u32[]{:S(2)}) collective-permute-start(bf16[4,64,256]{2,1,0:T(8,128)(2,1)S(1)} %get-tuple-element.46), channel_id=1, source_target_pairs={{0,13},{1,12},{4,9},{5,8},{8,5},{9,4},{12,1},{13,0},{2,15},{3,14},... | collective-permute-start | bytes 393224 | tf_op jit(solution)/shard_map/ppermute | solution.py:238
  8.7 0.1 collective-permute-start.1
  8.8 1.4 %collective-permute-start.2 = (bf16[4,64,256]{2,1,0:T(8,128)(2,1)S(1)}, bf16[4,64,256]{2,1,0:T(8,128)(2,1)S(1)}, u32[]{:S(2)}, u32[]{:S(2)}) collective-permute-start(bf16[4,64,256]{2,1,0:T(8,128)(2,1)S(1)} %get-tuple-element.48), channel_id=1, source_target_pairs={{0,12},{1,13},{4,8},{5,9},{8,4},{9,5},{12,0},{13,1},{2,14},{3,15},... | collective-permute-start | bytes 393224 | tf_op jit(solution)/shard_map/ppermute | solution.py:238
  10.2 1.1 %collective-permute-start.3 = (bf16[4,64,256]{2,1,0:T(8,128)(2,1)S(1)}, bf16[4,64,256]{2,1,0:T(8,128)(2,1)S(1)}, u32[]{:S(2)}, u32[]{:S(2)}) collective-permute-start(bf16[4,64,256]{2,1,0:T(8,128)(2,1)S(1)} %get-tuple-element.49), channel_id=1, source_target_pairs={{0,4},{1,5},{4,0},{5,1},{8,12},{9,13},{12,8},{13,9},{2,6},{3,7},{6... | collective-permute-start | bytes 393224 | tf_op jit(solution)/shard_map/ppermute | solution.py:238
  11.3 2.2 %collective-permute-done.refs_6_ = bf16[4,64,256]{2,1,0:T(8,128)(2,1)S(1)} collective-permute-done((bf16[4,64,256]{2,1,0:T(8,128)(2,1)S(1)}, bf16[4,64,256]{2,1,0:T(8,128)(2,1)S(1)}, u32[]{:S(2)}, u32[]{:S(2)}) %collective-permute-start) | collective-permute-done | bytes 131104 | tf_op jit(solution)/shard_map/ppermute | solution.py:238
  13.5 2.9 %collective-permute-start.4 = (bf16[4,64,256]{2,1,0:T(8,128)(2,1)S(1)}, bf16[4,64,256]{2,1,0:T(8,128)(2,1)S(1)}, u32[]{:S(2)}, u32[]{:S(2)}) collective-permute-start(bf16[4,64,256]{2,1,0:T(8,128)(2,1)S(1)} %get-tuple-element.50), channel_id=1, source_target_pairs={{0,9},{1,8},{4,13},{5,12},{8,1},{9,0},{12,5},{13,4},{2,11},{3,10},... | collective-permute-start | bytes 393224 | tf_op jit(solution)/shard_map/ppermute | solution.py:238
  16.4 0.2 collective-permute-done.1.refs_7_
  16.6 0.8 collective-permute-start.5
  17.4 2.1 %collective-permute-done.2.refs_8_ = bf16[4,64,256]{2,1,0:T(8,128)(2,1)S(1)} collective-permute-done((bf16[4,64,256]{2,1,0:T(8,128)(2,1)S(1)}, bf16[4,64,256]{2,1,0:T(8,128)(2,1)S(1)}, u32[]{:S(2)}, u32[]{:S(2)}) %collective-permute-start.2) | collective-permute-done | bytes 131104 | tf_op jit(solution)/shard_map/ppermute | solution.py:238
  19.5 2.7 %collective-permute-start.6 = (bf16[4,64,256]{2,1,0:T(8,128)(2,1)S(1)}, bf16[4,64,256]{2,1,0:T(8,128)(2,1)S(1)}, u32[]{:S(2)}, u32[]{:S(2)}) collective-permute-start(bf16[4,64,256]{2,1,0:T(8,128)(2,1)S(1)} %get-tuple-element.52), channel_id=1, source_target_pairs={{0,8},{1,9},{4,12},{5,13},{8,0},{9,1},{12,4},{13,5},{2,10},{3,11},... | collective-permute-start | bytes 393224 | tf_op jit(solution)/shard_map/ppermute | solution.py:238
  22.4 1.8 %pack.4 = (bf16[4,64,256]{2,1,0:T(8,128)(2,1)S(1)}, bf16[4,64,256]{2,1,0:T(8,128)(2,1)S(1)}, bf16[4,64,256]{2,1,0:T(8,128)(2,1)S(1)}, bf16[4,64,256]{2,1,0:T(8,128)(2,1)S(1)}, bf16[4,64,256]{2,1,0:T(8,128)(2,1)S(1)}) custom-call(s32[2]{0:T(128)S(1)} %pad_add_fusion.place, bf16[64,4096]{1,0:T(8,128)(2,1)} %bitcast.23, bf16[64,4096]{1,0:T(8,128)(2,1)} %bitcast.28, ...), custom_call_target="tpu_custom_call" | custom-call | tf_op jit(solution)/shard_map/pack/pallas_call | solution.py:247
  24.2 1.3 %collective-permute-start.15 = (bf16[4,64,256]{2,1,0:T(8,128)(2,1)S(1)}, bf16[4,64,256]{2,1,0:T(8,128)(2,1)S(1)}, u32[]{:S(2)}, u32[]{:S(2)}) collective-permute-start(bf16[4,64,256]{2,1,0:T(8,128)(2,1)S(1)} %get-tuple-element.65), channel_id=1, source_target_pairs={{0,13},{1,12},{4,9},{5,8},{8,5},{9,4},{12,1},{13,0},{2,15},{3,14},... | collective-permute-start | bytes 393224 | tf_op jit(solution)/shard_map/ppermute | solution.py:238
  25.4 6.9 %collective-permute-done.4.refs_10_ = bf16[4,64,256]{2,1,0:T(8,128)(2,1)S(1)} collective-permute-done((bf16[4,64,256]{2,1,0:T(8,128)(2,1)S(1)}, bf16[4,64,256]{2,1,0:T(8,128)(2,1)S(1)}, u32[]{:S(2)}, u32[]{:S(2)}) %collective-permute-start.4) | collective-permute-done | bytes 131104 | tf_op jit(solution)/shard_map/ppermute | solution.py:238
  32.3 2.6 %collective-permute-start.17 = (bf16[4,64,256]{2,1,0:T(8,128)(2,1)S(1)}, bf16[4,64,256]{2,1,0:T(8,128)(2,1)S(1)}, u32[]{:S(2)}, u32[]{:S(2)}) collective-permute-start(bf16[4,64,256]{2,1,0:T(8,128)(2,1)S(1)} %get-tuple-element.67), channel_id=1, source_target_pairs={{0,12},{1,13},{4,8},{5,9},{8,4},{9,5},{12,0},{13,1},{2,14},{3,15},... | collective-permute-start | bytes 393224 | tf_op jit(solution)/shard_map/ppermute | solution.py:238
  34.9 0.5 collective-permute-done.6.refs_12_
  35.4 2.1 %collective-permute-start.19 = (bf16[4,64,256]{2,1,0:T(8,128)(2,1)S(1)}, bf16[4,64,256]{2,1,0:T(8,128)(2,1)S(1)}, u32[]{:S(2)}, u32[]{:S(2)}) collective-permute-start(bf16[4,64,256]{2,1,0:T(8,128)(2,1)S(1)} %get-tuple-element.69), channel_id=1, source_target_pairs={{0,9},{1,8},{4,13},{5,12},{8,1},{9,0},{12,5},{13,4},{2,11},{3,10},... | collective-permute-start | bytes 393224 | tf_op jit(solution)/shard_map/ppermute | solution.py:238
  37.4 0.7 copy-done
  38.1 7.8 %grads.2 = (bf16[3,64,256]{2,1,0:T(8,128)(2,1)S(1)}, bf16[3,64,256]{2,1,0:T(8,128)(2,1)S(1)}, bf16[3,64,256]{2,1,0:T(8,128)(2,1)S(1)}, bf16[3,64,256]{2,1,0:T(8,...) custom-call(s32[2]{0:T(128)S(1)} %pad_add_fusion.place, ...), custom_call_target="tpu_custom_call" | custom-call | flops 10737418240 | bytes 1835008 | tf_op jit(solution)/shard_map/grads/pallas_call | solution.py:264
  45.9 1.5 %pack.5 = (bf16[4,64,256]{2,1,0:T(8,128)(2,1)S(1)}, bf16[4,64,256]{2,1,0:T(8,128)(2,1)S(1)}) custom-call(s32[2]{0:T(128)S(1)} %pad_add_fusion.place, bf16[64,4096]{1,0:T(8,128)(2,1)} %bitcast.25, bf16[64,4096]{1,0:T(8,128)(2,1)} %bitcast.30, bf16[64,4096]{1,0:T(8,128)(2,1)} %bitcast.35, bf16[64,4096]{1,0:T(8,128)(2,1)} %bitcast.40, ...), custom_call_target="tpu_custom_call" | custom-call | tf_op jit(solution)/shard_map/pack/pallas_call | solution.py:247
  47.4 0.5 collective-permute-start.20
  47.9 0.5 collective-permute-start.21
  48.5 1.5 %collective-permute-start.8 = (bf16[3,64,256]{2,1,0:T(8,128)(2,1)S(1)}, bf16[3,64,256]{2,1,0:T(8,128)(2,1)S(1)}, u32[]{:S(2)}, u32[]{:S(2)}) collective-permute-start(bf16[3,64,256]{2,1,0:T(8,128)(2,1)S(1)} %get-tuple-element.55), channel_id=1, source_target_pairs={{0,13},{1,12},{4,9},{5,8},{8,5},{9,4},{12,1},{13,0},{2,15},{3,14},... | collective-permute-start | bytes 294920 | tf_op jit(solution)/shard_map/ppermute | solution.py:238
  50.0 0.5 collective-permute-start.29
  50.5 5.1 %collective-permute-done.8.refs_1_.refs_14_ = bf16[3,64,256]{2,1,0:T(8,128)(2,1)S(1)} collective-permute-done((bf16[3,64,256]{2,1,0:T(8,128)(2,1)S(1)}, bf16[3,64,256]{2,1,0:T(8,128)(2,1)S(1)}, u32[]{:S(2)}, u32[]{:S(2)}) %collective-permute-start.8) | collective-permute-done | bytes 98336 | tf_op jit(solution)/shard_map/ppermute | solution.py:238
  55.7 3.4 %collective-permute-done.21.refs_12_ = bf16[4,64,256]{2,1,0:T(8,128)(2,1)S(1)} collective-permute-done((bf16[4,64,256]{2,1,0:T(8,128)(2,1)S(1)}, bf16[4,64,256]{2,1,0:T(8,128)(2,1)S(1)}, u32[]{:S(2)}, u32[]{:S(2)}) %collective-permute-start.21) | collective-permute-done | bytes 131104 | tf_op jit(solution)/shard_map/ppermute | solution.py:238
  59.0 7.8 %grads.3 = (bf16[3,64,256]{2,1,0:T(8,128)(2,1)S(1)}, bf16[3,64,256]{2,1,0:T(8,128)(2,1)S(1)}, bf16[3,64,256]{2,1,0:T(8,128)(2,1)S(1)}, bf16[3,64,256]{2,1,0:T(8,...) custom-call(s32[2]{0:T(128)S(1)} %pad_add_fusion.place, ...), custom_call_target="tpu_custom_call" | custom-call | flops 10737418240 | bytes 1835008 | tf_op jit(solution)/shard_map/grads/pallas_call | solution.py:264
  66.8 0.6 collective-permute-start.30
  67.4 2.0 %collective-permute-start.9 = (bf16[3,64,256]{2,1,0:T(8,128)(2,1)S(1)}, bf16[3,64,256]{2,1,0:T(8,128)(2,1)S(1)}, u32[]{:S(2)}, u32[]{:S(2)}) collective-permute-start(bf16[3,64,256]{2,1,0:T(8,128)(2,1)S(1)} %get-tuple-element.56), channel_id=1, source_target_pairs={{0,5},{1,4},{4,1},{5,0},{8,13},{9,12},{12,9},{13,8},{2,7},{3,6},{6... | collective-permute-start | bytes 294920 | tf_op jit(solution)/shard_map/ppermute | solution.py:238
  69.4 1.9 %collective-permute-start.10 = (bf16[3,64,256]{2,1,0:T(8,128)(2,1)S(1)}, bf16[3,64,256]{2,1,0:T(8,128)(2,1)S(1)}, u32[]{:S(2)}, u32[]{:S(2)}) collective-permute-start(bf16[3,64,256]{2,1,0:T(8,128)(2,1)S(1)} %get-tuple-element.57), channel_id=1, source_target_pairs={{0,12},{1,13},{4,8},{5,9},{8,4},{9,5},{12,0},{13,1},{2,14},{3,15},... | collective-permute-start | bytes 294920 | tf_op jit(solution)/shard_map/ppermute | solution.py:238
  71.3 1.3 %collective-permute-done.9.refs_2_ = bf16[3,64,256]{2,1,0:T(8,128)(2,1)S(1)} collective-permute-done((bf16[3,64,256]{2,1,0:T(8,128)(2,1)S(1)}, bf16[3,64,256]{2,1,0:T(8,128)(2,1)S(1)}, u32[]{:S(2)}, u32[]{:S(2)}) %collective-permute-start.9) | collective-permute-done | bytes 98336 | tf_op jit(solution)/shard_map/ppermute | solution.py:238
  72.6 2.6 %collective-permute-start.12 = (bf16[3,64,256]{2,1,0:T(8,128)(2,1)S(1)}, bf16[3,64,256]{2,1,0:T(8,128)(2,1)S(1)}, u32[]{:S(2)}, u32[]{:S(2)}) collective-permute-start(bf16[3,64,256]{2,1,0:T(8,128)(2,1)S(1)} %get-tuple-element.59), channel_id=1, source_target_pairs={{0,9},{1,8},{4,13},{5,12},{8,1},{9,0},{12,5},{13,4},{2,11},{3,10},... | collective-permute-start | bytes 294920 | tf_op jit(solution)/shard_map/ppermute | solution.py:238
  75.2 1.9 %collective-permute-done.10.refs_3_ = bf16[3,64,256]{2,1,0:T(8,128)(2,1)S(1)} collective-permute-done((bf16[3,64,256]{2,1,0:T(8,128)(2,1)S(1)}, bf16[3,64,256]{2,1,0:T(8,128)(2,1)S(1)}, u32[]{:S(2)}, u32[]{:S(2)}) %collective-permute-start.10) | collective-permute-done | bytes 98336 | tf_op jit(solution)/shard_map/ppermute | solution.py:238
  77.1 3.4 %collective-permute-done.11.refs_4_ = bf16[3,64,256]{2,1,0:T(8,128)(2,1)S(1)} collective-permute-done((bf16[3,64,256]{2,1,0:T(8,128)(2,1)S(1)}, bf16[3,64,256]{2,1,0:T(8,128)(2,1)S(1)}, u32[]{:S(2)}, u32[]{:S(2)}) %collective-permute-start.11) | collective-permute-done | bytes 98336 | tf_op jit(solution)/shard_map/ppermute | solution.py:238
  80.6 1.1 collective-permute-start.22
  81.7 2.1 %collective-permute-start.23 = (bf16[3,64,256]{2,1,0:T(8,128)(2,1)S(1)}, bf16[3,64,256]{2,1,0:T(8,128)(2,1)S(1)}, u32[]{:S(2)}, u32[]{:S(2)}) collective-permute-start(bf16[3,64,256]{2,1,0:T(8,128)(2,1)S(1)} %get-tuple-element.74), channel_id=1, source_target_pairs={{0,5},{1,4},{4,1},{5,0},{8,13},{9,12},{12,9},{13,8},{2,7},{3,6},{6... | collective-permute-start | bytes 294920 | tf_op jit(solution)/shard_map/ppermute | solution.py:238
  83.8 5.6 %collective-permute-done.14.refs_7_ = bf16[3,64,256]{2,1,0:T(8,128)(2,1)S(1)} collective-permute-done((bf16[3,64,256]{2,1,0:T(8,128)(2,1)S(1)}, bf16[3,64,256]{2,1,0:T(8,128)(2,1)S(1)}, u32[]{:S(2)}, u32[]{:S(2)}) %collective-permute-start.14) | collective-permute-done | bytes 98336 | tf_op jit(solution)/shard_map/ppermute | solution.py:238
  89.4 1.9 %collective-permute-start.24 = (bf16[3,64,256]{2,1,0:T(8,128)(2,1)S(1)}, bf16[3,64,256]{2,1,0:T(8,128)(2,1)S(1)}, u32[]{:S(2)}, u32[]{:S(2)}) collective-permute-start(bf16[3,64,256]{2,1,0:T(8,128)(2,1)S(1)} %get-tuple-element.75), channel_id=1, source_target_pairs={{0,12},{1,13},{4,8},{5,9},{8,4},{9,5},{12,0},{13,1},{2,14},{3,15},... | collective-permute-start | bytes 294920 | tf_op jit(solution)/shard_map/ppermute | solution.py:238
  91.2 0.6 collective-permute-start.25
  91.8 0.9 collective-permute-start.26
  92.7 4.2 %collective-permute-done.24.refs_6_ = bf16[3,64,256]{2,1,0:T(8,128)(2,1)S(1)} collective-permute-done((bf16[3,64,256]{2,1,0:T(8,128)(2,1)S(1)}, bf16[3,64,256]{2,1,0:T(8,128)(2,1)S(1)}, u32[]{:S(2)}, u32[]{:S(2)}) %collective-permute-start.24) | collective-permute-done | bytes 98336 | tf_op jit(solution)/shard_map/ppermute | solution.py:238
  96.9 2.4 %collective-permute-done.25.refs_7_ = bf16[3,64,256]{2,1,0:T(8,128)(2,1)S(1)} collective-permute-done((bf16[3,64,256]{2,1,0:T(8,128)(2,1)S(1)}, bf16[3,64,256]{2,1,0:T(8,128)(2,1)S(1)}, u32[]{:S(2)}, u32[]{:S(2)}) %collective-permute-start.25) | collective-permute-done | bytes 98336 | tf_op jit(solution)/shard_map/ppermute | solution.py:238
  99.3 0.2 collective-permute-start.28
  99.5 1.6 %unpack.2 = (bf16[64,4096]{1,0:T(8,128)(2,1)}, bf16[64,4096]{1,0:T(8,128)(2,1)}, bf16[64,4096]{1,0:T(8,128)(2,1)}) custom-call(s32[2]{0:T(128)S(1)} %pad_add_fusion.place, bf16[3,64,256]{2,1,0:T(8,128)(2,1)S(1)} %get-tuple-element.54.refs_0_.refs_6_, bf16[3,64,256]{2,1,0:T(8,128)(2,1)S(1)} %collective-permute-done.8.refs_1_.refs_14_, ...), custom_call_target="tpu_custom_call" | custom-call | tf_op jit(solution)/shard_map/unpack/pallas_call | solution.py:325
  101.1 5.0 %collective-permute-done.28.refs_10_ = bf16[3,64,256]{2,1,0:T(8,128)(2,1)S(1)} collective-permute-done((bf16[3,64,256]{2,1,0:T(8,128)(2,1)S(1)}, bf16[3,64,256]{2,1,0:T(8,128)(2,1)S(1)}, u32[]{:S(2)}, u32[]{:S(2)}) %collective-permute-start.28) | collective-permute-done | bytes 98336 | tf_op jit(solution)/shard_map/ppermute | solution.py:238
  106.2 1.6 %unpack.3 = (bf16[64,4096]{1,0:T(8,128)(2,1)}, bf16[64,4096]{1,0:T(8,128)(2,1)}, bf16[64,4096]{1,0:T(8,128)(2,1)}) custom-call(s32[2]{0:T(128)S(1)} %pad_add_fusion.place, bf16[64,4096]{1,0:T(8,128)(2,1)} %get-tuple-element.62.refs_0_, bf16[64,4096]{1,0:T(8,128)(2,1)} %get-tuple-element.63.refs_1_, ...), custom_call_target="tpu_custom_call", output_to_operand_aliasing={{0}: (1, {}), {1}: (2, {}), {2}: (3, {})} | custom-call | tf_op jit(solution)/shard_map/unpack/pallas_call | solution.py:325
  108.0 1.1 %fusion.2 = (f32[256,512]{1,0:T(8,128)}, f32[256,512]{1,0:T(8,128)}) fusion(f32[2,256,256]{2,1,0:T(8,128)S(1)} %add.11, f32[2,256,256]{2,1,0:T(8,128)S(1)} %add.10), kind=kLoop, calls=%fused_computation.5 | loop fusion | flops 262144 | bytes 2097152 | tf_op jit(solution)/shard_map/squeeze | solution.py:337
  (32 shorter events, 0.4 us)
Async XLA Ops:
  3.0 32.4 %collective-permute-start.7 = (bf16[2,256,512]{2,1,0:T(8,128)(2,1)S(1)}, bf16[2,256,512]{2,1,0:T(8,128)(2,1)S(1)}, u32[]{:S(2)}, u32[]{:S(2)}) collective-permute-start(bf16[2,256,512]{2,1,0:T(8,128)(2,1)S(1)} %get-tuple-element.53), channel_id=1, source_target_pairs={{0,2},{2,0},{1,3},{3,1},{4,6},{6,4},{5,7},{7,5},{8,10},{10,8},{9,1... | collective-permute-start | bytes 1572872 | tf_op jit(solution)/shard_map/ppermute | solution.py:238
  6.0 7.5 %collective-permute-start = (bf16[4,64,256]{2,1,0:T(8,128)(2,1)S(1)}, bf16[4,64,256]{2,1,0:T(8,128)(2,1)S(1)}, u32[]{:S(2)}, u32[]{:S(2)}) collective-permute-start(bf16[4,64,256]{2,1,0:T(8,128)(2,1)S(1)} %get-tuple-element.46), channel_id=1, source_target_pairs={{0,13},{1,12},{4,9},{5,8},{8,5},{9,4},{12,1},{13,0},{2,15},{3,14},... | collective-permute-start | bytes 393224 | tf_op jit(solution)/shard_map/ppermute | solution.py:238
  8.7 7.9 %collective-permute-start.1 = (bf16[4,64,256]{2,1,0:T(8,128)(2,1)S(1)}, bf16[4,64,256]{2,1,0:T(8,128)(2,1)S(1)}, u32[]{:S(2)}, u32[]{:S(2)}) collective-permute-start(bf16[4,64,256]{2,1,0:T(8,128)(2,1)S(1)} %get-tuple-element.47), channel_id=1, source_target_pairs={{0,5},{1,4},{4,1},{5,0},{8,13},{9,12},{12,9},{13,8},{2,7},{3,6},{6... | collective-permute-start | bytes 393224 | tf_op jit(solution)/shard_map/ppermute | solution.py:238
  8.8 10.7 %collective-permute-start.2 = (bf16[4,64,256]{2,1,0:T(8,128)(2,1)S(1)}, bf16[4,64,256]{2,1,0:T(8,128)(2,1)S(1)}, u32[]{:S(2)}, u32[]{:S(2)}) collective-permute-start(bf16[4,64,256]{2,1,0:T(8,128)(2,1)S(1)} %get-tuple-element.48), channel_id=1, source_target_pairs={{0,12},{1,13},{4,8},{5,9},{8,4},{9,5},{12,0},{13,1},{2,14},{3,15},... | collective-permute-start | bytes 393224 | tf_op jit(solution)/shard_map/ppermute | solution.py:238
  10.2 14.0 %collective-permute-start.3 = (bf16[4,64,256]{2,1,0:T(8,128)(2,1)S(1)}, bf16[4,64,256]{2,1,0:T(8,128)(2,1)S(1)}, u32[]{:S(2)}, u32[]{:S(2)}) collective-permute-start(bf16[4,64,256]{2,1,0:T(8,128)(2,1)S(1)} %get-tuple-element.49), channel_id=1, source_target_pairs={{0,4},{1,5},{4,0},{5,1},{8,12},{9,13},{12,8},{13,9},{2,6},{3,7},{6... | collective-permute-start | bytes 393224 | tf_op jit(solution)/shard_map/ppermute | solution.py:238
  13.5 8.8 %copy-start.2 = (s32[1,4,3]{1,0,2:T(1,128)S(1)}, s32[1,4,3]{1,0,2:T(1,128)}, u32[]{:S(2)}) copy-start(s32[1,4,3]{1,0,2:T(1,128)} %param.15) | copy-start | bytes 148
  13.5 18.8 %collective-permute-start.4 = (bf16[4,64,256]{2,1,0:T(8,128)(2,1)S(1)}, bf16[4,64,256]{2,1,0:T(8,128)(2,1)S(1)}, u32[]{:S(2)}, u32[]{:S(2)}) collective-permute-start(bf16[4,64,256]{2,1,0:T(8,128)(2,1)S(1)} %get-tuple-element.50), channel_id=1, source_target_pairs={{0,9},{1,8},{4,13},{5,12},{8,1},{9,0},{12,5},{13,4},{2,11},{3,10},... | collective-permute-start | bytes 393224 | tf_op jit(solution)/shard_map/ppermute | solution.py:238
  16.6 15.7 %collective-permute-start.5 = (bf16[4,64,256]{2,1,0:T(8,128)(2,1)S(1)}, bf16[4,64,256]{2,1,0:T(8,128)(2,1)S(1)}, u32[]{:S(2)}, u32[]{:S(2)}) collective-permute-start(bf16[4,64,256]{2,1,0:T(8,128)(2,1)S(1)} %get-tuple-element.51), channel_id=1, source_target_pairs={{0,1},{1,0},{4,5},{5,4},{8,9},{9,8},{12,13},{13,12},{2,3},{3,2},{6... | collective-permute-start | bytes 393224 | tf_op jit(solution)/shard_map/ppermute | solution.py:238
  19.5 15.8 %collective-permute-start.6 = (bf16[4,64,256]{2,1,0:T(8,128)(2,1)S(1)}, bf16[4,64,256]{2,1,0:T(8,128)(2,1)S(1)}, u32[]{:S(2)}, u32[]{:S(2)}) collective-permute-start(bf16[4,64,256]{2,1,0:T(8,128)(2,1)S(1)} %get-tuple-element.52), channel_id=1, source_target_pairs={{0,8},{1,9},{4,12},{5,13},{8,0},{9,1},{12,4},{13,5},{2,10},{3,11},... | collective-permute-start | bytes 393224 | tf_op jit(solution)/shard_map/ppermute | solution.py:238
  24.2 23.3 %collective-permute-start.15 = (bf16[4,64,256]{2,1,0:T(8,128)(2,1)S(1)}, bf16[4,64,256]{2,1,0:T(8,128)(2,1)S(1)}, u32[]{:S(2)}, u32[]{:S(2)}) collective-permute-start(bf16[4,64,256]{2,1,0:T(8,128)(2,1)S(1)} %get-tuple-element.65), channel_id=1, source_target_pairs={{0,13},{1,12},{4,9},{5,8},{8,5},{9,4},{12,1},{13,0},{2,15},{3,14},... | collective-permute-start | bytes 393224 | tf_op jit(solution)/shard_map/ppermute | solution.py:238
  32.3 15.6 %collective-permute-start.16 = (bf16[4,64,256]{2,1,0:T(8,128)(2,1)S(1)}, bf16[4,64,256]{2,1,0:T(8,128)(2,1)S(1)}, u32[]{:S(2)}, u32[]{:S(2)}) collective-permute-start(bf16[4,64,256]{2,1,0:T(8,128)(2,1)S(1)} %get-tuple-element.66), channel_id=1, source_target_pairs={{0,5},{1,4},{4,1},{5,0},{8,13},{9,12},{12,9},{13,8},{2,7},{3,6},{6... | collective-permute-start | bytes 393224 | tf_op jit(solution)/shard_map/ppermute | solution.py:238
  32.3 16.2 %collective-permute-start.17 = (bf16[4,64,256]{2,1,0:T(8,128)(2,1)S(1)}, bf16[4,64,256]{2,1,0:T(8,128)(2,1)S(1)}, u32[]{:S(2)}, u32[]{:S(2)}) collective-permute-start(bf16[4,64,256]{2,1,0:T(8,128)(2,1)S(1)} %get-tuple-element.67), channel_id=1, source_target_pairs={{0,12},{1,13},{4,8},{5,9},{8,4},{9,5},{12,0},{13,1},{2,14},{3,15},... | collective-permute-start | bytes 393224 | tf_op jit(solution)/shard_map/ppermute | solution.py:238
  35.4 14.6 %collective-permute-start.18 = (bf16[4,64,256]{2,1,0:T(8,128)(2,1)S(1)}, bf16[4,64,256]{2,1,0:T(8,128)(2,1)S(1)}, u32[]{:S(2)}, u32[]{:S(2)}) collective-permute-start(bf16[4,64,256]{2,1,0:T(8,128)(2,1)S(1)} %get-tuple-element.68), channel_id=1, source_target_pairs={{0,4},{1,5},{4,0},{5,1},{8,12},{9,13},{12,8},{13,9},{2,6},{3,7},{6... | collective-permute-start | bytes 393224 | tf_op jit(solution)/shard_map/ppermute | solution.py:238
  35.4 15.1 %collective-permute-start.19 = (bf16[4,64,256]{2,1,0:T(8,128)(2,1)S(1)}, bf16[4,64,256]{2,1,0:T(8,128)(2,1)S(1)}, u32[]{:S(2)}, u32[]{:S(2)}) collective-permute-start(bf16[4,64,256]{2,1,0:T(8,128)(2,1)S(1)} %get-tuple-element.69), channel_id=1, source_target_pairs={{0,9},{1,8},{4,13},{5,12},{8,1},{9,0},{12,5},{13,4},{2,11},{3,10},... | collective-permute-start | bytes 393224 | tf_op jit(solution)/shard_map/ppermute | solution.py:238
  37.4 0.7 copy-start
  37.4 0.7 copy-start.1
  47.4 8.2 %collective-permute-start.20 = (bf16[4,64,256]{2,1,0:T(8,128)(2,1)S(1)}, bf16[4,64,256]{2,1,0:T(8,128)(2,1)S(1)}, u32[]{:S(2)}, u32[]{:S(2)}) collective-permute-start(bf16[4,64,256]{2,1,0:T(8,128)(2,1)S(1)} %get-tuple-element.70), channel_id=1, source_target_pairs={{0,1},{1,0},{4,5},{5,4},{8,9},{9,8},{12,13},{13,12},{2,3},{3,2},{6... | collective-permute-start | bytes 393224 | tf_op jit(solution)/shard_map/ppermute | solution.py:238
  47.9 11.1 %collective-permute-start.21 = (bf16[4,64,256]{2,1,0:T(8,128)(2,1)S(1)}, bf16[4,64,256]{2,1,0:T(8,128)(2,1)S(1)}, u32[]{:S(2)}, u32[]{:S(2)}) collective-permute-start(bf16[4,64,256]{2,1,0:T(8,128)(2,1)S(1)} %get-tuple-element.71), channel_id=1, source_target_pairs={{0,8},{1,9},{4,12},{5,13},{8,0},{9,1},{12,4},{13,5},{2,10},{3,11},... | collective-permute-start | bytes 393224 | tf_op jit(solution)/shard_map/ppermute | solution.py:238
  48.5 7.2 %collective-permute-start.8 = (bf16[3,64,256]{2,1,0:T(8,128)(2,1)S(1)}, bf16[3,64,256]{2,1,0:T(8,128)(2,1)S(1)}, u32[]{:S(2)}, u32[]{:S(2)}) collective-permute-start(bf16[3,64,256]{2,1,0:T(8,128)(2,1)S(1)} %get-tuple-element.55), channel_id=1, source_target_pairs={{0,13},{1,12},{4,9},{5,8},{8,5},{9,4},{12,1},{13,0},{2,15},{3,14},... | collective-permute-start | bytes 294920 | tf_op jit(solution)/shard_map/ppermute | solution.py:238
  50.0 57.8 %collective-permute-start.29 = (f32[2,256,256]{2,1,0:T(8,128)S(1)}, f32[2,256,256]{2,1,0:T(8,128)S(1)}, u32[]{:S(2)}, u32[]{:S(2)}) collective-permute-start(f32[2,256,256]{2,1,0:T(8,128)S(1)} %get-tuple-element.84), channel_id=1, source_target_pairs={{0,2},{2,0},{1,3},{3,1},{4,6},{6,4},{5,7},{7,5},{8,10},{10,8},{9,1... | collective-permute-start | bytes 1572872 | tf_op jit(solution)/shard_map/ppermute | solution.py:238
  66.8 41.1 %collective-permute-start.30 = (f32[2,256,256]{2,1,0:T(8,128)S(1)}, f32[2,256,256]{2,1,0:T(8,128)S(1)}, u32[]{:S(2)}, u32[]{:S(2)}) collective-permute-start(f32[2,256,256]{2,1,0:T(8,128)S(1)} %get-tuple-element.86), channel_id=1, source_target_pairs={{0,2},{2,0},{1,3},{3,1},{4,6},{6,4},{5,7},{7,5},{8,10},{10,8},{9,1... | collective-permute-start | bytes 1572872 | tf_op jit(solution)/shard_map/ppermute | solution.py:238
  67.4 5.2 %collective-permute-start.9 = (bf16[3,64,256]{2,1,0:T(8,128)(2,1)S(1)}, bf16[3,64,256]{2,1,0:T(8,128)(2,1)S(1)}, u32[]{:S(2)}, u32[]{:S(2)}) collective-permute-start(bf16[3,64,256]{2,1,0:T(8,128)(2,1)S(1)} %get-tuple-element.56), channel_id=1, source_target_pairs={{0,5},{1,4},{4,1},{5,0},{8,13},{9,12},{12,9},{13,8},{2,7},{3,6},{6... | collective-permute-start | bytes 294920 | tf_op jit(solution)/shard_map/ppermute | solution.py:238
  69.4 7.7 %collective-permute-start.10 = (bf16[3,64,256]{2,1,0:T(8,128)(2,1)S(1)}, bf16[3,64,256]{2,1,0:T(8,128)(2,1)S(1)}, u32[]{:S(2)}, u32[]{:S(2)}) collective-permute-start(bf16[3,64,256]{2,1,0:T(8,128)(2,1)S(1)} %get-tuple-element.57), channel_id=1, source_target_pairs={{0,12},{1,13},{4,8},{5,9},{8,4},{9,5},{12,0},{13,1},{2,14},{3,15},... | collective-permute-start | bytes 294920 | tf_op jit(solution)/shard_map/ppermute | solution.py:238
  71.3 9.2 %collective-permute-start.11 = (bf16[3,64,256]{2,1,0:T(8,128)(2,1)S(1)}, bf16[3,64,256]{2,1,0:T(8,128)(2,1)S(1)}, u32[]{:S(2)}, u32[]{:S(2)}) collective-permute-start(bf16[3,64,256]{2,1,0:T(8,128)(2,1)S(1)} %get-tuple-element.58), channel_id=1, source_target_pairs={{0,4},{1,5},{4,0},{5,1},{8,12},{9,13},{12,8},{13,9},{2,6},{3,7},{6... | collective-permute-start | bytes 294920 | tf_op jit(solution)/shard_map/ppermute | solution.py:238
  72.6 7.9 %collective-permute-start.12 = (bf16[3,64,256]{2,1,0:T(8,128)(2,1)S(1)}, bf16[3,64,256]{2,1,0:T(8,128)(2,1)S(1)}, u32[]{:S(2)}, u32[]{:S(2)}) collective-permute-start(bf16[3,64,256]{2,1,0:T(8,128)(2,1)S(1)} %get-tuple-element.59), channel_id=1, source_target_pairs={{0,9},{1,8},{4,13},{5,12},{8,1},{9,0},{12,5},{13,4},{2,11},{3,10},... | collective-permute-start | bytes 294920 | tf_op jit(solution)/shard_map/ppermute | solution.py:238
  77.1 4.5 %collective-permute-start.13 = (bf16[3,64,256]{2,1,0:T(8,128)(2,1)S(1)}, bf16[3,64,256]{2,1,0:T(8,128)(2,1)S(1)}, u32[]{:S(2)}, u32[]{:S(2)}) collective-permute-start(bf16[3,64,256]{2,1,0:T(8,128)(2,1)S(1)} %get-tuple-element.60), channel_id=1, source_target_pairs={{0,1},{1,0},{4,5},{5,4},{8,9},{9,8},{12,13},{13,12},{2,3},{3,2},{6... | collective-permute-start | bytes 294920 | tf_op jit(solution)/shard_map/ppermute | solution.py:238
  80.5 8.8 %collective-permute-start.14 = (bf16[3,64,256]{2,1,0:T(8,128)(2,1)S(1)}, bf16[3,64,256]{2,1,0:T(8,128)(2,1)S(1)}, u32[]{:S(2)}, u32[]{:S(2)}) collective-permute-start(bf16[3,64,256]{2,1,0:T(8,128)(2,1)S(1)} %get-tuple-element.61), channel_id=1, source_target_pairs={{0,8},{1,9},{4,12},{5,13},{8,0},{9,1},{12,4},{13,5},{2,10},{3,11},... | collective-permute-start | bytes 294920 | tf_op jit(solution)/shard_map/ppermute | solution.py:238
  80.6 10.7 %collective-permute-start.22 = (bf16[3,64,256]{2,1,0:T(8,128)(2,1)S(1)}, bf16[3,64,256]{2,1,0:T(8,128)(2,1)S(1)}, u32[]{:S(2)}, u32[]{:S(2)}) collective-permute-start(bf16[3,64,256]{2,1,0:T(8,128)(2,1)S(1)} %get-tuple-element.73), channel_id=1, source_target_pairs={{0,13},{1,12},{4,9},{5,8},{8,5},{9,4},{12,1},{13,0},{2,15},{3,14},... | collective-permute-start | bytes 294920 | tf_op jit(solution)/shard_map/ppermute | solution.py:238
  81.7 10.2 %collective-permute-start.23 = (bf16[3,64,256]{2,1,0:T(8,128)(2,1)S(1)}, bf16[3,64,256]{2,1,0:T(8,128)(2,1)S(1)}, u32[]{:S(2)}, u32[]{:S(2)}) collective-permute-start(bf16[3,64,256]{2,1,0:T(8,128)(2,1)S(1)} %get-tuple-element.74), channel_id=1, source_target_pairs={{0,5},{1,4},{4,1},{5,0},{8,13},{9,12},{12,9},{13,8},{2,7},{3,6},{6... | collective-permute-start | bytes 294920 | tf_op jit(solution)/shard_map/ppermute | solution.py:238
  89.4 7.5 %collective-permute-start.24 = (bf16[3,64,256]{2,1,0:T(8,128)(2,1)S(1)}, bf16[3,64,256]{2,1,0:T(8,128)(2,1)S(1)}, u32[]{:S(2)}, u32[]{:S(2)}) collective-permute-start(bf16[3,64,256]{2,1,0:T(8,128)(2,1)S(1)} %get-tuple-element.75), channel_id=1, source_target_pairs={{0,12},{1,13},{4,8},{5,9},{8,4},{9,5},{12,0},{13,1},{2,14},{3,15},... | collective-permute-start | bytes 294920 | tf_op jit(solution)/shard_map/ppermute | solution.py:238
  91.2 8.0 %collective-permute-start.25 = (bf16[3,64,256]{2,1,0:T(8,128)(2,1)S(1)}, bf16[3,64,256]{2,1,0:T(8,128)(2,1)S(1)}, u32[]{:S(2)}, u32[]{:S(2)}) collective-permute-start(bf16[3,64,256]{2,1,0:T(8,128)(2,1)S(1)} %get-tuple-element.76), channel_id=1, source_target_pairs={{0,4},{1,5},{4,0},{5,1},{8,12},{9,13},{12,8},{13,9},{2,6},{3,7},{6... | collective-permute-start | bytes 294920 | tf_op jit(solution)/shard_map/ppermute | solution.py:238
  91.8 9.3 %collective-permute-start.26 = (bf16[3,64,256]{2,1,0:T(8,128)(2,1)S(1)}, bf16[3,64,256]{2,1,0:T(8,128)(2,1)S(1)}, u32[]{:S(2)}, u32[]{:S(2)}) collective-permute-start(bf16[3,64,256]{2,1,0:T(8,128)(2,1)S(1)} %get-tuple-element.77), channel_id=1, source_target_pairs={{0,9},{1,8},{4,13},{5,12},{8,1},{9,0},{12,5},{13,4},{2,11},{3,10},... | collective-permute-start | bytes 294920 | tf_op jit(solution)/shard_map/ppermute | solution.py:238
  96.9 4.2 %collective-permute-start.27 = (bf16[3,64,256]{2,1,0:T(8,128)(2,1)S(1)}, bf16[3,64,256]{2,1,0:T(8,128)(2,1)S(1)}, u32[]{:S(2)}, u32[]{:S(2)}) collective-permute-start(bf16[3,64,256]{2,1,0:T(8,128)(2,1)S(1)} %get-tuple-element.78), channel_id=1, source_target_pairs={{0,1},{1,0},{4,5},{5,4},{8,9},{9,8},{12,13},{13,12},{2,3},{3,2},{6... | collective-permute-start | bytes 294920 | tf_op jit(solution)/shard_map/ppermute | solution.py:238
  99.3 6.9 %collective-permute-start.28 = (bf16[3,64,256]{2,1,0:T(8,128)(2,1)S(1)}, bf16[3,64,256]{2,1,0:T(8,128)(2,1)S(1)}, u32[]{:S(2)}, u32[]{:S(2)}) collective-permute-start(bf16[3,64,256]{2,1,0:T(8,128)(2,1)S(1)} %get-tuple-element.79), channel_id=1, source_target_pairs={{0,8},{1,9},{4,12},{5,13},{8,0},{9,1},{12,4},{13,5},{2,10},{3,11},... | collective-permute-start | bytes 294920 | tf_op jit(solution)/shard_map/ppermute | solution.py:238

commit v2 on v1

--- a/solution.py
+++ b/solution.py
@@ -11,7 +11,7 @@
 HD = 128
 BLOCK = 128
 K_MAX = 3
-EARLY = 5
+AHEAD = 0
 TOKENS = ("seq", "rep")
 ANY = pl.BlockSpec(memory_space=pl.ANY)
 SMEM = pl.BlockSpec(memory_space=pltpu.SMEM)
@@ -46,7 +46,7 @@
 
 
 def grads_kernel(
-    off, width, columns, order, gauge_order, waits, place, lists, counts, chosen, *refs
+    off, width, columns, order, gauge_order, waits, held, place, lists, counts, chosen, *refs
 ):
     n_tok, n_gauge = len(order), len(gauge_order)
     refs = list(refs)
@@ -58,7 +58,7 @@
 
     arrays, gauges = take(4), take(2)
     recvs, gauge_recvs = take(n_tok), take(n_gauge)
-    take(waits)
+    take(waits + held)
     outs, gauge_outs = take(n_tok + 1), take(n_gauge + 1)
     tok, gau, acc, gacc, res, in_sems, own_sems, gin_sems, gown_sems, out_sems, gout_sems = refs
     me, gauge_me = place[0], place[1]
@@ -116,8 +116,8 @@
             pl.ds(pl.multiple_of(lists[n, j] * BLOCK, BLOCK), BLOCK) for j in range(K_MAX)
         ]
         gslot = pl.ds(pl.multiple_of(chosen[n] * BLOCK, BLOCK), BLOCK)
-        row = lax.broadcasted_iota(jnp.int32, ((K_MAX + 1) * BLOCK, BLOCK), 0)
-        allowed = (row < counts[n] * BLOCK) | (row >= K_MAX * BLOCK)
+        third = jnp.where(counts[n] == K_MAX, 0.0, -jnp.inf).astype(jnp.float32)
+        base, listed = (K_MAX - 1) * BLOCK, K_MAX * BLOCK
         for h in range(width // HD):
             lanes = slice(h * HD, (h + 1) * HD)
             q = tok[0, here, lanes]
@@ -125,29 +125,32 @@
             k = jnp.concatenate([tok[1, s, lanes] for s in slots] + [gau[0, gslot, lanes]], axis=0)
             v = jnp.concatenate([tok[2, s, lanes] for s in slots] + [gau[1, gslot, lanes]], axis=0)
             last = (((1,), (1,)), ((), ()))
-            scores = lax.dot_general(k, q, last, preferred_element_type=jnp.float32) * scaling
-            scores = jnp.where(allowed, scores, -jnp.inf)
-            weights = jnp.exp(scores - jnp.max(scores, axis=0, keepdims=True))
+            scores = lax.dot_general(k, q, last, preferred_element_type=jnp.float32)
+            grad_probs = lax.dot_general(v, g, last, preferred_element_type=jnp.float32)
+            scores = jnp.concatenate(
+                [scores[:base], scores[base:listed] + third, scores[listed:]], axis=0
+            )
+            top = jnp.max(scores, axis=0, keepdims=True)
+            weights = jnp.exp2((scores - top) * (scaling * math.log2(math.e)))
             inverse = 1.0 / jnp.sum(weights, axis=0, keepdims=True)
+            delta = jnp.sum(weights * grad_probs, axis=0, keepdims=True) * inverse
             probs = weights * inverse
-            grad_probs = lax.dot_general(v, g, last, preferred_element_type=jnp.float32)
-            delta = jnp.sum(probs * grad_probs, axis=0, keepdims=True)
-            grad_scores = (probs * (grad_probs - delta) * scaling).astype(jnp.bfloat16)
+            grad_scores = (probs * ((grad_probs - delta) * scaling)).astype(jnp.bfloat16)
             probs_low = probs.astype(jnp.bfloat16)
+            dk = jnp.dot(grad_scores, q, preferred_element_type=jnp.float32)
+            dv = jnp.dot(probs_low, g, preferred_element_type=jnp.float32)
             res[0, here, lanes] = lax.dot_general(
                 grad_scores, k, (((0,), (0,)), ((), ())), preferred_element_type=jnp.float32
             ).astype(jnp.bfloat16)
-            dk = jnp.dot(grad_scores, q, preferred_element_type=jnp.float32)
-            dv = jnp.dot(probs_low, g, preferred_element_type=jnp.float32)
             for j in range(K_MAX):
                 part = slice(j * BLOCK, (j + 1) * BLOCK)
                 acc[0, slots[j], lanes] += dk[part]
                 acc[1, slots[j], lanes] += dv[part]
-            gacc[0, gslot, lanes] += dk[K_MAX * BLOCK :]
-            gacc[1, gslot, lanes] += dv[K_MAX * BLOCK :]
+            gacc[0, gslot, lanes] += dk[listed:]
+            gacc[1, gslot, lanes] += dv[listed:]
         return carry
 
-    lax.fori_loop(0, length // BLOCK, block, 0)
+    lax.fori_loop(0, length // BLOCK, block, 0, unroll=4)
 
     copies = []
     for at, k in enumerate((0,) + tuple(gauge_order)):
@@ -165,12 +168,12 @@
     res[1] = acc[0].astype(jnp.bfloat16)
     res[2] = acc[1].astype(jnp.bfloat16)
     token_copies = []
-    for at, k in enumerate((0,) + tuple(order)):
+    for k in range(n_tok + 1):
         token_copies.append(
             pltpu.make_async_copy(
                 res.at[:, pl.ds(pl.multiple_of((me ^ k) * rows, rows), rows), :],
-                outs[at],
-                out_sems.at[at],
+                outs[k].at[:, :, pl.ds(off, width)],
+                out_sems.at[k],
             )
         )
     run_copies(token_copies)
@@ -178,18 +181,16 @@
         copy.wait()
 
 
-def unpack_kernel(off, width, columns, order, held, place, *refs):
-    parts = refs[held : held + len(order)]
-    outs = refs[held + len(order) : held + len(order) + 3]
-    sems = refs[-1]
+def unpack_kernel(columns, order, place, *refs):
+    outs, sems = refs[-4:-1], refs[-1]
     me = place[0]
     copies = []
     for at, k in enumerate(order):
-        start = pl.multiple_of((me ^ k) * columns + off, HD)
+        start = pl.multiple_of((me ^ k) * columns, HD)
         for a in range(3):
             copies.append(
                 pltpu.make_async_copy(
-                    parts[at].at[a], outs[a].at[:, pl.ds(start, width)], sems.at[at, a]
+                    refs[at].at[a], outs[a].at[:, pl.ds(start, columns)], sems.at[at, a]
                 )
             )
     run_copies(copies)
@@ -259,15 +260,16 @@
             name="pack",
         )(place, *arrays, gauge_key, gauge_value, *after)
 
-    def grads(chunk, recvs, after):
+    def grads(chunk, recvs, order, after, held):
         off, width = chunk
         return pl.pallas_call(
             functools.partial(
-                grads_kernel, off, width, columns, order, gauge_order, len(after)
+                grads_kernel, off, width, columns, order, gauge_order, len(after), len(held)
             ),
-            out_shape=[jax.ShapeDtypeStruct((3, rows, width), bf16)] * total
+            out_shape=[jax.ShapeDtypeStruct((3, rows, columns), bf16)] * total
             + [jax.ShapeDtypeStruct((2, gauge_rows, width), f32)] * head_total,
-            in_specs=[SMEM] * 4 + [ANY] * (6 + len(order) + len(gauge_order) + len(after)),
+            in_specs=[SMEM] * 4
+            + [ANY] * (6 + len(order) + len(gauge_order) + len(after) + len(held)),
             out_specs=[ANY] * (total + head_total),
             scratch_shapes=[
                 pltpu.VMEM((4, length, width), bf16),
@@ -288,15 +290,11 @@
                 bytes_accessed=14 * length * width,
                 transcendentals=0,
             ),
+            input_output_aliases={
+                10 + len(order) + len(gauge_order) + len(after) + i: i for i in range(len(held))
+            },
             name="grads",
-        )(place, *lists, *arrays, gauge_key, gauge_value, *recvs, *gauge_recvs, *after)
-
-    def give_back(pieces):
-        gauge_back = [
-            swap(p, "head", head_total, k) for p, k in zip(pieces[total + 1 :], gauge_order)
-        ]
-        back = [pieces[0]] + [swap(p, TOKENS, total, k) for p, k in zip(pieces[1:total], order)]
-        return back, functools.reduce(jnp.add, gauge_back, pieces[total])
+        )(place, *lists, *arrays, gauge_key, gauge_value, *recvs, *gauge_recvs, *after, *held)
 
     def send(packed, part):
         return [swap(s, TOKENS, total, k) for s, k in zip(packed, part)]
@@ -304,37 +302,31 @@
     *packed, gauge_send = pack(chunks[0], order, [], True)
     gauge_recvs = [swap(gauge_send, "head", head_total, k) for k in gauge_order]
     recvs = send(packed, order)
-    returned, gauge_parts = [], []
+    pieces, gauge_sums = [], []
     for at, chunk in enumerate(chunks):
-        after = [returned[-1][0][1]] if returned else []
         ahead = []
         if at + 1 < len(chunks):
-            ahead = send(pack(chunks[at + 1], order[:EARLY], recvs[:1], False), order[:EARLY])
-        pieces = grads(chunk, recvs, after)
-        if at + 1 < len(chunks):
-            late = pack(chunks[at + 1], order[EARLY:], pieces[:1], False)
-            recvs = ahead + send(late, order[EARLY:])
-        returned.append(give_back(pieces))
-    gauge_parts = [part for _, part in returned]
-    returned = [back for back, _ in returned]
-    outs = None
-
-    for (off, width), back in zip(chunks, returned):
-        held = 0 if outs is None else 3
-        slots = (0,) + order
-        outs = pl.pallas_call(
-            functools.partial(unpack_kernel, off, width, columns, slots, held),
-            out_shape=[jax.ShapeDtypeStruct((rows, model), bf16)] * 3,
-            in_specs=[SMEM] + [ANY] * (held + total),
-            out_specs=[ANY] * 3,
-            scratch_shapes=[pltpu.SemaphoreType.DMA((total, 3))],
-            input_output_aliases={1 + a: a for a in range(held)},
-            compiler_params=params,
-            name="unpack",
-        )(place, *(outs if held else []), *back)
-
-    gauge_grads = jnp.concatenate(gauge_parts, axis=2)
-    return (outs[0][None], outs[1][None], outs[2][None], gauge_grads[0], gauge_grads[1])
+            ahead = send(pack(chunks[at + 1], order, recvs[:1], False), order)
+        out = grads(chunk, recvs, order, ahead[:AHEAD], pieces)
+        pieces = out[:total]
+        gauge_back = [
+            swap(x, "head", head_total, k) for x, k in zip(out[total + 1 :], gauge_order)
+        ]
+        gauge_sums.append(functools.reduce(jnp.add, gauge_back, out[total]))
+        recvs = ahead
+    back = [pieces[0]] + [swap(pieces[k], TOKENS, total, k) for k in order]
+    gauge_sum = jnp.concatenate(gauge_sums, axis=2)
+    gauge_grads = [gauge_sum[0], gauge_sum[1]]
+    outs = pl.pallas_call(
+        functools.partial(unpack_kernel, columns, (0, *order)),
+        out_shape=[jax.ShapeDtypeStruct((rows, model), bf16)] * 3,
+        in_specs=[SMEM] + [ANY] * (total + 2),
+        out_specs=[ANY] * 3,
+        scratch_shapes=[pltpu.SemaphoreType.DMA((total, 3))],
+        compiler_params=params,
+        name="unpack",
+    )(place, *back, *gauge_grads)
+    return (outs[0][None], outs[1][None], outs[2][None], *gauge_grads)
 
 
 def solution(mesh):

time: 110 us -> 99 us (0.900)
  Pallas kernels: 24.3 us -> 17.7 us
  waiting for transfers between devices: 44.3 us -> 42.7 us
  starting transfers between devices: 37.6 us -> 36.3 us
    pallas_call x2, Pallas kernels: 15.6 us -> 11.7 us  [grads(): pl.pallas_call(functools.partial(grads_kernel, off, width, columns, order...]
    ppermute x31 -> x24, waiting for transfers between devices: 44.3 us -> 42.7 us  [swap(): return lax.ppermute(x, axis, [(i, i ^ k) for i in range(size)])]
    pallas_call x2 -> x1, Pallas kernels: 3.23 us -> 1.87 us  [local(): pl.pallas_call(functools.partial(unpack_kernel, columns, (0, *order)), ou...]
    pallas_call x3 -> x2, Pallas kernels: 5.55 us -> 4.2 us  [pack(): pl.pallas_call(functools.partial(pack_kernel, off, width, columns, part,...]
    ppermute x31 -> x24, starting transfers between devices: 37.6 us -> 36.3 us  [swap(): return lax.ppermute(x, axis, [(i, i ^ k) for i in range(size)])]
  transfers between devices with their start and end apart: 31 -> 24, of which waited for: 14 -> 13; matrix products, arithmetic and copies ran while one was open for 0% -> 0% of each run, Pallas kernels for 20% -> 14%
where the time goes in v2:
time: 99 us; the launch traced here: 98.6 us
  waiting for transfers between devices  42.7 us (43%)
  starting transfers between devices  36.3 us (37%)
  Pallas kernels  17.7 us (18%)
    ppermute x24, waiting for transfers between devices, swap(): return lax.ppermute(x, axis, [(i, i ^ k) for i in range(size)])  42.7 us
    ppermute x24, starting transfers between devices, swap(): return lax.ppermute(x, axis, [(i, i ^ k) for i in range(size)])  36.3 us
    pallas_call x2, Pallas kernels, grads(): pl.pallas_call(functools.partial(grads_kernel, off, width, columns, order...  11.7 us
    pallas_call x2, Pallas kernels, pack(): pl.pallas_call(functools.partial(pack_kernel, off, width, columns, part,...  4.2 us
  transfers between devices with their start and end apart: 24, of which 13 were waited for; matrix products, arithmetic and copies ran while one was open for 0% of the time, Pallas kernels for 14%

profile of v2, /device:TPU:0, one launch (start us, length us, event | category | flops | bytes accessed | tf_op | source)
XLA Modules:
  0.0 98.6 jit_solution(10474474046288621203)
XLA Ops:
  0.6 0.1 pad_add_fusion.place
  0.7 2.3 %pack.2 = (bf16[4,64,256]{2,1,0:T(8,128)(2,1)S(1)}, bf16[4,64,256]{2,1,0:T(8,128)(2,1)S(1)}, bf16[4,64,256]{2,1,0:T(8,128)(2,1)S(1)}, bf16[4,64,256]{2,1,0:T(8,1...) custom-call(s32[2]{0:T(128)S(1)} %pad_add_fusion.place, ...), custom_call_target="tpu_custom_call" | custom-call | tf_op jit(solution)/shard_map/pack/pallas_call | solution.py:248
  3.0 3.0 %collective-permute-start.8 = (bf16[2,256,512]{2,1,0:T(8,128)(2,1)S(1)}, bf16[2,256,512]{2,1,0:T(8,128)(2,1)S(1)}, u32[]{:S(2)}, u32[]{:S(2)}) collective-permute-start(bf16[2,256,512]{2,1,0:T(8,128)(2,1)S(1)} %get-tuple-element.51), channel_id=1, source_target_pairs={{0,2},{2,0},{1,3},{3,1},{4,6},{6,4},{5,7},{7,5},{8,10},{10,8},{9,1... | collective-permute-start | bytes 1572872 | tf_op jit(solution)/shard_map/ppermute | solution.py:239
  6.0 2.8 %collective-permute-start = (bf16[4,64,256]{2,1,0:T(8,128)(2,1)S(1)}, bf16[4,64,256]{2,1,0:T(8,128)(2,1)S(1)}, u32[]{:S(2)}, u32[]{:S(2)}) collective-permute-start(bf16[4,64,256]{2,1,0:T(8,128)(2,1)S(1)} %get-tuple-element.43), channel_id=1, source_target_pairs={{0,13},{1,12},{4,9},{5,8},{8,5},{9,4},{12,1},{13,0},{2,15},{3,14},... | collective-permute-start | bytes 393224 | tf_op jit(solution)/shard_map/ppermute | solution.py:239
  8.7 0.9 collective-permute-start.10
  9.6 3.5 %collective-permute-start.12 = (bf16[4,64,256]{2,1,0:T(8,128)(2,1)S(1)}, bf16[4,64,256]{2,1,0:T(8,128)(2,1)S(1)}, u32[]{:S(2)}, u32[]{:S(2)}) collective-permute-start(bf16[4,64,256]{2,1,0:T(8,128)(2,1)S(1)} %get-tuple-element.55), channel_id=1, source_target_pairs={{0,9},{1,8},{4,13},{5,12},{8,1},{9,0},{12,5},{13,4},{2,11},{3,10},... | collective-permute-start | bytes 393224 | tf_op jit(solution)/shard_map/ppermute | solution.py:239
  13.2 0.3 collective-permute-done.refs_6_
  13.5 0.1 collective-permute-start.13
  13.6 1.9 %pack.3 = (bf16[4,64,256]{2,1,0:T(8,128)(2,1)S(1)}, bf16[4,64,256]{2,1,0:T(8,128)(2,1)S(1)}, bf16[4,64,256]{2,1,0:T(8,128)(2,1)S(1)}, bf16[4,64,256]{2,1,0:T(8,1...) custom-call(s32[2]{0:T(128)S(1)} %pad_add_fusion.place, ...), custom_call_target="tpu_custom_call" | custom-call | tf_op jit(solution)/shard_map/pack/pallas_call | solution.py:248
  15.6 1.5 %collective-permute-done.10.refs_8_ = bf16[4,64,256]{2,1,0:T(8,128)(2,1)S(1)} collective-permute-done((bf16[4,64,256]{2,1,0:T(8,128)(2,1)S(1)}, bf16[4,64,256]{2,1,0:T(8,128)(2,1)S(1)}, u32[]{:S(2)}, u32[]{:S(2)}) %collective-permute-start.10) | collective-permute-done | bytes 131104 | tf_op jit(solution)/shard_map/ppermute | solution.py:239
  17.0 8.1 %collective-permute-start.14 = (bf16[4,64,256]{2,1,0:T(8,128)(2,1)S(1)}, bf16[4,64,256]{2,1,0:T(8,128)(2,1)S(1)}, u32[]{:S(2)}, u32[]{:S(2)}) collective-permute-start(bf16[4,64,256]{2,1,0:T(8,128)(2,1)S(1)} %get-tuple-element.57), channel_id=1, source_target_pairs={{0,8},{1,9},{4,12},{5,13},{8,0},{9,1},{12,4},{13,5},{2,10},{3,11},... | collective-permute-start | bytes 393224 | tf_op jit(solution)/shard_map/ppermute | solution.py:239
  25.1 0.0 collective-permute-done.11.refs_9_
  25.1 0.0 collective-permute-start.9
  25.1 1.6 %collective-permute-done.12.refs_10_ = bf16[4,64,256]{2,1,0:T(8,128)(2,1)S(1)} collective-permute-done((bf16[4,64,256]{2,1,0:T(8,128)(2,1)S(1)}, bf16[4,64,256]{2,1,0:T(8,128)(2,1)S(1)}, u32[]{:S(2)}, u32[]{:S(2)}) %collective-permute-start.12) | collective-permute-done | bytes 131104 | tf_op jit(solution)/shard_map/ppermute | solution.py:239
  26.7 1.8 %collective-permute-start.1 = (bf16[4,64,256]{2,1,0:T(8,128)(2,1)S(1)}, bf16[4,64,256]{2,1,0:T(8,128)(2,1)S(1)}, u32[]{:S(2)}, u32[]{:S(2)}) collective-permute-start(bf16[4,64,256]{2,1,0:T(8,128)(2,1)S(1)} %get-tuple-element.44), channel_id=1, source_target_pairs={{0,13},{1,12},{4,9},{5,8},{8,5},{9,4},{12,1},{13,0},{2,15},{3,14},... | collective-permute-start | bytes 393224 | tf_op jit(solution)/shard_map/ppermute | solution.py:239
  28.5 0.1 copy.22
  28.6 4.6 %collective-permute-done.14.refs_12_ = bf16[4,64,256]{2,1,0:T(8,128)(2,1)S(1)} collective-permute-done((bf16[4,64,256]{2,1,0:T(8,128)(2,1)S(1)}, bf16[4,64,256]{2,1,0:T(8,128)(2,1)S(1)}, u32[]{:S(2)}, u32[]{:S(2)}) %collective-permute-start.14) | collective-permute-done | bytes 131104 | tf_op jit(solution)/shard_map/ppermute | solution.py:239
  33.2 1.3 %collective-permute-start.3 = (bf16[4,64,256]{2,1,0:T(8,128)(2,1)S(1)}, bf16[4,64,256]{2,1,0:T(8,128)(2,1)S(1)}, u32[]{:S(2)}, u32[]{:S(2)}) collective-permute-start(bf16[4,64,256]{2,1,0:T(8,128)(2,1)S(1)} %get-tuple-element.46), channel_id=1, source_target_pairs={{0,12},{1,13},{4,8},{5,9},{8,4},{9,5},{12,0},{13,1},{2,14},{3,15},... | collective-permute-start | bytes 393224 | tf_op jit(solution)/shard_map/ppermute | solution.py:239
  34.5 0.5 collective-permute-done.1.refs_6_
  35.0 3.9 %collective-permute-start.5 = (bf16[4,64,256]{2,1,0:T(8,128)(2,1)S(1)}, bf16[4,64,256]{2,1,0:T(8,128)(2,1)S(1)}, u32[]{:S(2)}, u32[]{:S(2)}) collective-permute-start(bf16[4,64,256]{2,1,0:T(8,128)(2,1)S(1)} %get-tuple-element.48), channel_id=1, source_target_pairs={{0,9},{1,8},{4,13},{5,12},{8,1},{9,0},{12,5},{13,4},{2,11},{3,10},... | collective-permute-start | bytes 393224 | tf_op jit(solution)/shard_map/ppermute | solution.py:239
  38.9 0.9 collective-permute-start.6
  39.8 0.7 collective-permute-start.7
  40.5 0.7 copy-done.2
  41.2 0.0 copy-done.3
  41.2 5.8 %grads.2 = (bf16[3,64,512]{2,1,0:T(8,128)(2,1)S(1)}, bf16[3,64,512]{2,1,0:T(8,128)(2,1)S(1)}, bf16[3,64,512]{2,1,0:T(8,128)(2,1)S(1)}, bf16[3,64,512]{2,1,0:T(8,...) custom-call(s32[2]{0:T(128)S(1)} %pad_add_fusion.place, ...), custom_call_target="tpu_custom_call" | custom-call | flops 10737418240 | bytes 1835008 | tf_op jit(solution)/shard_map/grads/pallas_call | solution.py:265
  47.1 0.6 collective-permute-start.22
  47.7 4.4 %collective-permute-done.5.refs_10_ = bf16[4,64,256]{2,1,0:T(8,128)(2,1)S(1)} collective-permute-done((bf16[4,64,256]{2,1,0:T(8,128)(2,1)S(1)}, bf16[4,64,256]{2,1,0:T(8,128)(2,1)S(1)}, u32[]{:S(2)}, u32[]{:S(2)}) %collective-permute-start.5) | collective-permute-done | bytes 131104 | tf_op jit(solution)/shard_map/ppermute | solution.py:239
  52.0 2.9 %collective-permute-done.7.refs_12_ = bf16[4,64,256]{2,1,0:T(8,128)(2,1)S(1)} collective-permute-done((bf16[4,64,256]{2,1,0:T(8,128)(2,1)S(1)}, bf16[4,64,256]{2,1,0:T(8,128)(2,1)S(1)}, u32[]{:S(2)}, u32[]{:S(2)}) %collective-permute-start.7) | collective-permute-done | bytes 131104 | tf_op jit(solution)/shard_map/ppermute | solution.py:239
  55.0 5.8 %grads.3 = (bf16[3,64,512]{2,1,0:T(8,128)(2,1)S(1)}, bf16[3,64,512]{2,1,0:T(8,128)(2,1)S(1)}, bf16[3,64,512]{2,1,0:T(8,128)(2,1)S(1)}, bf16[3,64,512]{2,1,0:T(8,...) custom-call(s32[2]{0:T(128)S(1)} %pad_add_fusion.place, ...), custom_call_target="tpu_custom_call", output_to_operand_aliasing={{0}: (18, {}), {1}: (19, {}), {2}: (20, {}), {3}: (21, {}),... | custom-call | flops 10737418240 | bytes 1835008 | tf_op jit(solution)/shard_map/grads/pallas_call | solution.py:265
  60.8 0.6 collective-permute-start.23
  61.4 1.4 %collective-permute-start.15 = (bf16[3,64,512]{2,1,0:T(8,128)(2,1)S(1)}, bf16[3,64,512]{2,1,0:T(8,128)(2,1)S(1)}, u32[]{:S(2)}, u32[]{:S(2)}) collective-permute-start(bf16[3,64,512]{2,1,0:T(8,128)(2,1)S(1)} %get-tuple-element.67), channel_id=1, source_target_pairs={{0,13},{1,12},{4,9},{5,8},{8,5},{9,4},{12,1},{13,0},{2,15},{3,14},... | collective-permute-start | bytes 589832 | tf_op jit(solution)/shard_map/ppermute | solution.py:239
  62.8 1.8 %collective-permute-start.17 = (bf16[3,64,512]{2,1,0:T(8,128)(2,1)S(1)}, bf16[3,64,512]{2,1,0:T(8,128)(2,1)S(1)}, u32[]{:S(2)}, u32[]{:S(2)}) collective-permute-start(bf16[3,64,512]{2,1,0:T(8,128)(2,1)S(1)} %get-tuple-element.69), channel_id=1, source_target_pairs={{0,12},{1,13},{4,8},{5,9},{8,4},{9,5},{12,0},{13,1},{2,14},{3,15},... | collective-permute-start | bytes 589832 | tf_op jit(solution)/shard_map/ppermute | solution.py:239
  64.5 5.9 %collective-permute-done.15.refs_1_ = bf16[3,64,512]{2,1,0:T(8,128)(2,1)S(1)} collective-permute-done((bf16[3,64,512]{2,1,0:T(8,128)(2,1)S(1)}, bf16[3,64,512]{2,1,0:T(8,128)(2,1)S(1)}, u32[]{:S(2)}, u32[]{:S(2)}) %collective-permute-start.15) | collective-permute-done | bytes 196640 | tf_op jit(solution)/shard_map/ppermute | solution.py:239
  70.5 1.2 %collective-permute-start.18 = (bf16[3,64,512]{2,1,0:T(8,128)(2,1)S(1)}, bf16[3,64,512]{2,1,0:T(8,128)(2,1)S(1)}, u32[]{:S(2)}, u32[]{:S(2)}) collective-permute-start(bf16[3,64,512]{2,1,0:T(8,128)(2,1)S(1)} %get-tuple-element.70), channel_id=1, source_target_pairs={{0,4},{1,5},{4,0},{5,1},{8,12},{9,13},{12,8},{13,9},{2,6},{3,7},{6... | collective-permute-start | bytes 589832 | tf_op jit(solution)/shard_map/ppermute | solution.py:239
  71.7 2.1 %collective-permute-done.16.refs_2_ = bf16[3,64,512]{2,1,0:T(8,128)(2,1)S(1)} collective-permute-done((bf16[3,64,512]{2,1,0:T(8,128)(2,1)S(1)}, bf16[3,64,512]{2,1,0:T(8,128)(2,1)S(1)}, u32[]{:S(2)}, u32[]{:S(2)}) %collective-permute-start.16) | collective-permute-done | bytes 196640 | tf_op jit(solution)/shard_map/ppermute | solution.py:239
  73.8 0.9 collective-permute-start.19
  74.7 0.6 collective-permute-start.20
  75.4 2.1 %collective-permute-start.21 = (bf16[3,64,512]{2,1,0:T(8,128)(2,1)S(1)}, bf16[3,64,512]{2,1,0:T(8,128)(2,1)S(1)}, u32[]{:S(2)}, u32[]{:S(2)}) collective-permute-start(bf16[3,64,512]{2,1,0:T(8,128)(2,1)S(1)} %get-tuple-element.73), channel_id=1, source_target_pairs={{0,8},{1,9},{4,12},{5,13},{8,0},{9,1},{12,4},{13,5},{2,10},{3,11},... | collective-permute-start | bytes 589832 | tf_op jit(solution)/shard_map/ppermute | solution.py:239
  77.5 0.1 add.10
  77.6 0.1 add.11
  77.7 0.1 fusion.2
  77.8 0.0 copy-start
  77.8 0.0 copy-start.1
  77.8 1.0 %collective-permute-done.17.refs_3_ = bf16[3,64,512]{2,1,0:T(8,128)(2,1)S(1)} collective-permute-done((bf16[3,64,512]{2,1,0:T(8,128)(2,1)S(1)}, bf16[3,64,512]{2,1,0:T(8,128)(2,1)S(1)}, u32[]{:S(2)}, u32[]{:S(2)}) %collective-permute-start.17) | collective-permute-done | bytes 196640 | tf_op jit(solution)/shard_map/ppermute | solution.py:239
  78.8 7.1 %collective-permute-done.18.refs_4_ = bf16[3,64,512]{2,1,0:T(8,128)(2,1)S(1)} collective-permute-done((bf16[3,64,512]{2,1,0:T(8,128)(2,1)S(1)}, bf16[3,64,512]{2,1,0:T(8,128)(2,1)S(1)}, u32[]{:S(2)}, u32[]{:S(2)}) %collective-permute-start.18) | collective-permute-done | bytes 196640 | tf_op jit(solution)/shard_map/ppermute | solution.py:239
  85.9 6.4 %collective-permute-done.19.refs_5_ = bf16[3,64,512]{2,1,0:T(8,128)(2,1)S(1)} collective-permute-done((bf16[3,64,512]{2,1,0:T(8,128)(2,1)S(1)}, bf16[3,64,512]{2,1,0:T(8,128)(2,1)S(1)}, u32[]{:S(2)}, u32[]{:S(2)}) %collective-permute-start.19) | collective-permute-done | bytes 196640 | tf_op jit(solution)/shard_map/ppermute | solution.py:239
  92.3 4.5 %collective-permute-done.21.refs_7_ = bf16[3,64,512]{2,1,0:T(8,128)(2,1)S(1)} collective-permute-done((bf16[3,64,512]{2,1,0:T(8,128)(2,1)S(1)}, bf16[3,64,512]{2,1,0:T(8,128)(2,1)S(1)}, u32[]{:S(2)}, u32[]{:S(2)}) %collective-permute-start.21) | collective-permute-done | bytes 196640 | tf_op jit(solution)/shard_map/ppermute | solution.py:239
  96.7 1.9 %unpack.1 = (bf16[64,4096]{1,0:T(8,128)(2,1)}, bf16[64,4096]{1,0:T(8,128)(2,1)}, bf16[64,4096]{1,0:T(8,128)(2,1)}) custom-call(s32[2]{0:T(128)S(1)} %pad_add_fusion.place, bf16[3,64,512]{2,1,0:T(8,128)(2,1)S(1)} %get-tuple-element.66.refs_0_, bf16[3,64,512]{2,1,0:T(8,128)(2,1)S(1)} %collective-permute-done.15.refs_1_, ...), custom_call_target="tpu_custom_call" | custom-call | tf_op jit(solution)/shard_map/unpack/pallas_call | solution.py:320
  (20 shorter events, 0.0 us)
Async XLA Ops:
  3.0 36.8 %collective-permute-start.8 = (bf16[2,256,512]{2,1,0:T(8,128)(2,1)S(1)}, bf16[2,256,512]{2,1,0:T(8,128)(2,1)S(1)}, u32[]{:S(2)}, u32[]{:S(2)}) collective-permute-start(bf16[2,256,512]{2,1,0:T(8,128)(2,1)S(1)} %get-tuple-element.51), channel_id=1, source_target_pairs={{0,2},{2,0},{1,3},{3,1},{4,6},{6,4},{5,7},{7,5},{8,10},{10,8},{9,1... | collective-permute-start | bytes 1572872 | tf_op jit(solution)/shard_map/ppermute | solution.py:239
  6.0 7.5 %collective-permute-start = (bf16[4,64,256]{2,1,0:T(8,128)(2,1)S(1)}, bf16[4,64,256]{2,1,0:T(8,128)(2,1)S(1)}, u32[]{:S(2)}, u32[]{:S(2)}) collective-permute-start(bf16[4,64,256]{2,1,0:T(8,128)(2,1)S(1)} %get-tuple-element.43), channel_id=1, source_target_pairs={{0,13},{1,12},{4,9},{5,8},{8,5},{9,4},{12,1},{13,0},{2,15},{3,14},... | collective-permute-start | bytes 393224 | tf_op jit(solution)/shard_map/ppermute | solution.py:239
  8.7 8.3 %collective-permute-start.10 = (bf16[4,64,256]{2,1,0:T(8,128)(2,1)S(1)}, bf16[4,64,256]{2,1,0:T(8,128)(2,1)S(1)}, u32[]{:S(2)}, u32[]{:S(2)}) collective-permute-start(bf16[4,64,256]{2,1,0:T(8,128)(2,1)S(1)} %get-tuple-element.53), channel_id=1, source_target_pairs={{0,12},{1,13},{4,8},{5,9},{8,4},{9,5},{12,0},{13,1},{2,14},{3,15},... | collective-permute-start | bytes 393224 | tf_op jit(solution)/shard_map/ppermute | solution.py:239
  9.6 15.5 %collective-permute-start.11 = (bf16[4,64,256]{2,1,0:T(8,128)(2,1)S(1)}, bf16[4,64,256]{2,1,0:T(8,128)(2,1)S(1)}, u32[]{:S(2)}, u32[]{:S(2)}) collective-permute-start(bf16[4,64,256]{2,1,0:T(8,128)(2,1)S(1)} %get-tuple-element.54), channel_id=1, source_target_pairs={{0,4},{1,5},{4,0},{5,1},{8,12},{9,13},{12,8},{13,9},{2,6},{3,7},{6... | collective-permute-start | bytes 393224 | tf_op jit(solution)/shard_map/ppermute | solution.py:239
  9.6 17.1 %collective-permute-start.12 = (bf16[4,64,256]{2,1,0:T(8,128)(2,1)S(1)}, bf16[4,64,256]{2,1,0:T(8,128)(2,1)S(1)}, u32[]{:S(2)}, u32[]{:S(2)}) collective-permute-start(bf16[4,64,256]{2,1,0:T(8,128)(2,1)S(1)} %get-tuple-element.55), channel_id=1, source_target_pairs={{0,9},{1,8},{4,13},{5,12},{8,1},{9,0},{12,5},{13,4},{2,11},{3,10},... | collective-permute-start | bytes 393224 | tf_op jit(solution)/shard_map/ppermute | solution.py:239
  13.5 15.0 %collective-permute-start.13 = (bf16[4,64,256]{2,1,0:T(8,128)(2,1)S(1)}, bf16[4,64,256]{2,1,0:T(8,128)(2,1)S(1)}, u32[]{:S(2)}, u32[]{:S(2)}) collective-permute-start(bf16[4,64,256]{2,1,0:T(8,128)(2,1)S(1)} %get-tuple-element.56), channel_id=1, source_target_pairs={{0,1},{1,0},{4,5},{5,4},{8,9},{9,8},{12,13},{13,12},{2,3},{3,2},{6... | collective-permute-start | bytes 393224 | tf_op jit(solution)/shard_map/ppermute | solution.py:239
  17.0 16.1 %collective-permute-start.14 = (bf16[4,64,256]{2,1,0:T(8,128)(2,1)S(1)}, bf16[4,64,256]{2,1,0:T(8,128)(2,1)S(1)}, u32[]{:S(2)}, u32[]{:S(2)}) collective-permute-start(bf16[4,64,256]{2,1,0:T(8,128)(2,1)S(1)} %get-tuple-element.57), channel_id=1, source_target_pairs={{0,8},{1,9},{4,12},{5,13},{8,0},{9,1},{12,4},{13,5},{2,10},{3,11},... | collective-permute-start | bytes 393224 | tf_op jit(solution)/shard_map/ppermute | solution.py:239
  25.1 3.4 %copy-start.4 = (s32[1,4,3]{1,0,2:T(1,128)S(1)}, s32[1,4,3]{1,0,2:T(1,128)}, u32[]{:S(2)}) copy-start(s32[1,4,3]{1,0,2:T(1,128)} %param.15) | copy-start | bytes 148
  25.1 9.4 %collective-permute-start.9 = (bf16[4,64,256]{2,1,0:T(8,128)(2,1)S(1)}, bf16[4,64,256]{2,1,0:T(8,128)(2,1)S(1)}, u32[]{:S(2)}, u32[]{:S(2)}) collective-permute-start(bf16[4,64,256]{2,1,0:T(8,128)(2,1)S(1)} %get-tuple-element.52), channel_id=1, source_target_pairs={{0,5},{1,4},{4,1},{5,0},{8,13},{9,12},{12,9},{13,8},{2,7},{3,6},{6... | collective-permute-start | bytes 393224 | tf_op jit(solution)/shard_map/ppermute | solution.py:239
  26.7 8.3 %collective-permute-start.1 = (bf16[4,64,256]{2,1,0:T(8,128)(2,1)S(1)}, bf16[4,64,256]{2,1,0:T(8,128)(2,1)S(1)}, u32[]{:S(2)}, u32[]{:S(2)}) collective-permute-start(bf16[4,64,256]{2,1,0:T(8,128)(2,1)S(1)} %get-tuple-element.44), channel_id=1, source_target_pairs={{0,13},{1,12},{4,9},{5,8},{8,5},{9,4},{12,1},{13,0},{2,15},{3,14},... | collective-permute-start | bytes 393224 | tf_op jit(solution)/shard_map/ppermute | solution.py:239
  28.5 10.4 %collective-permute-start.2 = (bf16[4,64,256]{2,1,0:T(8,128)(2,1)S(1)}, bf16[4,64,256]{2,1,0:T(8,128)(2,1)S(1)}, u32[]{:S(2)}, u32[]{:S(2)}) collective-permute-start(bf16[4,64,256]{2,1,0:T(8,128)(2,1)S(1)} %get-tuple-element.45), channel_id=1, source_target_pairs={{0,5},{1,4},{4,1},{5,0},{8,13},{9,12},{12,9},{13,8},{2,7},{3,6},{6... | collective-permute-start | bytes 393224 | tf_op jit(solution)/shard_map/ppermute | solution.py:239
  33.2 13.9 %collective-permute-start.3 = (bf16[4,64,256]{2,1,0:T(8,128)(2,1)S(1)}, bf16[4,64,256]{2,1,0:T(8,128)(2,1)S(1)}, u32[]{:S(2)}, u32[]{:S(2)}) collective-permute-start(bf16[4,64,256]{2,1,0:T(8,128)(2,1)S(1)} %get-tuple-element.46), channel_id=1, source_target_pairs={{0,12},{1,13},{4,8},{5,9},{8,4},{9,5},{12,0},{13,1},{2,14},{3,15},... | collective-permute-start | bytes 393224 | tf_op jit(solution)/shard_map/ppermute | solution.py:239
  34.5 13.2 %collective-permute-start.4 = (bf16[4,64,256]{2,1,0:T(8,128)(2,1)S(1)}, bf16[4,64,256]{2,1,0:T(8,128)(2,1)S(1)}, u32[]{:S(2)}, u32[]{:S(2)}) collective-permute-start(bf16[4,64,256]{2,1,0:T(8,128)(2,1)S(1)} %get-tuple-element.47), channel_id=1, source_target_pairs={{0,4},{1,5},{4,0},{5,1},{8,12},{9,13},{12,8},{13,9},{2,6},{3,7},{6... | collective-permute-start | bytes 393224 | tf_op jit(solution)/shard_map/ppermute | solution.py:239
  35.0 17.1 %collective-permute-start.5 = (bf16[4,64,256]{2,1,0:T(8,128)(2,1)S(1)}, bf16[4,64,256]{2,1,0:T(8,128)(2,1)S(1)}, u32[]{:S(2)}, u32[]{:S(2)}) collective-permute-start(bf16[4,64,256]{2,1,0:T(8,128)(2,1)S(1)} %get-tuple-element.48), channel_id=1, source_target_pairs={{0,9},{1,8},{4,13},{5,12},{8,1},{9,0},{12,5},{13,4},{2,11},{3,10},... | collective-permute-start | bytes 393224 | tf_op jit(solution)/shard_map/ppermute | solution.py:239
  38.9 13.2 %collective-permute-start.6 = (bf16[4,64,256]{2,1,0:T(8,128)(2,1)S(1)}, bf16[4,64,256]{2,1,0:T(8,128)(2,1)S(1)}, u32[]{:S(2)}, u32[]{:S(2)}) collective-permute-start(bf16[4,64,256]{2,1,0:T(8,128)(2,1)S(1)} %get-tuple-element.49), channel_id=1, source_target_pairs={{0,1},{1,0},{4,5},{5,4},{8,9},{9,8},{12,13},{13,12},{2,3},{3,2},{6... | collective-permute-start | bytes 393224 | tf_op jit(solution)/shard_map/ppermute | solution.py:239
  39.8 15.1 %collective-permute-start.7 = (bf16[4,64,256]{2,1,0:T(8,128)(2,1)S(1)}, bf16[4,64,256]{2,1,0:T(8,128)(2,1)S(1)}, u32[]{:S(2)}, u32[]{:S(2)}) collective-permute-start(bf16[4,64,256]{2,1,0:T(8,128)(2,1)S(1)} %get-tuple-element.50), channel_id=1, source_target_pairs={{0,8},{1,9},{4,12},{5,13},{8,0},{9,1},{12,4},{13,5},{2,10},{3,11},... | collective-permute-start | bytes 393224 | tf_op jit(solution)/shard_map/ppermute | solution.py:239
  40.5 0.7 copy-start.2
  40.5 0.7 copy-start.3
  47.1 27.6 %collective-permute-start.22 = (f32[2,256,256]{2,1,0:T(8,128)S(1)}, f32[2,256,256]{2,1,0:T(8,128)S(1)}, u32[]{:S(2)}, u32[]{:S(2)}) collective-permute-start(f32[2,256,256]{2,1,0:T(8,128)S(1)} %get-tuple-element.75), channel_id=1, source_target_pairs={{0,2},{2,0},{1,3},{3,1},{4,6},{6,4},{5,7},{7,5},{8,10},{10,8},{9,1... | collective-permute-start | bytes 1572872 | tf_op jit(solution)/shard_map/ppermute | solution.py:239
  60.8 14.5 %collective-permute-start.23 = (f32[2,256,256]{2,1,0:T(8,128)S(1)}, f32[2,256,256]{2,1,0:T(8,128)S(1)}, u32[]{:S(2)}, u32[]{:S(2)}) collective-permute-start(f32[2,256,256]{2,1,0:T(8,128)S(1)} %get-tuple-element.77), channel_id=1, source_target_pairs={{0,2},{2,0},{1,3},{3,1},{4,6},{6,4},{5,7},{7,5},{8,10},{10,8},{9,1... | collective-permute-start | bytes 1572872 | tf_op jit(solution)/shard_map/ppermute | solution.py:239
  61.4 9.1 %collective-permute-start.15 = (bf16[3,64,512]{2,1,0:T(8,128)(2,1)S(1)}, bf16[3,64,512]{2,1,0:T(8,128)(2,1)S(1)}, u32[]{:S(2)}, u32[]{:S(2)}) collective-permute-start(bf16[3,64,512]{2,1,0:T(8,128)(2,1)S(1)} %get-tuple-element.67), channel_id=1, source_target_pairs={{0,13},{1,12},{4,9},{5,8},{8,5},{9,4},{12,1},{13,0},{2,15},{3,14},... | collective-permute-start | bytes 589832 | tf_op jit(solution)/shard_map/ppermute | solution.py:239
  62.8 11.0 %collective-permute-start.16 = (bf16[3,64,512]{2,1,0:T(8,128)(2,1)S(1)}, bf16[3,64,512]{2,1,0:T(8,128)(2,1)S(1)}, u32[]{:S(2)}, u32[]{:S(2)}) collective-permute-start(bf16[3,64,512]{2,1,0:T(8,128)(2,1)S(1)} %get-tuple-element.68), channel_id=1, source_target_pairs={{0,5},{1,4},{4,1},{5,0},{8,13},{9,12},{12,9},{13,8},{2,7},{3,6},{6... | collective-permute-start | bytes 589832 | tf_op jit(solution)/shard_map/ppermute | solution.py:239
  62.8 16.0 %collective-permute-start.17 = (bf16[3,64,512]{2,1,0:T(8,128)(2,1)S(1)}, bf16[3,64,512]{2,1,0:T(8,128)(2,1)S(1)}, u32[]{:S(2)}, u32[]{:S(2)}) collective-permute-start(bf16[3,64,512]{2,1,0:T(8,128)(2,1)S(1)} %get-tuple-element.69), channel_id=1, source_target_pairs={{0,12},{1,13},{4,8},{5,9},{8,4},{9,5},{12,0},{13,1},{2,14},{3,15},... | collective-permute-start | bytes 589832 | tf_op jit(solution)/shard_map/ppermute | solution.py:239
  70.5 15.4 %collective-permute-start.18 = (bf16[3,64,512]{2,1,0:T(8,128)(2,1)S(1)}, bf16[3,64,512]{2,1,0:T(8,128)(2,1)S(1)}, u32[]{:S(2)}, u32[]{:S(2)}) collective-permute-start(bf16[3,64,512]{2,1,0:T(8,128)(2,1)S(1)} %get-tuple-element.70), channel_id=1, source_target_pairs={{0,4},{1,5},{4,0},{5,1},{8,12},{9,13},{12,8},{13,9},{2,6},{3,7},{6... | collective-permute-start | bytes 589832 | tf_op jit(solution)/shard_map/ppermute | solution.py:239
  73.8 18.5 %collective-permute-start.19 = (bf16[3,64,512]{2,1,0:T(8,128)(2,1)S(1)}, bf16[3,64,512]{2,1,0:T(8,128)(2,1)S(1)}, u32[]{:S(2)}, u32[]{:S(2)}) collective-permute-start(bf16[3,64,512]{2,1,0:T(8,128)(2,1)S(1)} %get-tuple-element.71), channel_id=1, source_target_pairs={{0,9},{1,8},{4,13},{5,12},{8,1},{9,0},{12,5},{13,4},{2,11},{3,10},... | collective-permute-start | bytes 589832 | tf_op jit(solution)/shard_map/ppermute | solution.py:239
  74.7 17.5 %collective-permute-start.20 = (bf16[3,64,512]{2,1,0:T(8,128)(2,1)S(1)}, bf16[3,64,512]{2,1,0:T(8,128)(2,1)S(1)}, u32[]{:S(2)}, u32[]{:S(2)}) collective-permute-start(bf16[3,64,512]{2,1,0:T(8,128)(2,1)S(1)} %get-tuple-element.72), channel_id=1, source_target_pairs={{0,1},{1,0},{4,5},{5,4},{8,9},{9,8},{12,13},{13,12},{2,3},{3,2},{6... | collective-permute-start | bytes 589832 | tf_op jit(solution)/shard_map/ppermute | solution.py:239
  75.4 21.4 %collective-permute-start.21 = (bf16[3,64,512]{2,1,0:T(8,128)(2,1)S(1)}, bf16[3,64,512]{2,1,0:T(8,128)(2,1)S(1)}, u32[]{:S(2)}, u32[]{:S(2)}) collective-permute-start(bf16[3,64,512]{2,1,0:T(8,128)(2,1)S(1)} %get-tuple-element.73), channel_id=1, source_target_pairs={{0,8},{1,9},{4,12},{5,13},{8,0},{9,1},{12,4},{13,5},{2,10},{3,11},... | collective-permute-start | bytes 589832 | tf_op jit(solution)/shard_map/ppermute | solution.py:239
  77.8 20.8 %copy-start = (f32[256,512]{1,0:T(8,128)}, f32[256,512]{1,0:T(8,128)S(1)}, u32[]{:S(2)}) copy-start(f32[256,512]{1,0:T(8,128)S(1)} %get-tuple-element.81.refs_9_) | copy-start | bytes 1572868
  77.8 20.8 %copy-start.1 = (f32[256,512]{1,0:T(8,128)}, f32[256,512]{1,0:T(8,128)S(1)}, u32[]{:S(2)}) copy-start(f32[256,512]{1,0:T(8,128)S(1)} %get-tuple-element.82.refs_8_) | copy-start | bytes 1572868

commit v3 on v2

--- a/solution.py
+++ b/solution.py
@@ -11,7 +11,9 @@
 HD = 128
 BLOCK = 128
 K_MAX = 3
-AHEAD = 0
+EARLY = 2
+EHOLD = 5
+TAIL = 3
 TOKENS = ("seq", "rep")
 ANY = pl.BlockSpec(memory_space=pl.ANY)
 SMEM = pl.BlockSpec(memory_space=pltpu.SMEM)
@@ -46,7 +48,7 @@
 
 
 def grads_kernel(
-    off, width, columns, order, gauge_order, waits, held, place, lists, counts, chosen, *refs
+    off, width, columns, order, targets, gauge_order, waits, held, place, lists, counts, chosen, *refs
 ):
     n_tok, n_gauge = len(order), len(gauge_order)
     refs = list(refs)
@@ -60,7 +62,7 @@
     recvs, gauge_recvs = take(n_tok), take(n_gauge)
     take(waits + held)
     outs, gauge_outs = take(n_tok + 1), take(n_gauge + 1)
-    tok, gau, acc, gacc, res, in_sems, own_sems, gin_sems, gown_sems, out_sems, gout_sems = refs
+    tok, gau, acc, gacc, glow, res, in_sems, own_sems, gin_sems, gown_sems, out_sems, gout_sems = refs
     me, gauge_me = place[0], place[1]
     rows = arrays[0].shape[0]
     gauge_rows = gauges[0].shape[0]
@@ -152,15 +154,13 @@
 
     lax.fori_loop(0, length // BLOCK, block, 0, unroll=4)
 
+    glow[...] = gacc[...].astype(jnp.bfloat16)
     copies = []
     for at, k in enumerate((0,) + tuple(gauge_order)):
-        copies.append(
-            pltpu.make_async_copy(
-                gacc.at[
-                    :, pl.ds(pl.multiple_of((gauge_me ^ k) * gauge_rows, gauge_rows), gauge_rows), :
-                ],
-                gauge_outs[at],
-                gout_sems.at[at],
+        part = pl.ds(pl.multiple_of((gauge_me ^ k) * gauge_rows, gauge_rows), gauge_rows)
+        copies.append(
+            pltpu.make_async_copy(
+                (glow if k else gacc).at[:, part, :], gauge_outs[at], gout_sems.at[at]
             )
         )
     for copy in copies:
@@ -168,12 +168,12 @@
     res[1] = acc[0].astype(jnp.bfloat16)
     res[2] = acc[1].astype(jnp.bfloat16)
     token_copies = []
-    for k in range(n_tok + 1):
+    for at, (k, merged) in enumerate(targets):
         token_copies.append(
             pltpu.make_async_copy(
                 res.at[:, pl.ds(pl.multiple_of((me ^ k) * rows, rows), rows), :],
-                outs[k].at[:, :, pl.ds(off, width)],
-                out_sems.at[k],
+                outs[at].at[:, :, pl.ds(off, width)] if merged else outs[at],
+                out_sems.at[at],
             )
         )
     run_copies(token_copies)
@@ -181,16 +181,16 @@
         copy.wait()
 
 
-def unpack_kernel(columns, order, place, *refs):
+def unpack_kernel(columns, parts, place, *refs):
     outs, sems = refs[-4:-1], refs[-1]
     me = place[0]
     copies = []
-    for at, k in enumerate(order):
-        start = pl.multiple_of((me ^ k) * columns, HD)
+    for at, (k, off, width) in enumerate(parts):
+        start = pl.multiple_of((me ^ k) * columns + off, HD)
         for a in range(3):
             copies.append(
                 pltpu.make_async_copy(
-                    refs[at].at[a], outs[a].at[:, pl.ds(start, columns)], sems.at[at, a]
+                    refs[at].at[a], outs[a].at[:, pl.ds(start, width)], sems.at[at, a]
                 )
             )
     run_copies(copies)
@@ -260,22 +260,27 @@
             name="pack",
         )(place, *arrays, gauge_key, gauge_value, *after)
 
-    def grads(chunk, recvs, order, after, held):
+    def grads(chunk, recvs, targets, held):
         off, width = chunk
         return pl.pallas_call(
             functools.partial(
-                grads_kernel, off, width, columns, order, gauge_order, len(after), len(held)
+                grads_kernel, off, width, columns, order, targets, gauge_order, 0, len(held)
             ),
-            out_shape=[jax.ShapeDtypeStruct((3, rows, columns), bf16)] * total
-            + [jax.ShapeDtypeStruct((2, gauge_rows, width), f32)] * head_total,
+            out_shape=[
+                jax.ShapeDtypeStruct((3, rows, columns if merged else width), bf16)
+                for _, merged in targets
+            ]
+            + [jax.ShapeDtypeStruct((2, gauge_rows, width), f32)]
+            + [jax.ShapeDtypeStruct((2, gauge_rows, width), bf16)] * (head_total - 1),
             in_specs=[SMEM] * 4
-            + [ANY] * (6 + len(order) + len(gauge_order) + len(after) + len(held)),
+            + [ANY] * (6 + len(order) + len(gauge_order) + len(held)),
             out_specs=[ANY] * (total + head_total),
             scratch_shapes=[
                 pltpu.VMEM((4, length, width), bf16),
                 pltpu.VMEM((2, gauge_total, width), bf16),
                 pltpu.VMEM((2, length, width), f32),
                 pltpu.VMEM((2, gauge_total, width), f32),
+                pltpu.VMEM((2, gauge_total, width), bf16),
                 pltpu.VMEM((3, length, width), bf16),
                 pltpu.SemaphoreType.DMA((max(len(order), 1),)),
                 pltpu.SemaphoreType.DMA((4,)),
@@ -291,41 +296,73 @@
                 transcendentals=0,
             ),
             input_output_aliases={
-                10 + len(order) + len(gauge_order) + len(after) + i: i for i in range(len(held))
+                10 + len(order) + len(gauge_order) + i: i for i in range(len(held))
             },
             name="grads",
-        )(place, *lists, *arrays, gauge_key, gauge_value, *recvs, *gauge_recvs, *after, *held)
+        )(place, *lists, *arrays, gauge_key, gauge_value, *recvs, *gauge_recvs, *held)
+
+    def hold(buffers, after):
+        return pl.pallas_call(
+            lambda *refs: None,
+            out_shape=[jax.ShapeDtypeStruct(x.shape, x.dtype) for x in buffers],
+            in_specs=[ANY] * (len(buffers) + len(after)),
+            out_specs=[ANY] * len(buffers),
+            input_output_aliases={i: i for i in range(len(buffers))},
+            compiler_params=params,
+            name="hold",
+        )(*buffers, *after)
+
+    def unpack(parts, outs, after):
+        held = len(outs)
+        return pl.pallas_call(
+            functools.partial(unpack_kernel, columns, [part[1:] for part in parts]),
+            out_shape=[jax.ShapeDtypeStruct((rows, model), bf16)] * 3,
+            in_specs=[SMEM] + [ANY] * (len(parts) + held + len(after)),
+            out_specs=[ANY] * 3,
+            scratch_shapes=[pltpu.SemaphoreType.DMA((len(parts), 3))],
+            input_output_aliases={1 + len(parts) + i: i for i in range(held)},
+            compiler_params=params,
+            name="unpack",
+        )(place, *[part[0] for part in parts], *outs, *after)
 
     def send(packed, part):
         return [swap(s, TOKENS, total, k) for s, k in zip(packed, part)]
 
+    single = len(chunks) == 1
     *packed, gauge_send = pack(chunks[0], order, [], True)
     gauge_recvs = [swap(gauge_send, "head", head_total, k) for k in gauge_order]
     recvs = send(packed, order)
-    pieces, gauge_sums = [], []
+    early = () if single else order[0 : 2 * EARLY : 2]
+    far, near = order[0::2], order[1::2]
+    whole = (*far[2:3], *near[:2], *far[3:], *near[2:]) if early else order
+    targets = tuple((k, True) for k in (0, *whole)) + tuple((k, False) for k in early)
+    merged, parts, gauge_sums, back_early = [], [], [], []
     for at, chunk in enumerate(chunks):
         ahead = []
         if at + 1 < len(chunks):
             ahead = send(pack(chunks[at + 1], order, recvs[:1], False), order)
-        out = grads(chunk, recvs, order, ahead[:AHEAD], pieces)
-        pieces = out[:total]
+        out = grads(chunk, recvs, targets, merged)
+        if gauge_sums:
+            out = hold(out, back_early[:1] + gauge_back)
+        merged, cut = list(out[: 1 + len(whole)]), out[1 + len(whole) : total]
+        if at + 1 < len(chunks):
+            cut = hold(cut, ahead[:EHOLD])
+            back_early = send(cut, early)
+            parts += [(x, k, *chunk) for x, k in zip(back_early, early)]
         gauge_back = [
             swap(x, "head", head_total, k) for x, k in zip(out[total + 1 :], gauge_order)
         ]
-        gauge_sums.append(functools.reduce(jnp.add, gauge_back, out[total]))
+        gauge_sums.append(sum((x.astype(f32) for x in gauge_back), out[total]))
         recvs = ahead
-    back = [pieces[0]] + [swap(pieces[k], TOKENS, total, k) for k in order]
+    pieces = dict(zip(whole, merged[1:]))
+    late = [(swap(pieces[k], TOKENS, total, k), k, 0, columns) for k in whole]
+    if early:
+        late = [(x, k, *chunks[-1]) for x, k in zip(send(cut, early), early)] + late
     gauge_sum = jnp.concatenate(gauge_sums, axis=2)
     gauge_grads = [gauge_sum[0], gauge_sum[1]]
-    outs = pl.pallas_call(
-        functools.partial(unpack_kernel, columns, (0, *order)),
-        out_shape=[jax.ShapeDtypeStruct((rows, model), bf16)] * 3,
-        in_specs=[SMEM] + [ANY] * (total + 2),
-        out_specs=[ANY] * 3,
-        scratch_shapes=[pltpu.SemaphoreType.DMA((total, 3))],
-        compiler_params=params,
-        name="unpack",
-    )(place, *back, *gauge_grads)
+    parts = parts + [(merged[0], 0, 0, columns)] + late
+    outs = unpack(parts[:-TAIL], [], [])
+    outs = unpack(parts[-TAIL:], outs, gauge_grads)
     return (outs[0][None], outs[1][None], outs[2][None], *gauge_grads)
 
 

time: 99 us -> 91.7 us (0.926)
  waiting for transfers between devices: 42.7 us -> 32.5 us
  starting transfers between devices: 36.3 us -> 37.8 us
  Pallas kernels: 17.7 us -> 19.1 us
    ppermute x24 -> x26, waiting for transfers between devices: 42.7 us -> 32.5 us  [swap(): return lax.ppermute(x, axis, [(i, i ^ k) for i in range(size)])]
    ppermute x24 -> x26, starting transfers between devices: 36.3 us -> 37.8 us  [swap(): return lax.ppermute(x, axis, [(i, i ^ k) for i in range(size)])]
    pallas_call x1 -> x4, Pallas kernels: 1.87 us -> 3.08 us  [the longest x2 3.08 us: unpack(): pl.pallas_call(functools.partial(unpack_kernel, columns, [part[1:] for pa...]
  transfers between devices with their start and end apart: 24 -> 26, of which waited for: 13 -> 11; matrix products, arithmetic and copies ran while one was open for 0% -> 0% of each run, Pallas kernels for 14% -> 17%
where the time goes in v3:
time: 91.7 us; the launch traced here: 91.3 us
  starting transfers between devices  37.8 us (41%)
  waiting for transfers between devices  32.5 us (35%)
  Pallas kernels  19.1 us (21%)
    ppermute x26, starting transfers between devices, swap(): return lax.ppermute(x, axis, [(i, i ^ k) for i in range(size)])  37.8 us
    ppermute x26, waiting for transfers between devices, swap(): return lax.ppermute(x, axis, [(i, i ^ k) for i in range(size)])  32.5 us
    pallas_call x2, Pallas kernels, grads(): pl.pallas_call(functools.partial(grads_kernel, off, width, columns, order...  11.8 us
    pallas_call x2, Pallas kernels, pack(): pl.pallas_call(functools.partial(pack_kernel, off, width, columns, part,...  4.2 us
    pallas_call x2, Pallas kernels, unpack(): pl.pallas_call(functools.partial(unpack_kernel, columns, [part[1:] for pa...  3.08 us
  transfers between devices with their start and end apart: 26, of which 11 were waited for; matrix products, arithmetic and copies ran while one was open for 0% of the time, Pallas kernels for 17%

profile of v3, /device:TPU:0, one launch (start us, length us, event | category | flops | bytes accessed | tf_op | source)
XLA Modules:
  0.0 91.3 jit_solution(12638728313144931162)
XLA Ops:
  0.6 0.1 pad_add_fusion.place
  0.7 2.3 %pack.2 = (bf16[4,64,256]{2,1,0:T(8,128)(2,1)S(1)}, bf16[4,64,256]{2,1,0:T(8,128)(2,1)S(1)}, bf16[4,64,256]{2,1,0:T(8,128)(2,1)S(1)}, bf16[4,64,256]{2,1,0:T(8,1...) custom-call(s32[2]{0:T(128)S(1)} %pad_add_fusion.place, ...), custom_call_target="tpu_custom_call" | custom-call | tf_op jit(solution)/shard_map/pack/pallas_call | solution.py:248
  3.0 3.0 %collective-permute-start.8 = (bf16[2,256,512]{2,1,0:T(8,128)(2,1)S(1)}, bf16[2,256,512]{2,1,0:T(8,128)(2,1)S(1)}, u32[]{:S(2)}, u32[]{:S(2)}) collective-permute-start(bf16[2,256,512]{2,1,0:T(8,128)(2,1)S(1)} %get-tuple-element.66), channel_id=1, source_target_pairs={{0,2},{2,0},{1,3},{3,1},{4,6},{6,4},{5,7},{7,5},{8,10},{10,8},{9,1... | collective-permute-start | bytes 1572872 | tf_op jit(solution)/shard_map/ppermute | solution.py:239
  6.0 2.8 %collective-permute-start = (bf16[4,64,256]{2,1,0:T(8,128)(2,1)S(1)}, bf16[4,64,256]{2,1,0:T(8,128)(2,1)S(1)}, u32[]{:S(2)}, u32[]{:S(2)}) collective-permute-start(bf16[4,64,256]{2,1,0:T(8,128)(2,1)S(1)} %get-tuple-element.58), channel_id=1, source_target_pairs={{0,13},{1,12},{4,9},{5,8},{8,5},{9,4},{12,1},{13,0},{2,15},{3,14},... | collective-permute-start | bytes 393224 | tf_op jit(solution)/shard_map/ppermute | solution.py:239
  8.7 0.1 collective-permute-start.9
  8.9 1.3 %collective-permute-start.10 = (bf16[4,64,256]{2,1,0:T(8,128)(2,1)S(1)}, bf16[4,64,256]{2,1,0:T(8,128)(2,1)S(1)}, u32[]{:S(2)}, u32[]{:S(2)}) collective-permute-start(bf16[4,64,256]{2,1,0:T(8,128)(2,1)S(1)} %get-tuple-element.68), channel_id=1, source_target_pairs={{0,12},{1,13},{4,8},{5,9},{8,4},{9,5},{12,0},{13,1},{2,14},{3,15},... | collective-permute-start | bytes 393224 | tf_op jit(solution)/shard_map/ppermute | solution.py:239
  10.2 1.1 %collective-permute-start.11 = (bf16[4,64,256]{2,1,0:T(8,128)(2,1)S(1)}, bf16[4,64,256]{2,1,0:T(8,128)(2,1)S(1)}, u32[]{:S(2)}, u32[]{:S(2)}) collective-permute-start(bf16[4,64,256]{2,1,0:T(8,128)(2,1)S(1)} %get-tuple-element.69), channel_id=1, source_target_pairs={{0,4},{1,5},{4,0},{5,1},{8,12},{9,13},{12,8},{13,9},{2,6},{3,7},{6... | collective-permute-start | bytes 393224 | tf_op jit(solution)/shard_map/ppermute | solution.py:239
  11.3 2.2 %collective-permute-done.refs_6_ = bf16[4,64,256]{2,1,0:T(8,128)(2,1)S(1)} collective-permute-done((bf16[4,64,256]{2,1,0:T(8,128)(2,1)S(1)}, bf16[4,64,256]{2,1,0:T(8,128)(2,1)S(1)}, u32[]{:S(2)}, u32[]{:S(2)}) %collective-permute-start) | collective-permute-done | bytes 131104 | tf_op jit(solution)/shard_map/ppermute | solution.py:239
  13.5 2.8 %collective-permute-start.12 = (bf16[4,64,256]{2,1,0:T(8,128)(2,1)S(1)}, bf16[4,64,256]{2,1,0:T(8,128)(2,1)S(1)}, u32[]{:S(2)}, u32[]{:S(2)}) collective-permute-start(bf16[4,64,256]{2,1,0:T(8,128)(2,1)S(1)} %get-tuple-element.70), channel_id=1, source_target_pairs={{0,9},{1,8},{4,13},{5,12},{8,1},{9,0},{12,5},{13,4},{2,11},{3,10},... | collective-permute-start | bytes 393224 | tf_op jit(solution)/shard_map/ppermute | solution.py:239
  16.4 1.9 %pack.3 = (bf16[4,64,256]{2,1,0:T(8,128)(2,1)S(1)}, bf16[4,64,256]{2,1,0:T(8,128)(2,1)S(1)}, bf16[4,64,256]{2,1,0:T(8,128)(2,1)S(1)}, bf16[4,64,256]{2,1,0:T(8,1...) custom-call(s32[2]{0:T(128)S(1)} %pad_add_fusion.place, ...), custom_call_target="tpu_custom_call" | custom-call | tf_op jit(solution)/shard_map/pack/pallas_call | solution.py:248
  18.3 1.0 %collective-permute-start.13 = (bf16[4,64,256]{2,1,0:T(8,128)(2,1)S(1)}, bf16[4,64,256]{2,1,0:T(8,128)(2,1)S(1)}, u32[]{:S(2)}, u32[]{:S(2)}) collective-permute-start(bf16[4,64,256]{2,1,0:T(8,128)(2,1)S(1)} %get-tuple-element.71), channel_id=1, source_target_pairs={{0,1},{1,0},{4,5},{5,4},{8,9},{9,8},{12,13},{13,12},{2,3},{3,2},{6... | collective-permute-start | bytes 393224 | tf_op jit(solution)/shard_map/ppermute | solution.py:239
  19.3 0.2 collective-permute-done.10.refs_8_
  19.5 2.7 %collective-permute-start.14 = (bf16[4,64,256]{2,1,0:T(8,128)(2,1)S(1)}, bf16[4,64,256]{2,1,0:T(8,128)(2,1)S(1)}, u32[]{:S(2)}, u32[]{:S(2)}) collective-permute-start(bf16[4,64,256]{2,1,0:T(8,128)(2,1)S(1)} %get-tuple-element.72), channel_id=1, source_target_pairs={{0,8},{1,9},{4,12},{5,13},{8,0},{9,1},{12,4},{13,5},{2,10},{3,11},... | collective-permute-start | bytes 393224 | tf_op jit(solution)/shard_map/ppermute | solution.py:239
  22.3 0.8 collective-permute-done.11.refs_9_
  23.1 0.4 collective-permute-start.1
  23.5 8.9 %collective-permute-done.12.refs_10_ = bf16[4,64,256]{2,1,0:T(8,128)(2,1)S(1)} collective-permute-done((bf16[4,64,256]{2,1,0:T(8,128)(2,1)S(1)}, bf16[4,64,256]{2,1,0:T(8,128)(2,1)S(1)}, u32[]{:S(2)}, u32[]{:S(2)}) %collective-permute-start.12) | collective-permute-done | bytes 131104 | tf_op jit(solution)/shard_map/ppermute | solution.py:239
  32.3 0.1 copy.35
  32.4 2.6 %collective-permute-start.3 = (bf16[4,64,256]{2,1,0:T(8,128)(2,1)S(1)}, bf16[4,64,256]{2,1,0:T(8,128)(2,1)S(1)}, u32[]{:S(2)}, u32[]{:S(2)}) collective-permute-start(bf16[4,64,256]{2,1,0:T(8,128)(2,1)S(1)} %get-tuple-element.61), channel_id=1, source_target_pairs={{0,12},{1,13},{4,8},{5,9},{8,4},{9,5},{12,0},{13,1},{2,14},{3,15},... | collective-permute-start | bytes 393224 | tf_op jit(solution)/shard_map/ppermute | solution.py:239
  35.0 0.4 collective-permute-done.14.refs_12_
  35.4 4.0 %collective-permute-start.5 = (bf16[4,64,256]{2,1,0:T(8,128)(2,1)S(1)}, bf16[4,64,256]{2,1,0:T(8,128)(2,1)S(1)}, u32[]{:S(2)}, u32[]{:S(2)}) collective-permute-start(bf16[4,64,256]{2,1,0:T(8,128)(2,1)S(1)} %get-tuple-element.63), channel_id=1, source_target_pairs={{0,9},{1,8},{4,13},{5,12},{8,1},{9,0},{12,5},{13,4},{2,11},{3,10},... | collective-permute-start | bytes 393224 | tf_op jit(solution)/shard_map/ppermute | solution.py:239
  39.4 3.2 %collective-permute-start.6 = (bf16[4,64,256]{2,1,0:T(8,128)(2,1)S(1)}, bf16[4,64,256]{2,1,0:T(8,128)(2,1)S(1)}, u32[]{:S(2)}, u32[]{:S(2)}) collective-permute-start(bf16[4,64,256]{2,1,0:T(8,128)(2,1)S(1)} %get-tuple-element.64), channel_id=1, source_target_pairs={{0,1},{1,0},{4,5},{5,4},{8,9},{9,8},{12,13},{13,12},{2,3},{3,2},{6... | collective-permute-start | bytes 393224 | tf_op jit(solution)/shard_map/ppermute | solution.py:239
  42.6 0.6 copy-done.2
  43.2 0.0 copy-done.3
  43.3 5.9 %grads.2 = (bf16[3,64,512]{2,1,0:T(8,128)(2,1)S(1)}, bf16[3,64,512]{2,1,0:T(8,128)(2,1)S(1)}, bf16[3,64,512]{2,1,0:T(8,128)(2,1)S(1)}, bf16[3,64,512]{2,1,0:T(8,...) custom-call(s32[2]{0:T(128)S(1)} %pad_add_fusion.place, ...), custom_call_target="tpu_custom_call" | custom-call | flops 10737418240 | bytes 1835008 | tf_op jit(solution)/shard_map/grads/pallas_call | solution.py:265
  49.2 2.8 %collective-permute-done.5.refs_10_.refs_6_ = bf16[4,64,256]{2,1,0:T(8,128)(2,1)S(1)} collective-permute-done((bf16[4,64,256]{2,1,0:T(8,128)(2,1)S(1)}, bf16[4,64,256]{2,1,0:T(8,128)(2,1)S(1)}, u32[]{:S(2)}, u32[]{:S(2)}) %collective-permute-start.5) | collective-permute-done | bytes 131104 | tf_op jit(solution)/shard_map/ppermute | solution.py:239
  52.0 1.8 %collective-permute-start.15 = (bf16[3,64,256]{2,1,0:T(8,128)(2,1)S(1)}, bf16[3,64,256]{2,1,0:T(8,128)(2,1)S(1)}, u32[]{:S(2)}, u32[]{:S(2)}) collective-permute-start(bf16[3,64,256]{2,1,0:T(8,128)(2,1)S(1)} %get-tuple-element.91), channel_id=1, source_target_pairs={{0,13},{1,12},{4,9},{5,8},{8,5},{9,4},{12,1},{13,0},{2,15},{3,14},... | collective-permute-start | bytes 294920 | tf_op jit(solution)/shard_map/ppermute | solution.py:239
  53.8 1.8 %collective-permute-start.20 = (bf16[3,64,256]{2,1,0:T(8,128)(2,1)S(1)}, bf16[3,64,256]{2,1,0:T(8,128)(2,1)S(1)}, u32[]{:S(2)}, u32[]{:S(2)}) collective-permute-start(bf16[3,64,256]{2,1,0:T(8,128)(2,1)S(1)} %get-tuple-element.96), channel_id=1, source_target_pairs={{0,12},{1,13},{4,8},{5,9},{8,4},{9,5},{12,0},{13,1},{2,14},{3,15},... | collective-permute-start | bytes 294920 | tf_op jit(solution)/shard_map/ppermute | solution.py:239
  55.5 0.5 collective-permute-start.16
  56.1 5.9 %grads.3 = (bf16[3,64,512]{2,1,0:T(8,128)(2,1)S(1)}, bf16[3,64,512]{2,1,0:T(8,128)(2,1)S(1)}, bf16[3,64,512]{2,1,0:T(8,128)(2,1)S(1)}, bf16[3,64,512]{2,1,0:T(8,...) custom-call(s32[2]{0:T(128)S(1)} %pad_add_fusion.place, ...), custom_call_target="tpu_custom_call", output_to_operand_aliasing={{0}: (18, {}), {1}: (19, {}), {2}: (20, {}), {3}: (21, {}),... | custom-call | flops 10737418240 | bytes 1835008 | tf_op jit(solution)/shard_map/grads/pallas_call | solution.py:265
  62.0 1.9 %collective-permute-done.16.refs_11_ = bf16[2,256,256]{2,1,0:T(8,128)(2,1)S(1)} collective-permute-done((bf16[2,256,256]{2,1,0:T(8,128)(2,1)S(1)}, bf16[2,256,256]{2,1,0:T(8,128)(2,1)S(1)}, u32[]{:S(2)}, u32[]{:S(2)}) %collective-permute-start.16) | collective-permute-done | bytes 262176 | tf_op jit(solution)/shard_map/ppermute | solution.py:239
  63.9 0.5 collective-permute-start.25
  64.4 1.7 %collective-permute-start.21 = (bf16[3,64,256]{2,1,0:T(8,128)(2,1)S(1)}, bf16[3,64,256]{2,1,0:T(8,128)(2,1)S(1)}, u32[]{:S(2)}, u32[]{:S(2)}) collective-permute-start(bf16[3,64,256]{2,1,0:T(8,128)(2,1)S(1)} %get-tuple-element.98), channel_id=1, source_target_pairs={{0,13},{1,12},{4,9},{5,8},{8,5},{9,4},{12,1},{13,0},{2,15},{3,14},... | collective-permute-start | bytes 294920 | tf_op jit(solution)/shard_map/ppermute | solution.py:239
  66.1 0.9 %collective-permute-start.22 = (bf16[3,64,256]{2,1,0:T(8,128)(2,1)S(1)}, bf16[3,64,256]{2,1,0:T(8,128)(2,1)S(1)}, u32[]{:S(2)}, u32[]{:S(2)}) collective-permute-start(bf16[3,64,256]{2,1,0:T(8,128)(2,1)S(1)} %get-tuple-element.99), channel_id=1, source_target_pairs={{0,12},{1,13},{4,8},{5,9},{8,4},{9,5},{12,0},{13,1},{2,14},{3,15},... | collective-permute-start | bytes 294920 | tf_op jit(solution)/shard_map/ppermute | solution.py:239
  67.0 3.2 %collective-permute-start.24 = (bf16[3,64,512]{2,1,0:T(8,128)(2,1)S(1)}, bf16[3,64,512]{2,1,0:T(8,128)(2,1)S(1)}, u32[]{:S(2)}, u32[]{:S(2)}) collective-permute-start(bf16[3,64,512]{2,1,0:T(8,128)(2,1)S(1)} %get-tuple-element.101), channel_id=1, source_target_pairs={{0,5},{1,4},{4,1},{5,0},{8,13},{9,12},{12,9},{13,8},{2,7},{3,6},{6... | collective-permute-start | bytes 589832 | tf_op jit(solution)/shard_map/ppermute | solution.py:239
  70.2 0.1 convert_add_fusion.1
  70.3 0.4 collective-permute-done.21.refs_3_
  70.6 0.3 collective-permute-start.17
  71.0 2.8 %collective-permute-done.22.refs_4_ = bf16[3,64,256]{2,1,0:T(8,128)(2,1)S(1)} collective-permute-done((bf16[3,64,256]{2,1,0:T(8,128)(2,1)S(1)}, bf16[3,64,256]{2,1,0:T(8,128)(2,1)S(1)}, u32[]{:S(2)}, u32[]{:S(2)}) %collective-permute-start.22) | collective-permute-done | bytes 98336 | tf_op jit(solution)/shard_map/ppermute | solution.py:239
  73.7 0.8 collective-permute-start.18
  74.6 6.3 %collective-permute-done.23.refs_5_ = bf16[3,64,512]{2,1,0:T(8,128)(2,1)S(1)} collective-permute-done((bf16[3,64,512]{2,1,0:T(8,128)(2,1)S(1)}, bf16[3,64,512]{2,1,0:T(8,128)(2,1)S(1)}, u32[]{:S(2)}, u32[]{:S(2)}) %collective-permute-start.23) | collective-permute-done | bytes 196640 | tf_op jit(solution)/shard_map/ppermute | solution.py:239
  80.9 1.2 %collective-permute-start.19 = (bf16[3,64,512]{2,1,0:T(8,128)(2,1)S(1)}, bf16[3,64,512]{2,1,0:T(8,128)(2,1)S(1)}, u32[]{:S(2)}, u32[]{:S(2)}) collective-permute-start(bf16[3,64,512]{2,1,0:T(8,128)(2,1)S(1)} %get-tuple-element.95), channel_id=1, source_target_pairs={{0,1},{1,0},{4,5},{5,4},{8,9},{9,8},{12,13},{13,12},{2,3},{3,2},{6... | collective-permute-start | bytes 589832 | tf_op jit(solution)/shard_map/ppermute | solution.py:239
  82.1 1.7 %unpack.2 = (bf16[64,4096]{1,0:T(8,128)(2,1)}, bf16[64,4096]{1,0:T(8,128)(2,1)}, bf16[64,4096]{1,0:T(8,128)(2,1)}) custom-call(s32[2]{0:T(128)S(1)} %pad_add_fusion.place, bf16[3,64,256]{2,1,0:T(8,128)(2,1)S(1)} %collective-permute-done.15.refs_10_.refs_0_, bf16[3,64,256]{2,1,0:T(8,128)(2,1)S(1)} %collective-permute-done.20.refs_1_, ...), custom_call_target="tpu_custom_call" | custom-call | tf_op jit(solution)/shard_map/unpack/pallas_call | solution.py:317
  83.8 0.1 convert_add_fusion
  83.8 0.1 fusion.2
  84.0 0.0 copy-start
  84.0 0.0 copy-start.1
  84.0 5.9 %collective-permute-done.17.refs_0_ = bf16[3,64,512]{2,1,0:T(8,128)(2,1)S(1)} collective-permute-done((bf16[3,64,512]{2,1,0:T(8,128)(2,1)S(1)}, bf16[3,64,512]{2,1,0:T(8,128)(2,1)S(1)}, u32[]{:S(2)}, u32[]{:S(2)}) %collective-permute-start.17) | collective-permute-done | bytes 196640 | tf_op jit(solution)/shard_map/ppermute | solution.py:239
  89.9 1.4 %unpack.3 = (bf16[64,4096]{1,0:T(8,128)(2,1)}, bf16[64,4096]{1,0:T(8,128)(2,1)}, bf16[64,4096]{1,0:T(8,128)(2,1)}) custom-call(s32[2]{0:T(128)S(1)} %pad_add_fusion.place, bf16[3,64,512]{2,1,0:T(8,128)(2,1)S(1)} %collective-permute-done.17.refs_0_, ...), custom_call_target="tpu_custom_call", output_to_operand_aliasing={{0}: (4, {}), {1}: (5, {}), {2}: (6, {})} | custom-call | tf_op jit(solution)/shard_map/unpack/pallas_call | solution.py:317
  (27 shorter events, 0.1 us)
Async XLA Ops:
  3.0 39.6 %collective-permute-start.8 = (bf16[2,256,512]{2,1,0:T(8,128)(2,1)S(1)}, bf16[2,256,512]{2,1,0:T(8,128)(2,1)S(1)}, u32[]{:S(2)}, u32[]{:S(2)}) collective-permute-start(bf16[2,256,512]{2,1,0:T(8,128)(2,1)S(1)} %get-tuple-element.66), channel_id=1, source_target_pairs={{0,2},{2,0},{1,3},{3,1},{4,6},{6,4},{5,7},{7,5},{8,10},{10,8},{9,1... | collective-permute-start | bytes 1572872 | tf_op jit(solution)/shard_map/ppermute | solution.py:239
  6.0 7.5 %collective-permute-start = (bf16[4,64,256]{2,1,0:T(8,128)(2,1)S(1)}, bf16[4,64,256]{2,1,0:T(8,128)(2,1)S(1)}, u32[]{:S(2)}, u32[]{:S(2)}) collective-permute-start(bf16[4,64,256]{2,1,0:T(8,128)(2,1)S(1)} %get-tuple-element.58), channel_id=1, source_target_pairs={{0,13},{1,12},{4,9},{5,8},{8,5},{9,4},{12,1},{13,0},{2,15},{3,14},... | collective-permute-start | bytes 393224 | tf_op jit(solution)/shard_map/ppermute | solution.py:239
  8.7 9.6 %collective-permute-start.9 = (bf16[4,64,256]{2,1,0:T(8,128)(2,1)S(1)}, bf16[4,64,256]{2,1,0:T(8,128)(2,1)S(1)}, u32[]{:S(2)}, u32[]{:S(2)}) collective-permute-start(bf16[4,64,256]{2,1,0:T(8,128)(2,1)S(1)} %get-tuple-element.67), channel_id=1, source_target_pairs={{0,5},{1,4},{4,1},{5,0},{8,13},{9,12},{12,9},{13,8},{2,7},{3,6},{6... | collective-permute-start | bytes 393224 | tf_op jit(solution)/shard_map/ppermute | solution.py:239
  8.9 10.7 %collective-permute-start.10 = (bf16[4,64,256]{2,1,0:T(8,128)(2,1)S(1)}, bf16[4,64,256]{2,1,0:T(8,128)(2,1)S(1)}, u32[]{:S(2)}, u32[]{:S(2)}) collective-permute-start(bf16[4,64,256]{2,1,0:T(8,128)(2,1)S(1)} %get-tuple-element.68), channel_id=1, source_target_pairs={{0,12},{1,13},{4,8},{5,9},{8,4},{9,5},{12,0},{13,1},{2,14},{3,15},... | collective-permute-start | bytes 393224 | tf_op jit(solution)/shard_map/ppermute | solution.py:239
  10.2 12.9 %collective-permute-start.11 = (bf16[4,64,256]{2,1,0:T(8,128)(2,1)S(1)}, bf16[4,64,256]{2,1,0:T(8,128)(2,1)S(1)}, u32[]{:S(2)}, u32[]{:S(2)}) collective-permute-start(bf16[4,64,256]{2,1,0:T(8,128)(2,1)S(1)} %get-tuple-element.69), channel_id=1, source_target_pairs={{0,4},{1,5},{4,0},{5,1},{8,12},{9,13},{12,8},{13,9},{2,6},{3,7},{6... | collective-permute-start | bytes 393224 | tf_op jit(solution)/shard_map/ppermute | solution.py:239
  13.5 18.8 %collective-permute-start.12 = (bf16[4,64,256]{2,1,0:T(8,128)(2,1)S(1)}, bf16[4,64,256]{2,1,0:T(8,128)(2,1)S(1)}, u32[]{:S(2)}, u32[]{:S(2)}) collective-permute-start(bf16[4,64,256]{2,1,0:T(8,128)(2,1)S(1)} %get-tuple-element.70), channel_id=1, source_target_pairs={{0,9},{1,8},{4,13},{5,12},{8,1},{9,0},{12,5},{13,4},{2,11},{3,10},... | collective-permute-start | bytes 393224 | tf_op jit(solution)/shard_map/ppermute | solution.py:239
  18.3 14.1 %collective-permute-start.13 = (bf16[4,64,256]{2,1,0:T(8,128)(2,1)S(1)}, bf16[4,64,256]{2,1,0:T(8,128)(2,1)S(1)}, u32[]{:S(2)}, u32[]{:S(2)}) collective-permute-start(bf16[4,64,256]{2,1,0:T(8,128)(2,1)S(1)} %get-tuple-element.71), channel_id=1, source_target_pairs={{0,1},{1,0},{4,5},{5,4},{8,9},{9,8},{12,13},{13,12},{2,3},{3,2},{6... | collective-permute-start | bytes 393224 | tf_op jit(solution)/shard_map/ppermute | solution.py:239
  19.5 12.8 %copy-start.4 = (s32[1,4,3]{1,0,2:T(1,128)S(1)}, s32[1,4,3]{1,0,2:T(1,128)}, u32[]{:S(2)}) copy-start(s32[1,4,3]{1,0,2:T(1,128)} %param.15) | copy-start | bytes 148
  19.5 15.8 %collective-permute-start.14 = (bf16[4,64,256]{2,1,0:T(8,128)(2,1)S(1)}, bf16[4,64,256]{2,1,0:T(8,128)(2,1)S(1)}, u32[]{:S(2)}, u32[]{:S(2)}) collective-permute-start(bf16[4,64,256]{2,1,0:T(8,128)(2,1)S(1)} %get-tuple-element.72), channel_id=1, source_target_pairs={{0,8},{1,9},{4,12},{5,13},{8,0},{9,1},{12,4},{13,5},{2,10},{3,11},... | collective-permute-start | bytes 393224 | tf_op jit(solution)/shard_map/ppermute | solution.py:239
  23.1 12.3 %collective-permute-start.1 = (bf16[4,64,256]{2,1,0:T(8,128)(2,1)S(1)}, bf16[4,64,256]{2,1,0:T(8,128)(2,1)S(1)}, u32[]{:S(2)}, u32[]{:S(2)}) collective-permute-start(bf16[4,64,256]{2,1,0:T(8,128)(2,1)S(1)} %get-tuple-element.59), channel_id=1, source_target_pairs={{0,13},{1,12},{4,9},{5,8},{8,5},{9,4},{12,1},{13,0},{2,15},{3,14},... | collective-permute-start | bytes 393224 | tf_op jit(solution)/shard_map/ppermute | solution.py:239
  32.3 7.0 %collective-permute-start.2 = (bf16[4,64,256]{2,1,0:T(8,128)(2,1)S(1)}, bf16[4,64,256]{2,1,0:T(8,128)(2,1)S(1)}, u32[]{:S(2)}, u32[]{:S(2)}) collective-permute-start(bf16[4,64,256]{2,1,0:T(8,128)(2,1)S(1)} %get-tuple-element.60), channel_id=1, source_target_pairs={{0,5},{1,4},{4,1},{5,0},{8,13},{9,12},{12,9},{13,8},{2,7},{3,6},{6... | collective-permute-start | bytes 393224 | tf_op jit(solution)/shard_map/ppermute | solution.py:239
  32.4 16.8 %collective-permute-start.3 = (bf16[4,64,256]{2,1,0:T(8,128)(2,1)S(1)}, bf16[4,64,256]{2,1,0:T(8,128)(2,1)S(1)}, u32[]{:S(2)}, u32[]{:S(2)}) collective-permute-start(bf16[4,64,256]{2,1,0:T(8,128)(2,1)S(1)} %get-tuple-element.61), channel_id=1, source_target_pairs={{0,12},{1,13},{4,8},{5,9},{8,4},{9,5},{12,0},{13,1},{2,14},{3,15},... | collective-permute-start | bytes 393224 | tf_op jit(solution)/shard_map/ppermute | solution.py:239
  35.4 13.8 %collective-permute-start.4 = (bf16[4,64,256]{2,1,0:T(8,128)(2,1)S(1)}, bf16[4,64,256]{2,1,0:T(8,128)(2,1)S(1)}, u32[]{:S(2)}, u32[]{:S(2)}) collective-permute-start(bf16[4,64,256]{2,1,0:T(8,128)(2,1)S(1)} %get-tuple-element.62), channel_id=1, source_target_pairs={{0,4},{1,5},{4,0},{5,1},{8,12},{9,13},{12,8},{13,9},{2,6},{3,7},{6... | collective-permute-start | bytes 393224 | tf_op jit(solution)/shard_map/ppermute | solution.py:239
  35.4 16.6 %collective-permute-start.5 = (bf16[4,64,256]{2,1,0:T(8,128)(2,1)S(1)}, bf16[4,64,256]{2,1,0:T(8,128)(2,1)S(1)}, u32[]{:S(2)}, u32[]{:S(2)}) collective-permute-start(bf16[4,64,256]{2,1,0:T(8,128)(2,1)S(1)} %get-tuple-element.63), channel_id=1, source_target_pairs={{0,9},{1,8},{4,13},{5,12},{8,1},{9,0},{12,5},{13,4},{2,11},{3,10},... | collective-permute-start | bytes 393224 | tf_op jit(solution)/shard_map/ppermute | solution.py:239
  39.4 16.7 %collective-permute-start.6 = (bf16[4,64,256]{2,1,0:T(8,128)(2,1)S(1)}, bf16[4,64,256]{2,1,0:T(8,128)(2,1)S(1)}, u32[]{:S(2)}, u32[]{:S(2)}) collective-permute-start(bf16[4,64,256]{2,1,0:T(8,128)(2,1)S(1)} %get-tuple-element.64), channel_id=1, source_target_pairs={{0,1},{1,0},{4,5},{5,4},{8,9},{9,8},{12,13},{13,12},{2,3},{3,2},{6... | collective-permute-start | bytes 393224 | tf_op jit(solution)/shard_map/ppermute | solution.py:239
  42.6 13.5 %collective-permute-start.7 = (bf16[4,64,256]{2,1,0:T(8,128)(2,1)S(1)}, bf16[4,64,256]{2,1,0:T(8,128)(2,1)S(1)}, u32[]{:S(2)}, u32[]{:S(2)}) collective-permute-start(bf16[4,64,256]{2,1,0:T(8,128)(2,1)S(1)} %get-tuple-element.65), channel_id=1, source_target_pairs={{0,8},{1,9},{4,12},{5,13},{8,0},{9,1},{12,4},{13,5},{2,10},{3,11},... | collective-permute-start | bytes 393224 | tf_op jit(solution)/shard_map/ppermute | solution.py:239
  42.6 0.7 copy-start.2
  42.6 0.7 copy-start.3
  52.0 10.0 %collective-permute-start.15 = (bf16[3,64,256]{2,1,0:T(8,128)(2,1)S(1)}, bf16[3,64,256]{2,1,0:T(8,128)(2,1)S(1)}, u32[]{:S(2)}, u32[]{:S(2)}) collective-permute-start(bf16[3,64,256]{2,1,0:T(8,128)(2,1)S(1)} %get-tuple-element.91), channel_id=1, source_target_pairs={{0,13},{1,12},{4,9},{5,8},{8,5},{9,4},{12,1},{13,0},{2,15},{3,14},... | collective-permute-start | bytes 294920 | tf_op jit(solution)/shard_map/ppermute | solution.py:239
  53.8 13.3 %collective-permute-start.20 = (bf16[3,64,256]{2,1,0:T(8,128)(2,1)S(1)}, bf16[3,64,256]{2,1,0:T(8,128)(2,1)S(1)}, u32[]{:S(2)}, u32[]{:S(2)}) collective-permute-start(bf16[3,64,256]{2,1,0:T(8,128)(2,1)S(1)} %get-tuple-element.96), channel_id=1, source_target_pairs={{0,12},{1,13},{4,8},{5,9},{8,4},{9,5},{12,0},{13,1},{2,14},{3,15},... | collective-permute-start | bytes 294920 | tf_op jit(solution)/shard_map/ppermute | solution.py:239
  55.5 8.4 %collective-permute-start.16 = (bf16[2,256,256]{2,1,0:T(8,128)(2,1)S(1)}, bf16[2,256,256]{2,1,0:T(8,128)(2,1)S(1)}, u32[]{:S(2)}, u32[]{:S(2)}) collective-permute-start(bf16[2,256,256]{2,1,0:T(8,128)(2,1)S(1)} %get-tuple-element.92), channel_id=1, source_target_pairs={{0,2},{2,0},{1,3},{3,1},{4,6},{6,4},{5,7},{7,5},{8,10},{10,8},{9,1... | collective-permute-start | bytes 786440 | tf_op jit(solution)/shard_map/ppermute | solution.py:239
  63.9 19.9 %collective-permute-start.25 = (bf16[2,256,256]{2,1,0:T(8,128)(2,1)S(1)}, bf16[2,256,256]{2,1,0:T(8,128)(2,1)S(1)}, u32[]{:S(2)}, u32[]{:S(2)}) collective-permute-start(bf16[2,256,256]{2,1,0:T(8,128)(2,1)S(1)} %get-tuple-element.107), channel_id=1, source_target_pairs={{0,2},{2,0},{1,3},{3,1},{4,6},{6,4},{5,7},{7,5},{8,10},{10,8},{9,1... | collective-permute-start | bytes 786440 | tf_op jit(solution)/shard_map/ppermute | solution.py:239
  64.4 6.2 %collective-permute-start.21 = (bf16[3,64,256]{2,1,0:T(8,128)(2,1)S(1)}, bf16[3,64,256]{2,1,0:T(8,128)(2,1)S(1)}, u32[]{:S(2)}, u32[]{:S(2)}) collective-permute-start(bf16[3,64,256]{2,1,0:T(8,128)(2,1)S(1)} %get-tuple-element.98), channel_id=1, source_target_pairs={{0,13},{1,12},{4,9},{5,8},{8,5},{9,4},{12,1},{13,0},{2,15},{3,14},... | collective-permute-start | bytes 294920 | tf_op jit(solution)/shard_map/ppermute | solution.py:239
  66.1 7.6 %collective-permute-start.22 = (bf16[3,64,256]{2,1,0:T(8,128)(2,1)S(1)}, bf16[3,64,256]{2,1,0:T(8,128)(2,1)S(1)}, u32[]{:S(2)}, u32[]{:S(2)}) collective-permute-start(bf16[3,64,256]{2,1,0:T(8,128)(2,1)S(1)} %get-tuple-element.99), channel_id=1, source_target_pairs={{0,12},{1,13},{4,8},{5,9},{8,4},{9,5},{12,0},{13,1},{2,14},{3,15},... | collective-permute-start | bytes 294920 | tf_op jit(solution)/shard_map/ppermute | solution.py:239
  67.0 13.9 %collective-permute-start.23 = (bf16[3,64,512]{2,1,0:T(8,128)(2,1)S(1)}, bf16[3,64,512]{2,1,0:T(8,128)(2,1)S(1)}, u32[]{:S(2)}, u32[]{:S(2)}) collective-permute-start(bf16[3,64,512]{2,1,0:T(8,128)(2,1)S(1)} %get-tuple-element.100), channel_id=1, source_target_pairs={{0,9},{1,8},{4,13},{5,12},{8,1},{9,0},{12,5},{13,4},{2,11},{3,10},... | collective-permute-start | bytes 589832 | tf_op jit(solution)/shard_map/ppermute | solution.py:239
  67.0 15.1 %collective-permute-start.24 = (bf16[3,64,512]{2,1,0:T(8,128)(2,1)S(1)}, bf16[3,64,512]{2,1,0:T(8,128)(2,1)S(1)}, u32[]{:S(2)}, u32[]{:S(2)}) collective-permute-start(bf16[3,64,512]{2,1,0:T(8,128)(2,1)S(1)} %get-tuple-element.101), channel_id=1, source_target_pairs={{0,5},{1,4},{4,1},{5,0},{8,13},{9,12},{12,9},{13,8},{2,7},{3,6},{6... | collective-permute-start | bytes 589832 | tf_op jit(solution)/shard_map/ppermute | solution.py:239
  70.6 19.2 %collective-permute-start.17 = (bf16[3,64,512]{2,1,0:T(8,128)(2,1)S(1)}, bf16[3,64,512]{2,1,0:T(8,128)(2,1)S(1)}, u32[]{:S(2)}, u32[]{:S(2)}) collective-permute-start(bf16[3,64,512]{2,1,0:T(8,128)(2,1)S(1)} %get-tuple-element.93), channel_id=1, source_target_pairs={{0,4},{1,5},{4,0},{5,1},{8,12},{9,13},{12,8},{13,9},{2,6},{3,7},{6... | collective-permute-start | bytes 589832 | tf_op jit(solution)/shard_map/ppermute | solution.py:239
  73.7 16.1 %collective-permute-start.18 = (bf16[3,64,512]{2,1,0:T(8,128)(2,1)S(1)}, bf16[3,64,512]{2,1,0:T(8,128)(2,1)S(1)}, u32[]{:S(2)}, u32[]{:S(2)}) collective-permute-start(bf16[3,64,512]{2,1,0:T(8,128)(2,1)S(1)} %get-tuple-element.94), channel_id=1, source_target_pairs={{0,8},{1,9},{4,12},{5,13},{8,0},{9,1},{12,4},{13,5},{2,10},{3,11},... | collective-permute-start | bytes 589832 | tf_op jit(solution)/shard_map/ppermute | solution.py:239
  80.9 9.0 %collective-permute-start.19 = (bf16[3,64,512]{2,1,0:T(8,128)(2,1)S(1)}, bf16[3,64,512]{2,1,0:T(8,128)(2,1)S(1)}, u32[]{:S(2)}, u32[]{:S(2)}) collective-permute-start(bf16[3,64,512]{2,1,0:T(8,128)(2,1)S(1)} %get-tuple-element.95), channel_id=1, source_target_pairs={{0,1},{1,0},{4,5},{5,4},{8,9},{9,8},{12,13},{13,12},{2,3},{3,2},{6... | collective-permute-start | bytes 589832 | tf_op jit(solution)/shard_map/ppermute | solution.py:239
  84.0 7.3 %copy-start = (f32[256,512]{1,0:T(8,128)}, f32[256,512]{1,0:T(8,128)S(1)}, u32[]{:S(2)}) copy-start(f32[256,512]{1,0:T(8,128)S(1)} %get-tuple-element.111.refs_7_) | copy-start | bytes 1572868
  84.0 7.3 %copy-start.1 = (f32[256,512]{1,0:T(8,128)}, f32[256,512]{1,0:T(8,128)S(1)}, u32[]{:S(2)}) copy-start(f32[256,512]{1,0:T(8,128)S(1)} %get-tuple-element.112.refs_6_) | copy-start | bytes 1572868

commit v4 on v3

--- a/solution.py
+++ b/solution.py
@@ -14,6 +14,7 @@
 EARLY = 2
 EHOLD = 5
 TAIL = 3
+FIRST = 1
 TOKENS = ("seq", "rep")
 ANY = pl.BlockSpec(memory_space=pl.ANY)
 SMEM = pl.BlockSpec(memory_space=pltpu.SMEM)
@@ -43,7 +44,11 @@
             )
     if with_gauges:
         for a in range(2):
-            copies.append(pltpu.make_async_copy(gauges[a], refs[-3].at[a], gauge_sems.at[a]))
+            copies.append(
+                pltpu.make_async_copy(
+                    gauges[a].at[:, pl.ds(off, width)], refs[-3].at[a], gauge_sems.at[a]
+                )
+            )
     run_copies(copies)
 
 
@@ -98,7 +103,7 @@
     for at, k in enumerate(gauge_order):
         copies.append(
             pltpu.make_async_copy(
-                gauge_recvs[at].at[:, :, pl.ds(off, width)],
+                gauge_recvs[at],
                 gau.at[
                     :, pl.ds(pl.multiple_of((gauge_me ^ k) * gauge_rows, gauge_rows), gauge_rows), :
                 ],
@@ -230,7 +235,9 @@
     gauge_me = lax.axis_index("head").astype(jnp.int32)
     place = jnp.stack([me, gauge_me])
     half = total // 2
-    order = tuple(k for i in range(half) for k in (total - 1 - i, half - 1 - i) if k)
+    far, near = list(range(total - 1, half - 1, -1)), list(range(half - 1, -1, -1))
+    far[:2] = far[1::-1]
+    order = tuple(k for pair in zip(far, near) for k in pair if k)
     gauge_order = tuple(range(1, head_total))
     lists = (block_keys[0], block_count[0], gauge_block[0])
     params = pltpu.CompilerParams(vmem_limit_bytes=VMEM_LIMIT)
@@ -244,7 +251,7 @@
         off, width = chunk
         shapes = [jax.ShapeDtypeStruct((4, rows, width), bf16)] * len(part)
         if with_gauges:
-            shapes.append(jax.ShapeDtypeStruct((2, gauge_rows, columns), bf16))
+            shapes.append(jax.ShapeDtypeStruct((2, gauge_rows, width), bf16))
         return pl.pallas_call(
             functools.partial(
                 pack_kernel, off, width, columns, part, len(after), with_gauges
@@ -253,14 +260,14 @@
             in_specs=[SMEM] + [ANY] * (6 + len(after)),
             out_specs=[ANY] * len(shapes),
             scratch_shapes=[
-                pltpu.SemaphoreType.DMA((len(part), 4)),
+                pltpu.SemaphoreType.DMA((max(len(part), 1), 4)),
                 pltpu.SemaphoreType.DMA((2,)),
             ],
             compiler_params=params,
             name="pack",
         )(place, *arrays, gauge_key, gauge_value, *after)
 
-    def grads(chunk, recvs, targets, held):
+    def grads(chunk, recvs, gauge_recvs, targets, held):
         off, width = chunk
         return pl.pallas_call(
             functools.partial(
@@ -329,19 +336,21 @@
         return [swap(s, TOKENS, total, k) for s, k in zip(packed, part)]
 
     single = len(chunks) == 1
-    *packed, gauge_send = pack(chunks[0], order, [], True)
-    gauge_recvs = [swap(gauge_send, "head", head_total, k) for k in gauge_order]
+    packed = list(pack(chunks[0], order[:FIRST], [], False))
+    packed += pack(chunks[0], order[FIRST:], packed[:1], False)
     recvs = send(packed, order)
-    early = () if single else order[0 : 2 * EARLY : 2]
-    far, near = order[0::2], order[1::2]
-    whole = (*far[2:3], *near[:2], *far[3:], *near[2:]) if early else order
+    early = () if single else tuple(far[:EARLY])
+    rest = [k for k in near if k]
+    whole = (*far[2:3], *rest[:2], *far[3:], *rest[2:]) if early else order
     targets = tuple((k, True) for k in (0, *whole)) + tuple((k, False) for k in early)
     merged, parts, gauge_sums, back_early = [], [], [], []
     for at, chunk in enumerate(chunks):
         ahead = []
         if at + 1 < len(chunks):
             ahead = send(pack(chunks[at + 1], order, recvs[:1], False), order)
-        out = grads(chunk, recvs, targets, merged)
+        (gauge_send,) = pack(chunk, (), [], True)
+        gauge_recvs = [swap(gauge_send, "head", head_total, k) for k in gauge_order]
+        out = grads(chunk, recvs, gauge_recvs, targets, merged)
         if gauge_sums:
             out = hold(out, back_early[:1] + gauge_back)
         merged, cut = list(out[: 1 + len(whole)]), out[1 + len(whole) : total]

time: 91.7 us -> 90.5 us (0.987)
  waiting for transfers between devices: 32.5 us -> 20.4 us
  starting transfers between devices: 37.8 us -> 44.3 us
  Pallas kernels: 19.1 us -> 23.3 us
    ppermute x26 -> x27, waiting for transfers between devices: 32.5 us -> 20.4 us  [swap(): return lax.ppermute(x, axis, [(i, i ^ k) for i in range(size)])]
    ppermute x26 -> x27, starting transfers between devices: 37.8 us -> 44.3 us  [swap(): return lax.ppermute(x, axis, [(i, i ^ k) for i in range(size)])]
    pallas_call x2 -> x5, Pallas kernels: 4.2 us -> 8.33 us  [pack(): pl.pallas_call(functools.partial(pack_kernel, off, width, columns, part,...]
  transfers between devices with their start and end apart: 26 -> 27, of which waited for: 11 -> 10; matrix products, arithmetic and copies ran while one was open for 0% -> 0% of each run, Pallas kernels for 17% -> 23%
where the time goes in v4:
time: 90.5 us; the launch traced here: 89.9 us
  starting transfers between devices  44.3 us (49%)
  Pallas kernels  23.3 us (26%)
  waiting for transfers between devices  20.4 us (23%)
    ppermute x27, starting transfers between devices, swap(): return lax.ppermute(x, axis, [(i, i ^ k) for i in range(size)])  44.3 us
    ppermute x27, waiting for transfers between devices, swap(): return lax.ppermute(x, axis, [(i, i ^ k) for i in range(size)])  20.4 us
    pallas_call x2, Pallas kernels, grads(): pl.pallas_call(functools.partial(grads_kernel, off, width, columns, order...  11.8 us
    pallas_call x5, Pallas kernels, pack(): pl.pallas_call(functools.partial(pack_kernel, off, width, columns, part,...  8.33 us
    pallas_call x2, Pallas kernels, unpack(): pl.pallas_call(functools.partial(unpack_kernel, columns, [part[1:] for pa...  3.08 us
  transfers between devices with their start and end apart: 27, of which 10 were waited for; matrix products, arithmetic and copies ran while one was open for 0% of the time, Pallas kernels for 23%

profile of v4, /device:TPU:0, one launch (start us, length us, event | category | flops | bytes accessed | tf_op | source)
XLA Modules:
  0.0 89.9 jit_solution(14078097728991239033)
XLA Ops:
  0.6 0.1 pad_add_fusion.place
  0.7 1.4 %pack.5.refs_6_ = bf16[4,64,256]{2,1,0:T(8,128)(2,1)S(1)} custom-call(s32[2]{0:T(128)S(1)} %pad_add_fusion.place, bf16[64,4096]{1,0:T(8,128)(2,1)} %bitcast.22, bf16[64,4096]{1,0:T(8,128)(2,1)} %bitcast.29, bf16[64,4096]{1,0:T(8,128)(2,1)} %bitcast.36, bf16[64,4096]{1,0:T(8,128)(2,1)} %bitcast.43, bf16[256,512]{1,0:T(8,128)(2,1)} %refs_4_.13, ...), custom_call_target="tpu_custom_call" | custom-call | tf_op jit(solution)/shard_map/pack/pallas_call | solution.py:255
  2.1 5.1 %collective-permute-start = (bf16[4,64,256]{2,1,0:T(8,128)(2,1)S(1)}, bf16[4,64,256]{2,1,0:T(8,128)(2,1)S(1)}, u32[]{:S(2)}, u32[]{:S(2)}) collective-permute-start(bf16[4,64,256]{2,1,0:T(8,128)(2,1)S(1)} %pack.5.refs_6_), channel_id=1, source_target_pairs={{0,12},{1,13},{4,8},{5,9},{8,4},{9,5},{12,0},{13,1},{2,14},{3,15},... | collective-permute-start | bytes 393224 | tf_op jit(solution)/shard_map/ppermute | solution.py:246
  7.2 1.9 %pack.8 = (bf16[4,64,256]{2,1,0:T(8,128)(2,1)S(1)}, bf16[4,64,256]{2,1,0:T(8,128)(2,1)S(1)}, bf16[4,64,256]{2,1,0:T(8,128)(2,1)S(1)}, bf16[4,64,256]{2,1,0:T(8,1...) custom-call(s32[2]{0:T(128)S(1)} %pad_add_fusion.place, bf16[64,4096]{1,0:T(8,128)(2,1)} %bitcast.23, ...), custom_call_target="tpu_custom_call" | custom-call | tf_op jit(solution)/shard_map/pack/pallas_call | solution.py:255
  9.1 0.1 collective-permute-start.9
  9.2 0.6 collective-permute-start.10
  9.8 1.6 %pack.9 = bf16[2,256,256]{2,1,0:T(8,128)(2,1)S(1)} custom-call(s32[2]{0:T(128)S(1)} %pad_add_fusion.place, bf16[64,4096]{1,0:T(8,128)(2,1)} %bitcast.24, bf16[64,4096]{1,0:T(8,128)(2,1)} %bitcast.31, bf16[64,4096]{1,0:T(8,128)(2,1)} %bitcast.38, bf16[64,4096]{1,0:T(8,128)(2,1)} %bitcast.45, bf16[256,512]{1,0:T(8,128)(2,1)} %refs_4_.13, bf16[256,512]{1,0:T(8,128)(2,1)} %refs_5_.13), custom_call_target="tpu_custom_call" | custom-call | tf_op jit(solution)/shard_map/pack/pallas_call | solution.py:255
  11.4 1.6 %collective-permute-start.15 = (bf16[2,256,256]{2,1,0:T(8,128)(2,1)S(1)}, bf16[2,256,256]{2,1,0:T(8,128)(2,1)S(1)}, u32[]{:S(2)}, u32[]{:S(2)}) collective-permute-start(bf16[2,256,256]{2,1,0:T(8,128)(2,1)S(1)} %pack.9), channel_id=1, source_target_pairs={{0,2},{2,0},{1,3},{3,1},{4,6},{6,4},{5,7},{7,5},{8,10},{10,8},{9,1... | collective-permute-start | bytes 786440 | tf_op jit(solution)/shard_map/ppermute | solution.py:246
  12.9 0.6 collective-permute-start.11
  13.5 2.4 %collective-permute-start.12 = (bf16[4,64,256]{2,1,0:T(8,128)(2,1)S(1)}, bf16[4,64,256]{2,1,0:T(8,128)(2,1)S(1)}, u32[]{:S(2)}, u32[]{:S(2)}) collective-permute-start(bf16[4,64,256]{2,1,0:T(8,128)(2,1)S(1)} %get-tuple-element.66), channel_id=1, source_target_pairs={{0,9},{1,8},{4,13},{5,12},{8,1},{9,0},{12,5},{13,4},{2,11},{3,10},... | collective-permute-start | bytes 393224 | tf_op jit(solution)/shard_map/ppermute | solution.py:246
  15.9 2.2 %collective-permute-done.9.refs_7_ = bf16[4,64,256]{2,1,0:T(8,128)(2,1)S(1)} collective-permute-done((bf16[4,64,256]{2,1,0:T(8,128)(2,1)S(1)}, bf16[4,64,256]{2,1,0:T(8,128)(2,1)S(1)}, u32[]{:S(2)}, u32[]{:S(2)}) %collective-permute-start.9) | collective-permute-done | bytes 131104 | tf_op jit(solution)/shard_map/ppermute | solution.py:246
  18.1 1.6 %collective-permute-start.14 = (bf16[4,64,256]{2,1,0:T(8,128)(2,1)S(1)}, bf16[4,64,256]{2,1,0:T(8,128)(2,1)S(1)}, u32[]{:S(2)}, u32[]{:S(2)}) collective-permute-start(bf16[4,64,256]{2,1,0:T(8,128)(2,1)S(1)} %get-tuple-element.68), channel_id=1, source_target_pairs={{0,8},{1,9},{4,12},{5,13},{8,0},{9,1},{12,4},{13,5},{2,10},{3,11},... | collective-permute-start | bytes 393224 | tf_op jit(solution)/shard_map/ppermute | solution.py:246
  19.8 1.9 %pack.6 = (bf16[4,64,256]{2,1,0:T(8,128)(2,1)S(1)}, bf16[4,64,256]{2,1,0:T(8,128)(2,1)S(1)}, bf16[4,64,256]{2,1,0:T(8,128)(2,1)S(1)}, bf16[4,64,256]{2,1,0:T(8,1...) custom-call(s32[2]{0:T(128)S(1)} %pad_add_fusion.place, ...), custom_call_target="tpu_custom_call" | custom-call | tf_op jit(solution)/shard_map/pack/pallas_call | solution.py:255
  21.7 3.2 %collective-permute-start.1 = (bf16[4,64,256]{2,1,0:T(8,128)(2,1)S(1)}, bf16[4,64,256]{2,1,0:T(8,128)(2,1)S(1)}, u32[]{:S(2)}, u32[]{:S(2)}) collective-permute-start(bf16[4,64,256]{2,1,0:T(8,128)(2,1)S(1)} %get-tuple-element.56), channel_id=1, source_target_pairs={{0,12},{1,13},{4,8},{5,9},{8,4},{9,5},{12,0},{13,1},{2,14},{3,15},... | collective-permute-start | bytes 393224 | tf_op jit(solution)/shard_map/ppermute | solution.py:246
  24.9 0.9 %collective-permute-done.12.refs_10_ = bf16[4,64,256]{2,1,0:T(8,128)(2,1)S(1)} collective-permute-done((bf16[4,64,256]{2,1,0:T(8,128)(2,1)S(1)}, bf16[4,64,256]{2,1,0:T(8,128)(2,1)S(1)}, u32[]{:S(2)}, u32[]{:S(2)}) %collective-permute-start.12) | collective-permute-done | bytes 131104 | tf_op jit(solution)/shard_map/ppermute | solution.py:246
  25.9 0.4 collective-permute-start.2
  26.3 5.1 %collective-permute-start.3 = (bf16[4,64,256]{2,1,0:T(8,128)(2,1)S(1)}, bf16[4,64,256]{2,1,0:T(8,128)(2,1)S(1)}, u32[]{:S(2)}, u32[]{:S(2)}) collective-permute-start(bf16[4,64,256]{2,1,0:T(8,128)(2,1)S(1)} %get-tuple-element.58), channel_id=1, source_target_pairs={{0,13},{1,12},{4,9},{5,8},{8,5},{9,4},{12,1},{13,0},{2,15},{3,14},... | collective-permute-start | bytes 393224 | tf_op jit(solution)/shard_map/ppermute | solution.py:246
  31.4 1.6 %pack.7 = bf16[2,256,256]{2,1,0:T(8,128)(2,1)S(1)} custom-call(s32[2]{0:T(128)S(1)} %pad_add_fusion.place, bf16[64,4096]{1,0:T(8,128)(2,1)} %bitcast.26, bf16[64,4096]{1,0:T(8,128)(2,1)} %bitcast.33, bf16[64,4096]{1,0:T(8,128)(2,1)} %bitcast.40, bf16[64,4096]{1,0:T(8,128)(2,1)} %bitcast.47, bf16[256,512]{1,0:T(8,128)(2,1)} %refs_4_.13, bf16[256,512]{1,0:T(8,128)(2,1)} %refs_5_.13), custom_call_target="tpu_custom_call" | custom-call | tf_op jit(solution)/shard_map/pack/pallas_call | solution.py:255
  32.9 0.1 copy.35
  33.0 0.4 collective-permute-done.14.refs_12_
  33.4 1.7 %collective-permute-start.8 = (bf16[2,256,256]{2,1,0:T(8,128)(2,1)S(1)}, bf16[2,256,256]{2,1,0:T(8,128)(2,1)S(1)}, u32[]{:S(2)}, u32[]{:S(2)}) collective-permute-start(bf16[2,256,256]{2,1,0:T(8,128)(2,1)S(1)} %pack.7), channel_id=1, source_target_pairs={{0,2},{2,0},{1,3},{3,1},{4,6},{6,4},{5,7},{7,5},{8,10},{10,8},{9,1... | collective-permute-start | bytes 786440 | tf_op jit(solution)/shard_map/ppermute | solution.py:246
  35.1 0.4 collective-permute-start.4
  35.5 4.0 %collective-permute-start.5 = (bf16[4,64,256]{2,1,0:T(8,128)(2,1)S(1)}, bf16[4,64,256]{2,1,0:T(8,128)(2,1)S(1)}, u32[]{:S(2)}, u32[]{:S(2)}) collective-permute-start(bf16[4,64,256]{2,1,0:T(8,128)(2,1)S(1)} %get-tuple-element.60), channel_id=1, source_target_pairs={{0,9},{1,8},{4,13},{5,12},{8,1},{9,0},{12,5},{13,4},{2,11},{3,10},... | collective-permute-start | bytes 393224 | tf_op jit(solution)/shard_map/ppermute | solution.py:246
  39.5 0.1 collective-permute-start.6
  39.6 2.8 %collective-permute-start.7 = (bf16[4,64,256]{2,1,0:T(8,128)(2,1)S(1)}, bf16[4,64,256]{2,1,0:T(8,128)(2,1)S(1)}, u32[]{:S(2)}, u32[]{:S(2)}) collective-permute-start(bf16[4,64,256]{2,1,0:T(8,128)(2,1)S(1)} %get-tuple-element.62), channel_id=1, source_target_pairs={{0,8},{1,9},{4,12},{5,13},{8,0},{9,1},{12,4},{13,5},{2,10},{3,11},... | collective-permute-start | bytes 393224 | tf_op jit(solution)/shard_map/ppermute | solution.py:246
  42.4 0.7 copy-done.2
  43.1 5.9 %grads.2 = (bf16[3,64,512]{2,1,0:T(8,128)(2,1)S(1)}, bf16[3,64,512]{2,1,0:T(8,128)(2,1)S(1)}, bf16[3,64,512]{2,1,0:T(8,128)(2,1)S(1)}, bf16[3,64,512]{2,1,0:T(8,...) custom-call(s32[2]{0:T(128)S(1)} %pad_add_fusion.place, ...), custom_call_target="tpu_custom_call" | custom-call | flops 10737418240 | bytes 1835008 | tf_op jit(solution)/shard_map/grads/pallas_call | solution.py:272
  49.0 0.2 collective-permute-done.5.refs_10_.refs_6_
  49.2 2.2 %collective-permute-start.16 = (bf16[3,64,256]{2,1,0:T(8,128)(2,1)S(1)}, bf16[3,64,256]{2,1,0:T(8,128)(2,1)S(1)}, u32[]{:S(2)}, u32[]{:S(2)}) collective-permute-start(bf16[3,64,256]{2,1,0:T(8,128)(2,1)S(1)} %get-tuple-element.87), channel_id=1, source_target_pairs={{0,12},{1,13},{4,8},{5,9},{8,4},{9,5},{12,0},{13,1},{2,14},{3,15},... | collective-permute-start | bytes 294920 | tf_op jit(solution)/shard_map/ppermute | solution.py:246
  51.4 1.0 %collective-permute-start.21 = (bf16[3,64,256]{2,1,0:T(8,128)(2,1)S(1)}, bf16[3,64,256]{2,1,0:T(8,128)(2,1)S(1)}, u32[]{:S(2)}, u32[]{:S(2)}) collective-permute-start(bf16[3,64,256]{2,1,0:T(8,128)(2,1)S(1)} %get-tuple-element.92), channel_id=1, source_target_pairs={{0,13},{1,12},{4,9},{5,8},{8,5},{9,4},{12,1},{13,0},{2,15},{3,14},... | collective-permute-start | bytes 294920 | tf_op jit(solution)/shard_map/ppermute | solution.py:246
  52.5 1.9 %collective-permute-start.17 = (bf16[2,256,256]{2,1,0:T(8,128)(2,1)S(1)}, bf16[2,256,256]{2,1,0:T(8,128)(2,1)S(1)}, u32[]{:S(2)}, u32[]{:S(2)}) collective-permute-start(bf16[2,256,256]{2,1,0:T(8,128)(2,1)S(1)} %get-tuple-element.88), channel_id=1, source_target_pairs={{0,2},{2,0},{1,3},{3,1},{4,6},{6,4},{5,7},{7,5},{8,10},{10,8},{9,1... | collective-permute-start | bytes 786440 | tf_op jit(solution)/shard_map/ppermute | solution.py:246
  54.4 5.9 %grads.3 = (bf16[3,64,512]{2,1,0:T(8,128)(2,1)S(1)}, bf16[3,64,512]{2,1,0:T(8,128)(2,1)S(1)}, bf16[3,64,512]{2,1,0:T(8,128)(2,1)S(1)}, bf16[3,64,512]{2,1,0:T(8,...) custom-call(s32[2]{0:T(128)S(1)} %pad_add_fusion.place, ...), custom_call_target="tpu_custom_call", output_to_operand_aliasing={{0}: (18, {}), {1}: (19, {}), {2}: (20, {}), {3}: (21, {}),... | custom-call | flops 10737418240 | bytes 1835008 | tf_op jit(solution)/shard_map/grads/pallas_call | solution.py:272
  60.3 1.0 %collective-permute-done.17.refs_11_ = bf16[2,256,256]{2,1,0:T(8,128)(2,1)S(1)} collective-permute-done((bf16[2,256,256]{2,1,0:T(8,128)(2,1)S(1)}, bf16[2,256,256]{2,1,0:T(8,128)(2,1)S(1)}, u32[]{:S(2)}, u32[]{:S(2)}) %collective-permute-start.17) | collective-permute-done | bytes 262176 | tf_op jit(solution)/shard_map/ppermute | solution.py:246
  61.4 1.3 %collective-permute-start.26 = (bf16[2,256,256]{2,1,0:T(8,128)(2,1)S(1)}, bf16[2,256,256]{2,1,0:T(8,128)(2,1)S(1)}, u32[]{:S(2)}, u32[]{:S(2)}) collective-permute-start(bf16[2,256,256]{2,1,0:T(8,128)(2,1)S(1)} %get-tuple-element.103), channel_id=1, source_target_pairs={{0,2},{2,0},{1,3},{3,1},{4,6},{6,4},{5,7},{7,5},{8,10},{10,8},{9,1... | collective-permute-start | bytes 786440 | tf_op jit(solution)/shard_map/ppermute | solution.py:246
  62.6 2.5 %collective-permute-start.22 = (bf16[3,64,256]{2,1,0:T(8,128)(2,1)S(1)}, bf16[3,64,256]{2,1,0:T(8,128)(2,1)S(1)}, u32[]{:S(2)}, u32[]{:S(2)}) collective-permute-start(bf16[3,64,256]{2,1,0:T(8,128)(2,1)S(1)} %get-tuple-element.94), channel_id=1, source_target_pairs={{0,12},{1,13},{4,8},{5,9},{8,4},{9,5},{12,0},{13,1},{2,14},{3,15},... | collective-permute-start | bytes 294920 | tf_op jit(solution)/shard_map/ppermute | solution.py:246
  65.1 2.5 %collective-permute-start.25 = (bf16[3,64,512]{2,1,0:T(8,128)(2,1)S(1)}, bf16[3,64,512]{2,1,0:T(8,128)(2,1)S(1)}, u32[]{:S(2)}, u32[]{:S(2)}) collective-permute-start(bf16[3,64,512]{2,1,0:T(8,128)(2,1)S(1)} %get-tuple-element.97), channel_id=1, source_target_pairs={{0,5},{1,4},{4,1},{5,0},{8,13},{9,12},{12,9},{13,8},{2,7},{3,6},{6... | collective-permute-start | bytes 589832 | tf_op jit(solution)/shard_map/ppermute | solution.py:246
  67.7 1.5 %collective-permute-done.22.refs_3_ = bf16[3,64,256]{2,1,0:T(8,128)(2,1)S(1)} collective-permute-done((bf16[3,64,256]{2,1,0:T(8,128)(2,1)S(1)}, bf16[3,64,256]{2,1,0:T(8,128)(2,1)S(1)}, u32[]{:S(2)}, u32[]{:S(2)}) %collective-permute-start.22) | collective-permute-done | bytes 98336 | tf_op jit(solution)/shard_map/ppermute | solution.py:246
  69.2 0.2 collective-permute-start.18
  69.4 2.8 %collective-permute-done.23.refs_4_ = bf16[3,64,256]{2,1,0:T(8,128)(2,1)S(1)} collective-permute-done((bf16[3,64,256]{2,1,0:T(8,128)(2,1)S(1)}, bf16[3,64,256]{2,1,0:T(8,128)(2,1)S(1)}, u32[]{:S(2)}, u32[]{:S(2)}) %collective-permute-start.23) | collective-permute-done | bytes 98336 | tf_op jit(solution)/shard_map/ppermute | solution.py:246
  72.1 2.8 %collective-permute-start.19 = (bf16[3,64,512]{2,1,0:T(8,128)(2,1)S(1)}, bf16[3,64,512]{2,1,0:T(8,128)(2,1)S(1)}, u32[]{:S(2)}, u32[]{:S(2)}) collective-permute-start(bf16[3,64,512]{2,1,0:T(8,128)(2,1)S(1)} %get-tuple-element.90), channel_id=1, source_target_pairs={{0,8},{1,9},{4,12},{5,13},{8,0},{9,1},{12,4},{13,5},{2,10},{3,11},... | collective-permute-start | bytes 589832 | tf_op jit(solution)/shard_map/ppermute | solution.py:246
  74.9 5.0 %collective-permute-done.24.refs_5_ = bf16[3,64,512]{2,1,0:T(8,128)(2,1)S(1)} collective-permute-done((bf16[3,64,512]{2,1,0:T(8,128)(2,1)S(1)}, bf16[3,64,512]{2,1,0:T(8,128)(2,1)S(1)}, u32[]{:S(2)}, u32[]{:S(2)}) %collective-permute-start.24) | collective-permute-done | bytes 196640 | tf_op jit(solution)/shard_map/ppermute | solution.py:246
  79.9 0.3 collective-permute-start.20
  80.2 1.7 %unpack.2 = (bf16[64,4096]{1,0:T(8,128)(2,1)}, bf16[64,4096]{1,0:T(8,128)(2,1)}, bf16[64,4096]{1,0:T(8,128)(2,1)}) custom-call(s32[2]{0:T(128)S(1)} %pad_add_fusion.place, bf16[3,64,256]{2,1,0:T(8,128)(2,1)S(1)} %collective-permute-done.16.refs_10_.refs_0_, bf16[3,64,256]{2,1,0:T(8,128)(2,1)S(1)} %collective-permute-done.21.refs_1_, ...), custom_call_target="tpu_custom_call" | custom-call | tf_op jit(solution)/shard_map/unpack/pallas_call | solution.py:324
  81.9 0.1 convert_add_fusion
  81.9 0.1 fusion.2
  82.1 5.7 %collective-permute-done.18.refs_0_ = bf16[3,64,512]{2,1,0:T(8,128)(2,1)S(1)} collective-permute-done((bf16[3,64,512]{2,1,0:T(8,128)(2,1)S(1)}, bf16[3,64,512]{2,1,0:T(8,128)(2,1)S(1)}, u32[]{:S(2)}, u32[]{:S(2)}) %collective-permute-start.18) | collective-permute-done | bytes 196640 | tf_op jit(solution)/shard_map/ppermute | solution.py:246
  87.8 0.7 collective-permute-done.19.refs_1_
  88.5 1.4 %unpack.3 = (bf16[64,4096]{1,0:T(8,128)(2,1)}, bf16[64,4096]{1,0:T(8,128)(2,1)}, bf16[64,4096]{1,0:T(8,128)(2,1)}) custom-call(s32[2]{0:T(128)S(1)} %pad_add_fusion.place, bf16[3,64,512]{2,1,0:T(8,128)(2,1)S(1)} %collective-permute-done.18.refs_0_, ...), custom_call_target="tpu_custom_call", output_to_operand_aliasing={{0}: (4, {}), {1}: (5, {}), {2}: (6, {})} | custom-call | tf_op jit(solution)/shard_map/unpack/pallas_call | solution.py:324
  (32 shorter events, 0.1 us)
Async XLA Ops:
  2.1 11.4 %collective-permute-start = (bf16[4,64,256]{2,1,0:T(8,128)(2,1)S(1)}, bf16[4,64,256]{2,1,0:T(8,128)(2,1)S(1)}, u32[]{:S(2)}, u32[]{:S(2)}) collective-permute-start(bf16[4,64,256]{2,1,0:T(8,128)(2,1)S(1)} %pack.5.refs_6_), channel_id=1, source_target_pairs={{0,12},{1,13},{4,8},{5,9},{8,4},{9,5},{12,0},{13,1},{2,14},{3,15},... | collective-permute-start | bytes 393224 | tf_op jit(solution)/shard_map/ppermute | solution.py:246
  9.1 9.0 %collective-permute-start.9 = (bf16[4,64,256]{2,1,0:T(8,128)(2,1)S(1)}, bf16[4,64,256]{2,1,0:T(8,128)(2,1)S(1)}, u32[]{:S(2)}, u32[]{:S(2)}) collective-permute-start(bf16[4,64,256]{2,1,0:T(8,128)(2,1)S(1)} %get-tuple-element.63), channel_id=1, source_target_pairs={{0,5},{1,4},{4,1},{5,0},{8,13},{9,12},{12,9},{13,8},{2,7},{3,6},{6... | collective-permute-start | bytes 393224 | tf_op jit(solution)/shard_map/ppermute | solution.py:246
  9.2 8.9 %collective-permute-start.10 = (bf16[4,64,256]{2,1,0:T(8,128)(2,1)S(1)}, bf16[4,64,256]{2,1,0:T(8,128)(2,1)S(1)}, u32[]{:S(2)}, u32[]{:S(2)}) collective-permute-start(bf16[4,64,256]{2,1,0:T(8,128)(2,1)S(1)} %get-tuple-element.64), channel_id=1, source_target_pairs={{0,13},{1,12},{4,9},{5,8},{8,5},{9,4},{12,1},{13,0},{2,15},{3,14},... | collective-permute-start | bytes 393224 | tf_op jit(solution)/shard_map/ppermute | solution.py:246
  11.4 23.8 %collective-permute-start.15 = (bf16[2,256,256]{2,1,0:T(8,128)(2,1)S(1)}, bf16[2,256,256]{2,1,0:T(8,128)(2,1)S(1)}, u32[]{:S(2)}, u32[]{:S(2)}) collective-permute-start(bf16[2,256,256]{2,1,0:T(8,128)(2,1)S(1)} %pack.9), channel_id=1, source_target_pairs={{0,2},{2,0},{1,3},{3,1},{4,6},{6,4},{5,7},{7,5},{8,10},{10,8},{9,1... | collective-permute-start | bytes 786440 | tf_op jit(solution)/shard_map/ppermute | solution.py:246
  12.9 8.8 %collective-permute-start.11 = (bf16[4,64,256]{2,1,0:T(8,128)(2,1)S(1)}, bf16[4,64,256]{2,1,0:T(8,128)(2,1)S(1)}, u32[]{:S(2)}, u32[]{:S(2)}) collective-permute-start(bf16[4,64,256]{2,1,0:T(8,128)(2,1)S(1)} %get-tuple-element.65), channel_id=1, source_target_pairs={{0,4},{1,5},{4,0},{5,1},{8,12},{9,13},{12,8},{13,9},{2,6},{3,7},{6... | collective-permute-start | bytes 393224 | tf_op jit(solution)/shard_map/ppermute | solution.py:246
  13.5 12.4 %collective-permute-start.12 = (bf16[4,64,256]{2,1,0:T(8,128)(2,1)S(1)}, bf16[4,64,256]{2,1,0:T(8,128)(2,1)S(1)}, u32[]{:S(2)}, u32[]{:S(2)}) collective-permute-start(bf16[4,64,256]{2,1,0:T(8,128)(2,1)S(1)} %get-tuple-element.66), channel_id=1, source_target_pairs={{0,9},{1,8},{4,13},{5,12},{8,1},{9,0},{12,5},{13,4},{2,11},{3,10},... | collective-permute-start | bytes 393224 | tf_op jit(solution)/shard_map/ppermute | solution.py:246
  18.1 8.2 %collective-permute-start.13 = (bf16[4,64,256]{2,1,0:T(8,128)(2,1)S(1)}, bf16[4,64,256]{2,1,0:T(8,128)(2,1)S(1)}, u32[]{:S(2)}, u32[]{:S(2)}) collective-permute-start(bf16[4,64,256]{2,1,0:T(8,128)(2,1)S(1)} %get-tuple-element.67), channel_id=1, source_target_pairs={{0,1},{1,0},{4,5},{5,4},{8,9},{9,8},{12,13},{13,12},{2,3},{3,2},{6... | collective-permute-start | bytes 393224 | tf_op jit(solution)/shard_map/ppermute | solution.py:246
  18.1 15.3 %collective-permute-start.14 = (bf16[4,64,256]{2,1,0:T(8,128)(2,1)S(1)}, bf16[4,64,256]{2,1,0:T(8,128)(2,1)S(1)}, u32[]{:S(2)}, u32[]{:S(2)}) collective-permute-start(bf16[4,64,256]{2,1,0:T(8,128)(2,1)S(1)} %get-tuple-element.68), channel_id=1, source_target_pairs={{0,8},{1,9},{4,12},{5,13},{8,0},{9,1},{12,4},{13,5},{2,10},{3,11},... | collective-permute-start | bytes 393224 | tf_op jit(solution)/shard_map/ppermute | solution.py:246
  21.7 13.8 %collective-permute-start.1 = (bf16[4,64,256]{2,1,0:T(8,128)(2,1)S(1)}, bf16[4,64,256]{2,1,0:T(8,128)(2,1)S(1)}, u32[]{:S(2)}, u32[]{:S(2)}) collective-permute-start(bf16[4,64,256]{2,1,0:T(8,128)(2,1)S(1)} %get-tuple-element.56), channel_id=1, source_target_pairs={{0,12},{1,13},{4,8},{5,9},{8,4},{9,5},{12,0},{13,1},{2,14},{3,15},... | collective-permute-start | bytes 393224 | tf_op jit(solution)/shard_map/ppermute | solution.py:246
  25.9 13.6 %collective-permute-start.2 = (bf16[4,64,256]{2,1,0:T(8,128)(2,1)S(1)}, bf16[4,64,256]{2,1,0:T(8,128)(2,1)S(1)}, u32[]{:S(2)}, u32[]{:S(2)}) collective-permute-start(bf16[4,64,256]{2,1,0:T(8,128)(2,1)S(1)} %get-tuple-element.57), channel_id=1, source_target_pairs={{0,5},{1,4},{4,1},{5,0},{8,13},{9,12},{12,9},{13,8},{2,7},{3,6},{6... | collective-permute-start | bytes 393224 | tf_op jit(solution)/shard_map/ppermute | solution.py:246
  26.3 6.7 %copy-start.4 = (s32[1,4,3]{1,0,2:T(1,128)S(1)}, s32[1,4,3]{1,0,2:T(1,128)}, u32[]{:S(2)}) copy-start(s32[1,4,3]{1,0,2:T(1,128)} %param.15) | copy-start | bytes 148
  26.3 13.3 %collective-permute-start.3 = (bf16[4,64,256]{2,1,0:T(8,128)(2,1)S(1)}, bf16[4,64,256]{2,1,0:T(8,128)(2,1)S(1)}, u32[]{:S(2)}, u32[]{:S(2)}) collective-permute-start(bf16[4,64,256]{2,1,0:T(8,128)(2,1)S(1)} %get-tuple-element.58), channel_id=1, source_target_pairs={{0,13},{1,12},{4,9},{5,8},{8,5},{9,4},{12,1},{13,0},{2,15},{3,14},... | collective-permute-start | bytes 393224 | tf_op jit(solution)/shard_map/ppermute | solution.py:246
  33.4 19.0 %collective-permute-start.8 = (bf16[2,256,256]{2,1,0:T(8,128)(2,1)S(1)}, bf16[2,256,256]{2,1,0:T(8,128)(2,1)S(1)}, u32[]{:S(2)}, u32[]{:S(2)}) collective-permute-start(bf16[2,256,256]{2,1,0:T(8,128)(2,1)S(1)} %pack.7), channel_id=1, source_target_pairs={{0,2},{2,0},{1,3},{3,1},{4,6},{6,4},{5,7},{7,5},{8,10},{10,8},{9,1... | collective-permute-start | bytes 786440 | tf_op jit(solution)/shard_map/ppermute | solution.py:246
  35.1 13.9 %collective-permute-start.4 = (bf16[4,64,256]{2,1,0:T(8,128)(2,1)S(1)}, bf16[4,64,256]{2,1,0:T(8,128)(2,1)S(1)}, u32[]{:S(2)}, u32[]{:S(2)}) collective-permute-start(bf16[4,64,256]{2,1,0:T(8,128)(2,1)S(1)} %get-tuple-element.59), channel_id=1, source_target_pairs={{0,4},{1,5},{4,0},{5,1},{8,12},{9,13},{12,8},{13,9},{2,6},{3,7},{6... | collective-permute-start | bytes 393224 | tf_op jit(solution)/shard_map/ppermute | solution.py:246
  35.5 13.7 %collective-permute-start.5 = (bf16[4,64,256]{2,1,0:T(8,128)(2,1)S(1)}, bf16[4,64,256]{2,1,0:T(8,128)(2,1)S(1)}, u32[]{:S(2)}, u32[]{:S(2)}) collective-permute-start(bf16[4,64,256]{2,1,0:T(8,128)(2,1)S(1)} %get-tuple-element.60), channel_id=1, source_target_pairs={{0,9},{1,8},{4,13},{5,12},{8,1},{9,0},{12,5},{13,4},{2,11},{3,10},... | collective-permute-start | bytes 393224 | tf_op jit(solution)/shard_map/ppermute | solution.py:246
  39.5 14.9 %collective-permute-start.6 = (bf16[4,64,256]{2,1,0:T(8,128)(2,1)S(1)}, bf16[4,64,256]{2,1,0:T(8,128)(2,1)S(1)}, u32[]{:S(2)}, u32[]{:S(2)}) collective-permute-start(bf16[4,64,256]{2,1,0:T(8,128)(2,1)S(1)} %get-tuple-element.61), channel_id=1, source_target_pairs={{0,1},{1,0},{4,5},{5,4},{8,9},{9,8},{12,13},{13,12},{2,3},{3,2},{6... | collective-permute-start | bytes 393224 | tf_op jit(solution)/shard_map/ppermute | solution.py:246
  39.6 14.8 %collective-permute-start.7 = (bf16[4,64,256]{2,1,0:T(8,128)(2,1)S(1)}, bf16[4,64,256]{2,1,0:T(8,128)(2,1)S(1)}, u32[]{:S(2)}, u32[]{:S(2)}) collective-permute-start(bf16[4,64,256]{2,1,0:T(8,128)(2,1)S(1)} %get-tuple-element.62), channel_id=1, source_target_pairs={{0,8},{1,9},{4,12},{5,13},{8,0},{9,1},{12,4},{13,5},{2,10},{3,11},... | collective-permute-start | bytes 393224 | tf_op jit(solution)/shard_map/ppermute | solution.py:246
  42.4 0.7 copy-start.2
  42.4 0.7 copy-start.3
  49.2 11.1 %collective-permute-start.16 = (bf16[3,64,256]{2,1,0:T(8,128)(2,1)S(1)}, bf16[3,64,256]{2,1,0:T(8,128)(2,1)S(1)}, u32[]{:S(2)}, u32[]{:S(2)}) collective-permute-start(bf16[3,64,256]{2,1,0:T(8,128)(2,1)S(1)} %get-tuple-element.87), channel_id=1, source_target_pairs={{0,12},{1,13},{4,8},{5,9},{8,4},{9,5},{12,0},{13,1},{2,14},{3,15},... | collective-permute-start | bytes 294920 | tf_op jit(solution)/shard_map/ppermute | solution.py:246
  51.4 13.7 %collective-permute-start.21 = (bf16[3,64,256]{2,1,0:T(8,128)(2,1)S(1)}, bf16[3,64,256]{2,1,0:T(8,128)(2,1)S(1)}, u32[]{:S(2)}, u32[]{:S(2)}) collective-permute-start(bf16[3,64,256]{2,1,0:T(8,128)(2,1)S(1)} %get-tuple-element.92), channel_id=1, source_target_pairs={{0,13},{1,12},{4,9},{5,8},{8,5},{9,4},{12,1},{13,0},{2,15},{3,14},... | collective-permute-start | bytes 294920 | tf_op jit(solution)/shard_map/ppermute | solution.py:246
  52.5 8.9 %collective-permute-start.17 = (bf16[2,256,256]{2,1,0:T(8,128)(2,1)S(1)}, bf16[2,256,256]{2,1,0:T(8,128)(2,1)S(1)}, u32[]{:S(2)}, u32[]{:S(2)}) collective-permute-start(bf16[2,256,256]{2,1,0:T(8,128)(2,1)S(1)} %get-tuple-element.88), channel_id=1, source_target_pairs={{0,2},{2,0},{1,3},{3,1},{4,6},{6,4},{5,7},{7,5},{8,10},{10,8},{9,1... | collective-permute-start | bytes 786440 | tf_op jit(solution)/shard_map/ppermute | solution.py:246
  61.4 20.5 %collective-permute-start.26 = (bf16[2,256,256]{2,1,0:T(8,128)(2,1)S(1)}, bf16[2,256,256]{2,1,0:T(8,128)(2,1)S(1)}, u32[]{:S(2)}, u32[]{:S(2)}) collective-permute-start(bf16[2,256,256]{2,1,0:T(8,128)(2,1)S(1)} %get-tuple-element.103), channel_id=1, source_target_pairs={{0,2},{2,0},{1,3},{3,1},{4,6},{6,4},{5,7},{7,5},{8,10},{10,8},{9,1... | collective-permute-start | bytes 786440 | tf_op jit(solution)/shard_map/ppermute | solution.py:246
  62.6 6.5 %collective-permute-start.22 = (bf16[3,64,256]{2,1,0:T(8,128)(2,1)S(1)}, bf16[3,64,256]{2,1,0:T(8,128)(2,1)S(1)}, u32[]{:S(2)}, u32[]{:S(2)}) collective-permute-start(bf16[3,64,256]{2,1,0:T(8,128)(2,1)S(1)} %get-tuple-element.94), channel_id=1, source_target_pairs={{0,12},{1,13},{4,8},{5,9},{8,4},{9,5},{12,0},{13,1},{2,14},{3,15},... | collective-permute-start | bytes 294920 | tf_op jit(solution)/shard_map/ppermute | solution.py:246
  65.1 7.0 %collective-permute-start.23 = (bf16[3,64,256]{2,1,0:T(8,128)(2,1)S(1)}, bf16[3,64,256]{2,1,0:T(8,128)(2,1)S(1)}, u32[]{:S(2)}, u32[]{:S(2)}) collective-permute-start(bf16[3,64,256]{2,1,0:T(8,128)(2,1)S(1)} %get-tuple-element.95), channel_id=1, source_target_pairs={{0,13},{1,12},{4,9},{5,8},{8,5},{9,4},{12,1},{13,0},{2,15},{3,14},... | collective-permute-start | bytes 294920 | tf_op jit(solution)/shard_map/ppermute | solution.py:246
  65.1 14.7 %collective-permute-start.24 = (bf16[3,64,512]{2,1,0:T(8,128)(2,1)S(1)}, bf16[3,64,512]{2,1,0:T(8,128)(2,1)S(1)}, u32[]{:S(2)}, u32[]{:S(2)}) collective-permute-start(bf16[3,64,512]{2,1,0:T(8,128)(2,1)S(1)} %get-tuple-element.96), channel_id=1, source_target_pairs={{0,9},{1,8},{4,13},{5,12},{8,1},{9,0},{12,5},{13,4},{2,11},{3,10},... | collective-permute-start | bytes 589832 | tf_op jit(solution)/shard_map/ppermute | solution.py:246
  65.1 15.1 %collective-permute-start.25 = (bf16[3,64,512]{2,1,0:T(8,128)(2,1)S(1)}, bf16[3,64,512]{2,1,0:T(8,128)(2,1)S(1)}, u32[]{:S(2)}, u32[]{:S(2)}) collective-permute-start(bf16[3,64,512]{2,1,0:T(8,128)(2,1)S(1)} %get-tuple-element.97), channel_id=1, source_target_pairs={{0,5},{1,4},{4,1},{5,0},{8,13},{9,12},{12,9},{13,8},{2,7},{3,6},{6... | collective-permute-start | bytes 589832 | tf_op jit(solution)/shard_map/ppermute | solution.py:246
  69.2 18.6 %collective-permute-start.18 = (bf16[3,64,512]{2,1,0:T(8,128)(2,1)S(1)}, bf16[3,64,512]{2,1,0:T(8,128)(2,1)S(1)}, u32[]{:S(2)}, u32[]{:S(2)}) collective-permute-start(bf16[3,64,512]{2,1,0:T(8,128)(2,1)S(1)} %get-tuple-element.89), channel_id=1, source_target_pairs={{0,4},{1,5},{4,0},{5,1},{8,12},{9,13},{12,8},{13,9},{2,6},{3,7},{6... | collective-permute-start | bytes 589832 | tf_op jit(solution)/shard_map/ppermute | solution.py:246
  72.1 16.4 %collective-permute-start.19 = (bf16[3,64,512]{2,1,0:T(8,128)(2,1)S(1)}, bf16[3,64,512]{2,1,0:T(8,128)(2,1)S(1)}, u32[]{:S(2)}, u32[]{:S(2)}) collective-permute-start(bf16[3,64,512]{2,1,0:T(8,128)(2,1)S(1)} %get-tuple-element.90), channel_id=1, source_target_pairs={{0,8},{1,9},{4,12},{5,13},{8,0},{9,1},{12,4},{13,5},{2,10},{3,11},... | collective-permute-start | bytes 589832 | tf_op jit(solution)/shard_map/ppermute | solution.py:246
  79.9 8.6 %collective-permute-start.20 = (bf16[3,64,512]{2,1,0:T(8,128)(2,1)S(1)}, bf16[3,64,512]{2,1,0:T(8,128)(2,1)S(1)}, u32[]{:S(2)}, u32[]{:S(2)}) collective-permute-start(bf16[3,64,512]{2,1,0:T(8,128)(2,1)S(1)} %get-tuple-element.91), channel_id=1, source_target_pairs={{0,1},{1,0},{4,5},{5,4},{8,9},{9,8},{12,13},{13,12},{2,3},{3,2},{6... | collective-permute-start | bytes 589832 | tf_op jit(solution)/shard_map/ppermute | solution.py:246
  82.1 7.8 %copy-start = (f32[256,512]{1,0:T(8,128)}, f32[256,512]{1,0:T(8,128)S(1)}, u32[]{:S(2)}) copy-start(f32[256,512]{1,0:T(8,128)S(1)} %get-tuple-element.107.refs_7_) | copy-start | bytes 1572868
  82.1 7.8 %copy-start.1 = (f32[256,512]{1,0:T(8,128)}, f32[256,512]{1,0:T(8,128)S(1)}, u32[]{:S(2)}) copy-start(f32[256,512]{1,0:T(8,128)S(1)} %get-tuple-element.108.refs_6_) | copy-start | bytes 1572868

commit v5 on v4

--- a/solution.py
+++ b/solution.py
@@ -11,7 +11,7 @@
 HD = 128
 BLOCK = 128
 K_MAX = 3
-EARLY = 2
+EARLY = 3
 EHOLD = 5
 TAIL = 3
 FIRST = 1
@@ -341,7 +341,7 @@
     recvs = send(packed, order)
     early = () if single else tuple(far[:EARLY])
     rest = [k for k in near if k]
-    whole = (*far[2:3], *rest[:2], *far[3:], *rest[2:]) if early else order
+    whole = (*far[EARLY:], *rest) if early else order
     targets = tuple((k, True) for k in (0, *whole)) + tuple((k, False) for k in early)
     merged, parts, gauge_sums, back_early = [], [], [], []
     for at, chunk in enumerate(chunks):
@@ -366,7 +366,8 @@
     pieces = dict(zip(whole, merged[1:]))
     late = [(swap(pieces[k], TOKENS, total, k), k, 0, columns) for k in whole]
     if early:
-        late = [(x, k, *chunks[-1]) for x, k in zip(send(cut, early), early)] + late
+        cuts = [(x, k, *chunks[-1]) for x, k in zip(send(cut, early), early)]
+        late = [cuts[0], late[1], cuts[1], late[0], late[2], cuts[2], *late[3:]]
     gauge_sum = jnp.concatenate(gauge_sums, axis=2)
     gauge_grads = [gauge_sum[0], gauge_sum[1]]
     parts = parts + [(merged[0], 0, 0, columns)] + late

time: 90.5 us -> 90.4 us (level)
  waiting for transfers between devices: 20.4 us -> 7.64 us
  starting transfers between devices: 44.3 us -> 55.8 us
    ppermute x27 -> x28, waiting for transfers between devices: 20.4 us -> 7.64 us  [swap(): return lax.ppermute(x, axis, [(i, i ^ k) for i in range(size)])]
    ppermute x27 -> x28, starting transfers between devices: 44.3 us -> 55.8 us  [swap(): return lax.ppermute(x, axis, [(i, i ^ k) for i in range(size)])]
  transfers between devices with their start and end apart: 27 -> 28, of which waited for: 10 -> 5; matrix products, arithmetic and copies ran while one was open for 0% -> 0% of each run, Pallas kernels for 23% -> 23%
where the time goes in v5:
time: 90.4 us; the launch traced here: 88.9 us
  starting transfers between devices  55.8 us (62%)
  Pallas kernels  23.5 us (26%)
  waiting for transfers between devices  7.64 us (8%)
    ppermute x28, starting transfers between devices, swap(): return lax.ppermute(x, axis, [(i, i ^ k) for i in range(size)])  55.8 us
    pallas_call x2, Pallas kernels, grads(): pl.pallas_call(functools.partial(grads_kernel, off, width, columns, order...  12 us
    pallas_call x5, Pallas kernels, pack(): pl.pallas_call(functools.partial(pack_kernel, off, width, columns, part,...  8.33 us
    ppermute x28, waiting for transfers between devices, swap(): return lax.ppermute(x, axis, [(i, i ^ k) for i in range(size)])  7.64 us
    pallas_call x2, Pallas kernels, unpack(): pl.pallas_call(functools.partial(unpack_kernel, columns, [part[1:] for pa...  3.17 us
  transfers between devices with their start and end apart: 28, of which 5 were waited for; matrix products, arithmetic and copies ran while one was open for 0% of the time, Pallas kernels for 23%

profile of v5, /device:TPU:0, one launch (start us, length us, event | category | flops | bytes accessed | tf_op | source)
XLA Modules:
  0.0 88.9 jit_solution(14951828941751625823)
XLA Ops:
  0.6 0.1 pad_add_fusion.place
  0.7 1.4 %pack.5.refs_6_ = bf16[4,64,256]{2,1,0:T(8,128)(2,1)S(1)} custom-call(s32[2]{0:T(128)S(1)} %pad_add_fusion.place, bf16[64,4096]{1,0:T(8,128)(2,1)} %bitcast.22, bf16[64,4096]{1,0:T(8,128)(2,1)} %bitcast.29, bf16[64,4096]{1,0:T(8,128)(2,1)} %bitcast.36, bf16[64,4096]{1,0:T(8,128)(2,1)} %bitcast.43, bf16[256,512]{1,0:T(8,128)(2,1)} %refs_4_.13, ...), custom_call_target="tpu_custom_call" | custom-call | tf_op jit(solution)/shard_map/pack/pallas_call | solution.py:255
  2.1 5.1 %collective-permute-start = (bf16[4,64,256]{2,1,0:T(8,128)(2,1)S(1)}, bf16[4,64,256]{2,1,0:T(8,128)(2,1)S(1)}, u32[]{:S(2)}, u32[]{:S(2)}) collective-permute-start(bf16[4,64,256]{2,1,0:T(8,128)(2,1)S(1)} %pack.5.refs_6_), channel_id=1, source_target_pairs={{0,12},{1,13},{4,8},{5,9},{8,4},{9,5},{12,0},{13,1},{2,14},{3,15},... | collective-permute-start | bytes 393224 | tf_op jit(solution)/shard_map/ppermute | solution.py:246
  7.2 1.9 %pack.8 = (bf16[4,64,256]{2,1,0:T(8,128)(2,1)S(1)}, bf16[4,64,256]{2,1,0:T(8,128)(2,1)S(1)}, bf16[4,64,256]{2,1,0:T(8,128)(2,1)S(1)}, bf16[4,64,256]{2,1,0:T(8,1...) custom-call(s32[2]{0:T(128)S(1)} %pad_add_fusion.place, bf16[64,4096]{1,0:T(8,128)(2,1)} %bitcast.23, ...), custom_call_target="tpu_custom_call" | custom-call | tf_op jit(solution)/shard_map/pack/pallas_call | solution.py:255
  9.1 0.1 collective-permute-start.9
  9.2 0.6 collective-permute-start.10
  9.8 1.6 %pack.9 = bf16[2,256,256]{2,1,0:T(8,128)(2,1)S(1)} custom-call(s32[2]{0:T(128)S(1)} %pad_add_fusion.place, bf16[64,4096]{1,0:T(8,128)(2,1)} %bitcast.24, bf16[64,4096]{1,0:T(8,128)(2,1)} %bitcast.31, bf16[64,4096]{1,0:T(8,128)(2,1)} %bitcast.38, bf16[64,4096]{1,0:T(8,128)(2,1)} %bitcast.45, bf16[256,512]{1,0:T(8,128)(2,1)} %refs_4_.13, bf16[256,512]{1,0:T(8,128)(2,1)} %refs_5_.13), custom_call_target="tpu_custom_call" | custom-call | tf_op jit(solution)/shard_map/pack/pallas_call | solution.py:255
  11.4 1.6 %collective-permute-start.15 = (bf16[2,256,256]{2,1,0:T(8,128)(2,1)S(1)}, bf16[2,256,256]{2,1,0:T(8,128)(2,1)S(1)}, u32[]{:S(2)}, u32[]{:S(2)}) collective-permute-start(bf16[2,256,256]{2,1,0:T(8,128)(2,1)S(1)} %pack.9), channel_id=1, source_target_pairs={{0,2},{2,0},{1,3},{3,1},{4,6},{6,4},{5,7},{7,5},{8,10},{10,8},{9,1... | collective-permute-start | bytes 786440 | tf_op jit(solution)/shard_map/ppermute | solution.py:246
  12.9 0.6 collective-permute-start.11
  13.5 2.4 %collective-permute-start.12 = (bf16[4,64,256]{2,1,0:T(8,128)(2,1)S(1)}, bf16[4,64,256]{2,1,0:T(8,128)(2,1)S(1)}, u32[]{:S(2)}, u32[]{:S(2)}) collective-permute-start(bf16[4,64,256]{2,1,0:T(8,128)(2,1)S(1)} %get-tuple-element.67), channel_id=1, source_target_pairs={{0,9},{1,8},{4,13},{5,12},{8,1},{9,0},{12,5},{13,4},{2,11},{3,10},... | collective-permute-start | bytes 393224 | tf_op jit(solution)/shard_map/ppermute | solution.py:246
  15.9 2.2 %collective-permute-done.9.refs_7_ = bf16[4,64,256]{2,1,0:T(8,128)(2,1)S(1)} collective-permute-done((bf16[4,64,256]{2,1,0:T(8,128)(2,1)S(1)}, bf16[4,64,256]{2,1,0:T(8,128)(2,1)S(1)}, u32[]{:S(2)}, u32[]{:S(2)}) %collective-permute-start.9) | collective-permute-done | bytes 131104 | tf_op jit(solution)/shard_map/ppermute | solution.py:246
  18.1 1.6 %collective-permute-start.14 = (bf16[4,64,256]{2,1,0:T(8,128)(2,1)S(1)}, bf16[4,64,256]{2,1,0:T(8,128)(2,1)S(1)}, u32[]{:S(2)}, u32[]{:S(2)}) collective-permute-start(bf16[4,64,256]{2,1,0:T(8,128)(2,1)S(1)} %get-tuple-element.69), channel_id=1, source_target_pairs={{0,8},{1,9},{4,12},{5,13},{8,0},{9,1},{12,4},{13,5},{2,10},{3,11},... | collective-permute-start | bytes 393224 | tf_op jit(solution)/shard_map/ppermute | solution.py:246
  19.8 1.9 %pack.6 = (bf16[4,64,256]{2,1,0:T(8,128)(2,1)S(1)}, bf16[4,64,256]{2,1,0:T(8,128)(2,1)S(1)}, bf16[4,64,256]{2,1,0:T(8,128)(2,1)S(1)}, bf16[4,64,256]{2,1,0:T(8,1...) custom-call(s32[2]{0:T(128)S(1)} %pad_add_fusion.place, ...), custom_call_target="tpu_custom_call" | custom-call | tf_op jit(solution)/shard_map/pack/pallas_call | solution.py:255
  21.7 3.2 %collective-permute-start.1 = (bf16[4,64,256]{2,1,0:T(8,128)(2,1)S(1)}, bf16[4,64,256]{2,1,0:T(8,128)(2,1)S(1)}, u32[]{:S(2)}, u32[]{:S(2)}) collective-permute-start(bf16[4,64,256]{2,1,0:T(8,128)(2,1)S(1)} %get-tuple-element.57), channel_id=1, source_target_pairs={{0,12},{1,13},{4,8},{5,9},{8,4},{9,5},{12,0},{13,1},{2,14},{3,15},... | collective-permute-start | bytes 393224 | tf_op jit(solution)/shard_map/ppermute | solution.py:246
  24.9 0.9 %collective-permute-done.12.refs_10_ = bf16[4,64,256]{2,1,0:T(8,128)(2,1)S(1)} collective-permute-done((bf16[4,64,256]{2,1,0:T(8,128)(2,1)S(1)}, bf16[4,64,256]{2,1,0:T(8,128)(2,1)S(1)}, u32[]{:S(2)}, u32[]{:S(2)}) %collective-permute-start.12) | collective-permute-done | bytes 131104 | tf_op jit(solution)/shard_map/ppermute | solution.py:246
  25.9 0.4 collective-permute-start.2
  26.3 5.1 %collective-permute-start.3 = (bf16[4,64,256]{2,1,0:T(8,128)(2,1)S(1)}, bf16[4,64,256]{2,1,0:T(8,128)(2,1)S(1)}, u32[]{:S(2)}, u32[]{:S(2)}) collective-permute-start(bf16[4,64,256]{2,1,0:T(8,128)(2,1)S(1)} %get-tuple-element.59), channel_id=1, source_target_pairs={{0,13},{1,12},{4,9},{5,8},{8,5},{9,4},{12,1},{13,0},{2,15},{3,14},... | collective-permute-start | bytes 393224 | tf_op jit(solution)/shard_map/ppermute | solution.py:246
  31.4 1.6 %pack.7 = bf16[2,256,256]{2,1,0:T(8,128)(2,1)S(1)} custom-call(s32[2]{0:T(128)S(1)} %pad_add_fusion.place, bf16[64,4096]{1,0:T(8,128)(2,1)} %bitcast.26, bf16[64,4096]{1,0:T(8,128)(2,1)} %bitcast.33, bf16[64,4096]{1,0:T(8,128)(2,1)} %bitcast.40, bf16[64,4096]{1,0:T(8,128)(2,1)} %bitcast.47, bf16[256,512]{1,0:T(8,128)(2,1)} %refs_4_.13, bf16[256,512]{1,0:T(8,128)(2,1)} %refs_5_.13), custom_call_target="tpu_custom_call" | custom-call | tf_op jit(solution)/shard_map/pack/pallas_call | solution.py:255
  32.9 0.1 copy.35
  33.0 0.4 collective-permute-done.14.refs_12_
  33.4 1.7 %collective-permute-start.8 = (bf16[2,256,256]{2,1,0:T(8,128)(2,1)S(1)}, bf16[2,256,256]{2,1,0:T(8,128)(2,1)S(1)}, u32[]{:S(2)}, u32[]{:S(2)}) collective-permute-start(bf16[2,256,256]{2,1,0:T(8,128)(2,1)S(1)} %pack.7), channel_id=1, source_target_pairs={{0,2},{2,0},{1,3},{3,1},{4,6},{6,4},{5,7},{7,5},{8,10},{10,8},{9,1... | collective-permute-start | bytes 786440 | tf_op jit(solution)/shard_map/ppermute | solution.py:246
  35.1 0.4 collective-permute-start.4
  35.5 4.0 %collective-permute-start.5 = (bf16[4,64,256]{2,1,0:T(8,128)(2,1)S(1)}, bf16[4,64,256]{2,1,0:T(8,128)(2,1)S(1)}, u32[]{:S(2)}, u32[]{:S(2)}) collective-permute-start(bf16[4,64,256]{2,1,0:T(8,128)(2,1)S(1)} %get-tuple-element.61), channel_id=1, source_target_pairs={{0,9},{1,8},{4,13},{5,12},{8,1},{9,0},{12,5},{13,4},{2,11},{3,10},... | collective-permute-start | bytes 393224 | tf_op jit(solution)/shard_map/ppermute | solution.py:246
  39.5 0.1 collective-permute-start.6
  39.6 2.8 %collective-permute-start.7 = (bf16[4,64,256]{2,1,0:T(8,128)(2,1)S(1)}, bf16[4,64,256]{2,1,0:T(8,128)(2,1)S(1)}, u32[]{:S(2)}, u32[]{:S(2)}) collective-permute-start(bf16[4,64,256]{2,1,0:T(8,128)(2,1)S(1)} %get-tuple-element.63), channel_id=1, source_target_pairs={{0,8},{1,9},{4,12},{5,13},{8,0},{9,1},{12,4},{13,5},{2,10},{3,11},... | collective-permute-start | bytes 393224 | tf_op jit(solution)/shard_map/ppermute | solution.py:246
  42.4 0.7 copy-done.2
  43.1 0.0 copy-done.3
  43.1 6.0 %grads.2 = (bf16[3,64,512]{2,1,0:T(8,128)(2,1)S(1)}, bf16[3,64,512]{2,1,0:T(8,128)(2,1)S(1)}, bf16[3,64,512]{2,1,0:T(8,128)(2,1)S(1)}, bf16[3,64,512]{2,1,0:T(8,...) custom-call(s32[2]{0:T(128)S(1)} %pad_add_fusion.place, ...), custom_call_target="tpu_custom_call" | custom-call | flops 10737418240 | bytes 1835008 | tf_op jit(solution)/shard_map/grads/pallas_call | solution.py:272
  49.1 1.4 %collective-permute-start.17 = (bf16[2,256,256]{2,1,0:T(8,128)(2,1)S(1)}, bf16[2,256,256]{2,1,0:T(8,128)(2,1)S(1)}, u32[]{:S(2)}, u32[]{:S(2)}) collective-permute-start(bf16[2,256,256]{2,1,0:T(8,128)(2,1)S(1)} %get-tuple-element.89), channel_id=1, source_target_pairs={{0,2},{2,0},{1,3},{3,1},{4,6},{6,4},{5,7},{7,5},{8,10},{10,8},{9,1... | collective-permute-start | bytes 786440 | tf_op jit(solution)/shard_map/ppermute | solution.py:246
  50.5 0.9 %collective-permute-start.16 = (bf16[3,64,256]{2,1,0:T(8,128)(2,1)S(1)}, bf16[3,64,256]{2,1,0:T(8,128)(2,1)S(1)}, u32[]{:S(2)}, u32[]{:S(2)}) collective-permute-start(bf16[3,64,256]{2,1,0:T(8,128)(2,1)S(1)} %get-tuple-element.88), channel_id=1, source_target_pairs={{0,12},{1,13},{4,8},{5,9},{8,4},{9,5},{12,0},{13,1},{2,14},{3,15},... | collective-permute-start | bytes 294920 | tf_op jit(solution)/shard_map/ppermute | solution.py:246
  51.4 1.9 %collective-permute-start.21 = (bf16[3,64,256]{2,1,0:T(8,128)(2,1)S(1)}, bf16[3,64,256]{2,1,0:T(8,128)(2,1)S(1)}, u32[]{:S(2)}, u32[]{:S(2)}) collective-permute-start(bf16[3,64,256]{2,1,0:T(8,128)(2,1)S(1)} %get-tuple-element.93), channel_id=1, source_target_pairs={{0,13},{1,12},{4,9},{5,8},{8,5},{9,4},{12,1},{13,0},{2,15},{3,14},... | collective-permute-start | bytes 294920 | tf_op jit(solution)/shard_map/ppermute | solution.py:246
  53.3 6.0 %grads.3 = (bf16[3,64,512]{2,1,0:T(8,128)(2,1)S(1)}, bf16[3,64,512]{2,1,0:T(8,128)(2,1)S(1)}, bf16[3,64,512]{2,1,0:T(8,128)(2,1)S(1)}, bf16[3,64,512]{2,1,0:T(8,...) custom-call(s32[2]{0:T(128)S(1)} %pad_add_fusion.place, ...), custom_call_target="tpu_custom_call", output_to_operand_aliasing={{0}: (18, {}), {1}: (19, {}), {2}: (20, {}), {3}: (21, {}),... | custom-call | flops 10737418240 | bytes 1835008 | tf_op jit(solution)/shard_map/grads/pallas_call | solution.py:272
  59.4 1.1 %collective-permute-start.27 = (bf16[2,256,256]{2,1,0:T(8,128)(2,1)S(1)}, bf16[2,256,256]{2,1,0:T(8,128)(2,1)S(1)}, u32[]{:S(2)}, u32[]{:S(2)}) collective-permute-start(bf16[2,256,256]{2,1,0:T(8,128)(2,1)S(1)} %get-tuple-element.105), channel_id=1, source_target_pairs={{0,2},{2,0},{1,3},{3,1},{4,6},{6,4},{5,7},{7,5},{8,10},{10,8},{9,1... | collective-permute-start | bytes 786440 | tf_op jit(solution)/shard_map/ppermute | solution.py:246
  60.5 2.5 %collective-permute-start.23 = (bf16[3,64,256]{2,1,0:T(8,128)(2,1)S(1)}, bf16[3,64,256]{2,1,0:T(8,128)(2,1)S(1)}, u32[]{:S(2)}, u32[]{:S(2)}) collective-permute-start(bf16[3,64,256]{2,1,0:T(8,128)(2,1)S(1)} %get-tuple-element.96), channel_id=1, source_target_pairs={{0,12},{1,13},{4,8},{5,9},{8,4},{9,5},{12,0},{13,1},{2,14},{3,15},... | collective-permute-start | bytes 294920 | tf_op jit(solution)/shard_map/ppermute | solution.py:246
  63.0 1.1 %collective-permute-start.25 = (bf16[3,64,256]{2,1,0:T(8,128)(2,1)S(1)}, bf16[3,64,256]{2,1,0:T(8,128)(2,1)S(1)}, u32[]{:S(2)}, u32[]{:S(2)}) collective-permute-start(bf16[3,64,256]{2,1,0:T(8,128)(2,1)S(1)} %get-tuple-element.98), channel_id=1, source_target_pairs={{0,13},{1,12},{4,9},{5,8},{8,5},{9,4},{12,1},{13,0},{2,15},{3,14},... | collective-permute-start | bytes 294920 | tf_op jit(solution)/shard_map/ppermute | solution.py:246
  64.1 1.0 %collective-permute-start.24 = (bf16[3,64,512]{2,1,0:T(8,128)(2,1)S(1)}, bf16[3,64,512]{2,1,0:T(8,128)(2,1)S(1)}, u32[]{:S(2)}, u32[]{:S(2)}) collective-permute-start(bf16[3,64,512]{2,1,0:T(8,128)(2,1)S(1)} %get-tuple-element.97), channel_id=1, source_target_pairs={{0,5},{1,4},{4,1},{5,0},{8,13},{9,12},{12,9},{13,8},{2,7},{3,6},{6... | collective-permute-start | bytes 589832 | tf_op jit(solution)/shard_map/ppermute | solution.py:246
  65.2 0.2 collective-permute-done.22.refs_2_
  65.3 4.7 %collective-permute-start.26 = (bf16[3,64,512]{2,1,0:T(8,128)(2,1)S(1)}, bf16[3,64,512]{2,1,0:T(8,128)(2,1)S(1)}, u32[]{:S(2)}, u32[]{:S(2)}) collective-permute-start(bf16[3,64,512]{2,1,0:T(8,128)(2,1)S(1)} %get-tuple-element.99), channel_id=1, source_target_pairs={{0,8},{1,9},{4,12},{5,13},{8,0},{9,1},{12,4},{13,5},{2,10},{3,11},... | collective-permute-start | bytes 589832 | tf_op jit(solution)/shard_map/ppermute | solution.py:246
  70.0 0.1 convert_add_fusion.1
  70.1 2.7 %collective-permute-start.19 = (bf16[3,64,256]{2,1,0:T(8,128)(2,1)S(1)}, bf16[3,64,256]{2,1,0:T(8,128)(2,1)S(1)}, u32[]{:S(2)}, u32[]{:S(2)}) collective-permute-start(bf16[3,64,256]{2,1,0:T(8,128)(2,1)S(1)} %get-tuple-element.91), channel_id=1, source_target_pairs={{0,9},{1,8},{4,13},{5,12},{8,1},{9,0},{12,5},{13,4},{2,11},{3,10},... | collective-permute-start | bytes 294920 | tf_op jit(solution)/shard_map/ppermute | solution.py:246
  72.8 1.9 %collective-permute-start.18 = (bf16[3,64,512]{2,1,0:T(8,128)(2,1)S(1)}, bf16[3,64,512]{2,1,0:T(8,128)(2,1)S(1)}, u32[]{:S(2)}, u32[]{:S(2)}) collective-permute-start(bf16[3,64,512]{2,1,0:T(8,128)(2,1)S(1)} %get-tuple-element.90), channel_id=1, source_target_pairs={{0,4},{1,5},{4,0},{5,1},{8,12},{9,13},{12,8},{13,9},{2,6},{3,7},{6... | collective-permute-start | bytes 589832 | tf_op jit(solution)/shard_map/ppermute | solution.py:246
  74.8 6.8 %collective-permute-start.20 = (bf16[3,64,512]{2,1,0:T(8,128)(2,1)S(1)}, bf16[3,64,512]{2,1,0:T(8,128)(2,1)S(1)}, u32[]{:S(2)}, u32[]{:S(2)}) collective-permute-start(bf16[3,64,512]{2,1,0:T(8,128)(2,1)S(1)} %get-tuple-element.92), channel_id=1, source_target_pairs={{0,1},{1,0},{4,5},{5,4},{8,9},{9,8},{12,13},{13,12},{2,3},{3,2},{6... | collective-permute-start | bytes 589832 | tf_op jit(solution)/shard_map/ppermute | solution.py:246
  81.6 3.9 %collective-permute-done.26.refs_7_ = bf16[3,64,512]{2,1,0:T(8,128)(2,1)S(1)} collective-permute-done((bf16[3,64,512]{2,1,0:T(8,128)(2,1)S(1)}, bf16[3,64,512]{2,1,0:T(8,128)(2,1)S(1)}, u32[]{:S(2)}, u32[]{:S(2)}) %collective-permute-start.26) | collective-permute-done | bytes 196640 | tf_op jit(solution)/shard_map/ppermute | solution.py:246
  85.5 1.7 %unpack.2 = (bf16[64,4096]{1,0:T(8,128)(2,1)}, bf16[64,4096]{1,0:T(8,128)(2,1)}, bf16[64,4096]{1,0:T(8,128)(2,1)}) custom-call(s32[2]{0:T(128)S(1)} %pad_add_fusion.place, bf16[3,64,256]{2,1,0:T(8,128)(2,1)S(1)} %collective-permute-done.16.refs_10_.refs_0_, bf16[3,64,256]{2,1,0:T(8,128)(2,1)S(1)} %collective-permute-done.21.refs_1_, ...), custom_call_target="tpu_custom_call" | custom-call | tf_op jit(solution)/shard_map/unpack/pallas_call | solution.py:324
  87.2 0.1 convert_add_fusion
  87.3 0.1 fusion.2
  87.4 0.0 copy-start
  87.5 1.5 %unpack.3 = (bf16[64,4096]{1,0:T(8,128)(2,1)}, bf16[64,4096]{1,0:T(8,128)(2,1)}, bf16[64,4096]{1,0:T(8,128)(2,1)}) custom-call(s32[2]{0:T(128)S(1)} %pad_add_fusion.place, bf16[3,64,512]{2,1,0:T(8,128)(2,1)S(1)} %collective-permute-done.18.refs_0_, ...), custom_call_target="tpu_custom_call", output_to_operand_aliasing={{0}: (4, {}), {1}: (5, {}), {2}: (6, {})} | custom-call | tf_op jit(solution)/shard_map/unpack/pallas_call | solution.py:324
  (34 shorter events, 0.1 us)
Async XLA Ops:
  2.1 11.4 %collective-permute-start = (bf16[4,64,256]{2,1,0:T(8,128)(2,1)S(1)}, bf16[4,64,256]{2,1,0:T(8,128)(2,1)S(1)}, u32[]{:S(2)}, u32[]{:S(2)}) collective-permute-start(bf16[4,64,256]{2,1,0:T(8,128)(2,1)S(1)} %pack.5.refs_6_), channel_id=1, source_target_pairs={{0,12},{1,13},{4,8},{5,9},{8,4},{9,5},{12,0},{13,1},{2,14},{3,15},... | collective-permute-start | bytes 393224 | tf_op jit(solution)/shard_map/ppermute | solution.py:246
  9.1 9.0 %collective-permute-start.9 = (bf16[4,64,256]{2,1,0:T(8,128)(2,1)S(1)}, bf16[4,64,256]{2,1,0:T(8,128)(2,1)S(1)}, u32[]{:S(2)}, u32[]{:S(2)}) collective-permute-start(bf16[4,64,256]{2,1,0:T(8,128)(2,1)S(1)} %get-tuple-element.64), channel_id=1, source_target_pairs={{0,5},{1,4},{4,1},{5,0},{8,13},{9,12},{12,9},{13,8},{2,7},{3,6},{6... | collective-permute-start | bytes 393224 | tf_op jit(solution)/shard_map/ppermute | solution.py:246
  9.2 8.9 %collective-permute-start.10 = (bf16[4,64,256]{2,1,0:T(8,128)(2,1)S(1)}, bf16[4,64,256]{2,1,0:T(8,128)(2,1)S(1)}, u32[]{:S(2)}, u32[]{:S(2)}) collective-permute-start(bf16[4,64,256]{2,1,0:T(8,128)(2,1)S(1)} %get-tuple-element.65), channel_id=1, source_target_pairs={{0,13},{1,12},{4,9},{5,8},{8,5},{9,4},{12,1},{13,0},{2,15},{3,14},... | collective-permute-start | bytes 393224 | tf_op jit(solution)/shard_map/ppermute | solution.py:246
  11.4 23.8 %collective-permute-start.15 = (bf16[2,256,256]{2,1,0:T(8,128)(2,1)S(1)}, bf16[2,256,256]{2,1,0:T(8,128)(2,1)S(1)}, u32[]{:S(2)}, u32[]{:S(2)}) collective-permute-start(bf16[2,256,256]{2,1,0:T(8,128)(2,1)S(1)} %pack.9), channel_id=1, source_target_pairs={{0,2},{2,0},{1,3},{3,1},{4,6},{6,4},{5,7},{7,5},{8,10},{10,8},{9,1... | collective-permute-start | bytes 786440 | tf_op jit(solution)/shard_map/ppermute | solution.py:246
  12.9 8.8 %collective-permute-start.11 = (bf16[4,64,256]{2,1,0:T(8,128)(2,1)S(1)}, bf16[4,64,256]{2,1,0:T(8,128)(2,1)S(1)}, u32[]{:S(2)}, u32[]{:S(2)}) collective-permute-start(bf16[4,64,256]{2,1,0:T(8,128)(2,1)S(1)} %get-tuple-element.66), channel_id=1, source_target_pairs={{0,4},{1,5},{4,0},{5,1},{8,12},{9,13},{12,8},{13,9},{2,6},{3,7},{6... | collective-permute-start | bytes 393224 | tf_op jit(solution)/shard_map/ppermute | solution.py:246
  13.5 12.4 %collective-permute-start.12 = (bf16[4,64,256]{2,1,0:T(8,128)(2,1)S(1)}, bf16[4,64,256]{2,1,0:T(8,128)(2,1)S(1)}, u32[]{:S(2)}, u32[]{:S(2)}) collective-permute-start(bf16[4,64,256]{2,1,0:T(8,128)(2,1)S(1)} %get-tuple-element.67), channel_id=1, source_target_pairs={{0,9},{1,8},{4,13},{5,12},{8,1},{9,0},{12,5},{13,4},{2,11},{3,10},... | collective-permute-start | bytes 393224 | tf_op jit(solution)/shard_map/ppermute | solution.py:246
  18.1 8.2 %collective-permute-start.13 = (bf16[4,64,256]{2,1,0:T(8,128)(2,1)S(1)}, bf16[4,64,256]{2,1,0:T(8,128)(2,1)S(1)}, u32[]{:S(2)}, u32[]{:S(2)}) collective-permute-start(bf16[4,64,256]{2,1,0:T(8,128)(2,1)S(1)} %get-tuple-element.68), channel_id=1, source_target_pairs={{0,1},{1,0},{4,5},{5,4},{8,9},{9,8},{12,13},{13,12},{2,3},{3,2},{6... | collective-permute-start | bytes 393224 | tf_op jit(solution)/shard_map/ppermute | solution.py:246
  18.1 15.3 %collective-permute-start.14 = (bf16[4,64,256]{2,1,0:T(8,128)(2,1)S(1)}, bf16[4,64,256]{2,1,0:T(8,128)(2,1)S(1)}, u32[]{:S(2)}, u32[]{:S(2)}) collective-permute-start(bf16[4,64,256]{2,1,0:T(8,128)(2,1)S(1)} %get-tuple-element.69), channel_id=1, source_target_pairs={{0,8},{1,9},{4,12},{5,13},{8,0},{9,1},{12,4},{13,5},{2,10},{3,11},... | collective-permute-start | bytes 393224 | tf_op jit(solution)/shard_map/ppermute | solution.py:246
  21.7 13.8 %collective-permute-start.1 = (bf16[4,64,256]{2,1,0:T(8,128)(2,1)S(1)}, bf16[4,64,256]{2,1,0:T(8,128)(2,1)S(1)}, u32[]{:S(2)}, u32[]{:S(2)}) collective-permute-start(bf16[4,64,256]{2,1,0:T(8,128)(2,1)S(1)} %get-tuple-element.57), channel_id=1, source_target_pairs={{0,12},{1,13},{4,8},{5,9},{8,4},{9,5},{12,0},{13,1},{2,14},{3,15},... | collective-permute-start | bytes 393224 | tf_op jit(solution)/shard_map/ppermute | solution.py:246
  25.9 13.6 %collective-permute-start.2 = (bf16[4,64,256]{2,1,0:T(8,128)(2,1)S(1)}, bf16[4,64,256]{2,1,0:T(8,128)(2,1)S(1)}, u32[]{:S(2)}, u32[]{:S(2)}) collective-permute-start(bf16[4,64,256]{2,1,0:T(8,128)(2,1)S(1)} %get-tuple-element.58), channel_id=1, source_target_pairs={{0,5},{1,4},{4,1},{5,0},{8,13},{9,12},{12,9},{13,8},{2,7},{3,6},{6... | collective-permute-start | bytes 393224 | tf_op jit(solution)/shard_map/ppermute | solution.py:246
  26.3 6.7 %copy-start.4 = (s32[1,4,3]{1,0,2:T(1,128)S(1)}, s32[1,4,3]{1,0,2:T(1,128)}, u32[]{:S(2)}) copy-start(s32[1,4,3]{1,0,2:T(1,128)} %param.15) | copy-start | bytes 148
  26.3 13.3 %collective-permute-start.3 = (bf16[4,64,256]{2,1,0:T(8,128)(2,1)S(1)}, bf16[4,64,256]{2,1,0:T(8,128)(2,1)S(1)}, u32[]{:S(2)}, u32[]{:S(2)}) collective-permute-start(bf16[4,64,256]{2,1,0:T(8,128)(2,1)S(1)} %get-tuple-element.59), channel_id=1, source_target_pairs={{0,13},{1,12},{4,9},{5,8},{8,5},{9,4},{12,1},{13,0},{2,15},{3,14},... | collective-permute-start | bytes 393224 | tf_op jit(solution)/shard_map/ppermute | solution.py:246
  33.4 18.0 %collective-permute-start.8 = (bf16[2,256,256]{2,1,0:T(8,128)(2,1)S(1)}, bf16[2,256,256]{2,1,0:T(8,128)(2,1)S(1)}, u32[]{:S(2)}, u32[]{:S(2)}) collective-permute-start(bf16[2,256,256]{2,1,0:T(8,128)(2,1)S(1)} %pack.7), channel_id=1, source_target_pairs={{0,2},{2,0},{1,3},{3,1},{4,6},{6,4},{5,7},{7,5},{8,10},{10,8},{9,1... | collective-permute-start | bytes 786440 | tf_op jit(solution)/shard_map/ppermute | solution.py:246
  35.1 13.9 %collective-permute-start.4 = (bf16[4,64,256]{2,1,0:T(8,128)(2,1)S(1)}, bf16[4,64,256]{2,1,0:T(8,128)(2,1)S(1)}, u32[]{:S(2)}, u32[]{:S(2)}) collective-permute-start(bf16[4,64,256]{2,1,0:T(8,128)(2,1)S(1)} %get-tuple-element.60), channel_id=1, source_target_pairs={{0,4},{1,5},{4,0},{5,1},{8,12},{9,13},{12,8},{13,9},{2,6},{3,7},{6... | collective-permute-start | bytes 393224 | tf_op jit(solution)/shard_map/ppermute | solution.py:246
  35.5 15.0 %collective-permute-start.5 = (bf16[4,64,256]{2,1,0:T(8,128)(2,1)S(1)}, bf16[4,64,256]{2,1,0:T(8,128)(2,1)S(1)}, u32[]{:S(2)}, u32[]{:S(2)}) collective-permute-start(bf16[4,64,256]{2,1,0:T(8,128)(2,1)S(1)} %get-tuple-element.61), channel_id=1, source_target_pairs={{0,9},{1,8},{4,13},{5,12},{8,1},{9,0},{12,5},{13,4},{2,11},{3,10},... | collective-permute-start | bytes 393224 | tf_op jit(solution)/shard_map/ppermute | solution.py:246
  39.5 13.8 %collective-permute-start.6 = (bf16[4,64,256]{2,1,0:T(8,128)(2,1)S(1)}, bf16[4,64,256]{2,1,0:T(8,128)(2,1)S(1)}, u32[]{:S(2)}, u32[]{:S(2)}) collective-permute-start(bf16[4,64,256]{2,1,0:T(8,128)(2,1)S(1)} %get-tuple-element.62), channel_id=1, source_target_pairs={{0,1},{1,0},{4,5},{5,4},{8,9},{9,8},{12,13},{13,12},{2,3},{3,2},{6... | collective-permute-start | bytes 393224 | tf_op jit(solution)/shard_map/ppermute | solution.py:246
  39.6 13.8 %collective-permute-start.7 = (bf16[4,64,256]{2,1,0:T(8,128)(2,1)S(1)}, bf16[4,64,256]{2,1,0:T(8,128)(2,1)S(1)}, u32[]{:S(2)}, u32[]{:S(2)}) collective-permute-start(bf16[4,64,256]{2,1,0:T(8,128)(2,1)S(1)} %get-tuple-element.63), channel_id=1, source_target_pairs={{0,8},{1,9},{4,12},{5,13},{8,0},{9,1},{12,4},{13,5},{2,10},{3,11},... | collective-permute-start | bytes 393224 | tf_op jit(solution)/shard_map/ppermute | solution.py:246
  42.4 0.7 copy-start.2
  42.4 0.7 copy-start.3
  49.1 10.3 %collective-permute-start.17 = (bf16[2,256,256]{2,1,0:T(8,128)(2,1)S(1)}, bf16[2,256,256]{2,1,0:T(8,128)(2,1)S(1)}, u32[]{:S(2)}, u32[]{:S(2)}) collective-permute-start(bf16[2,256,256]{2,1,0:T(8,128)(2,1)S(1)} %get-tuple-element.89), channel_id=1, source_target_pairs={{0,2},{2,0},{1,3},{3,1},{4,6},{6,4},{5,7},{7,5},{8,10},{10,8},{9,1... | collective-permute-start | bytes 786440 | tf_op jit(solution)/shard_map/ppermute | solution.py:246
  50.5 8.8 %collective-permute-start.16 = (bf16[3,64,256]{2,1,0:T(8,128)(2,1)S(1)}, bf16[3,64,256]{2,1,0:T(8,128)(2,1)S(1)}, u32[]{:S(2)}, u32[]{:S(2)}) collective-permute-start(bf16[3,64,256]{2,1,0:T(8,128)(2,1)S(1)} %get-tuple-element.88), channel_id=1, source_target_pairs={{0,12},{1,13},{4,8},{5,9},{8,4},{9,5},{12,0},{13,1},{2,14},{3,15},... | collective-permute-start | bytes 294920 | tf_op jit(solution)/shard_map/ppermute | solution.py:246
  51.4 12.7 %collective-permute-start.21 = (bf16[3,64,256]{2,1,0:T(8,128)(2,1)S(1)}, bf16[3,64,256]{2,1,0:T(8,128)(2,1)S(1)}, u32[]{:S(2)}, u32[]{:S(2)}) collective-permute-start(bf16[3,64,256]{2,1,0:T(8,128)(2,1)S(1)} %get-tuple-element.93), channel_id=1, source_target_pairs={{0,13},{1,12},{4,9},{5,8},{8,5},{9,4},{12,1},{13,0},{2,15},{3,14},... | collective-permute-start | bytes 294920 | tf_op jit(solution)/shard_map/ppermute | solution.py:246
  53.3 12.0 %collective-permute-start.22 = (bf16[3,64,256]{2,1,0:T(8,128)(2,1)S(1)}, bf16[3,64,256]{2,1,0:T(8,128)(2,1)S(1)}, u32[]{:S(2)}, u32[]{:S(2)}) collective-permute-start(bf16[3,64,256]{2,1,0:T(8,128)(2,1)S(1)} %get-tuple-element.94), channel_id=1, source_target_pairs={{0,9},{1,8},{4,13},{5,12},{8,1},{9,0},{12,5},{13,4},{2,11},{3,10},... | collective-permute-start | bytes 294920 | tf_op jit(solution)/shard_map/ppermute | solution.py:246
  59.4 27.8 %collective-permute-start.27 = (bf16[2,256,256]{2,1,0:T(8,128)(2,1)S(1)}, bf16[2,256,256]{2,1,0:T(8,128)(2,1)S(1)}, u32[]{:S(2)}, u32[]{:S(2)}) collective-permute-start(bf16[2,256,256]{2,1,0:T(8,128)(2,1)S(1)} %get-tuple-element.105), channel_id=1, source_target_pairs={{0,2},{2,0},{1,3},{3,1},{4,6},{6,4},{5,7},{7,5},{8,10},{10,8},{9,1... | collective-permute-start | bytes 786440 | tf_op jit(solution)/shard_map/ppermute | solution.py:246
  60.5 9.6 %collective-permute-start.23 = (bf16[3,64,256]{2,1,0:T(8,128)(2,1)S(1)}, bf16[3,64,256]{2,1,0:T(8,128)(2,1)S(1)}, u32[]{:S(2)}, u32[]{:S(2)}) collective-permute-start(bf16[3,64,256]{2,1,0:T(8,128)(2,1)S(1)} %get-tuple-element.96), channel_id=1, source_target_pairs={{0,12},{1,13},{4,8},{5,9},{8,4},{9,5},{12,0},{13,1},{2,14},{3,15},... | collective-permute-start | bytes 294920 | tf_op jit(solution)/shard_map/ppermute | solution.py:246
  63.0 9.9 %collective-permute-start.25 = (bf16[3,64,256]{2,1,0:T(8,128)(2,1)S(1)}, bf16[3,64,256]{2,1,0:T(8,128)(2,1)S(1)}, u32[]{:S(2)}, u32[]{:S(2)}) collective-permute-start(bf16[3,64,256]{2,1,0:T(8,128)(2,1)S(1)} %get-tuple-element.98), channel_id=1, source_target_pairs={{0,13},{1,12},{4,9},{5,8},{8,5},{9,4},{12,1},{13,0},{2,15},{3,14},... | collective-permute-start | bytes 294920 | tf_op jit(solution)/shard_map/ppermute | solution.py:246
  64.1 10.6 %collective-permute-start.24 = (bf16[3,64,512]{2,1,0:T(8,128)(2,1)S(1)}, bf16[3,64,512]{2,1,0:T(8,128)(2,1)S(1)}, u32[]{:S(2)}, u32[]{:S(2)}) collective-permute-start(bf16[3,64,512]{2,1,0:T(8,128)(2,1)S(1)} %get-tuple-element.97), channel_id=1, source_target_pairs={{0,5},{1,4},{4,1},{5,0},{8,13},{9,12},{12,9},{13,8},{2,7},{3,6},{6... | collective-permute-start | bytes 589832 | tf_op jit(solution)/shard_map/ppermute | solution.py:246
  65.3 20.2 %collective-permute-start.26 = (bf16[3,64,512]{2,1,0:T(8,128)(2,1)S(1)}, bf16[3,64,512]{2,1,0:T(8,128)(2,1)S(1)}, u32[]{:S(2)}, u32[]{:S(2)}) collective-permute-start(bf16[3,64,512]{2,1,0:T(8,128)(2,1)S(1)} %get-tuple-element.99), channel_id=1, source_target_pairs={{0,8},{1,9},{4,12},{5,13},{8,0},{9,1},{12,4},{13,5},{2,10},{3,11},... | collective-permute-start | bytes 589832 | tf_op jit(solution)/shard_map/ppermute | solution.py:246
  70.1 17.3 %collective-permute-start.19 = (bf16[3,64,256]{2,1,0:T(8,128)(2,1)S(1)}, bf16[3,64,256]{2,1,0:T(8,128)(2,1)S(1)}, u32[]{:S(2)}, u32[]{:S(2)}) collective-permute-start(bf16[3,64,256]{2,1,0:T(8,128)(2,1)S(1)} %get-tuple-element.91), channel_id=1, source_target_pairs={{0,9},{1,8},{4,13},{5,12},{8,1},{9,0},{12,5},{13,4},{2,11},{3,10},... | collective-permute-start | bytes 294920 | tf_op jit(solution)/shard_map/ppermute | solution.py:246
  72.8 14.6 %collective-permute-start.18 = (bf16[3,64,512]{2,1,0:T(8,128)(2,1)S(1)}, bf16[3,64,512]{2,1,0:T(8,128)(2,1)S(1)}, u32[]{:S(2)}, u32[]{:S(2)}) collective-permute-start(bf16[3,64,512]{2,1,0:T(8,128)(2,1)S(1)} %get-tuple-element.90), channel_id=1, source_target_pairs={{0,4},{1,5},{4,0},{5,1},{8,12},{9,13},{12,8},{13,9},{2,6},{3,7},{6... | collective-permute-start | bytes 589832 | tf_op jit(solution)/shard_map/ppermute | solution.py:246
  74.8 12.7 %collective-permute-start.20 = (bf16[3,64,512]{2,1,0:T(8,128)(2,1)S(1)}, bf16[3,64,512]{2,1,0:T(8,128)(2,1)S(1)}, u32[]{:S(2)}, u32[]{:S(2)}) collective-permute-start(bf16[3,64,512]{2,1,0:T(8,128)(2,1)S(1)} %get-tuple-element.92), channel_id=1, source_target_pairs={{0,1},{1,0},{4,5},{5,4},{8,9},{9,8},{12,13},{13,12},{2,3},{3,2},{6... | collective-permute-start | bytes 589832 | tf_op jit(solution)/shard_map/ppermute | solution.py:246
  87.4 1.5 %copy-start = (f32[256,512]{1,0:T(8,128)}, f32[256,512]{1,0:T(8,128)S(1)}, u32[]{:S(2)}) copy-start(f32[256,512]{1,0:T(8,128)S(1)} %get-tuple-element.109.refs_7_) | copy-start | bytes 1572868
  87.4 1.5 %copy-start.1 = (f32[256,512]{1,0:T(8,128)}, f32[256,512]{1,0:T(8,128)S(1)}, u32[]{:S(2)}) copy-start(f32[256,512]{1,0:T(8,128)S(1)} %get-tuple-element.110.refs_6_) | copy-start | bytes 1572868
